TPU v7x, 256 devices: a whole 4x4x8 slice. The times are simulated.
256 devices in a mesh: fsdp: 8 (over z_lo, core), seq: 8 (over y, z_hi), dp: 4 (over x).
Axes of the slice: x: 4, y: 4, z: 8 (z_hi: 2, z_lo: 4; z = z_hi * 4 + z_lo), core: 2. Of those that a mesh axis runs over, the one named last changes fastest.
Arguments:
- hidden: bfloat16 [32, 2, 512, 2048], P(('fsdp', 'dp'), None, 'seq'), may hold values from -3 to 3
- answer_rows: bfloat16 [32, 2, 512, 2048], P(('fsdp', 'dp'), None, 'seq'), may hold values from -0.125 to 0.125
- resp_mask: int32 [32, 2, 512], P(('fsdp', 'dp'), None, 'seq'), may hold values from 0 to 1, as said below
- attn_gain: float32 [2048], replicated, may hold values from 0.5 to 1.5
- final_gain: float32 [2048], replicated, may hold values from 0.5 to 1.5
- w_query: bfloat16 [2048, 2048], P(('fsdp', 'dp'))
- w_key: bfloat16 [2048, 512], P(('fsdp', 'dp'))
- w_value: bfloat16 [2048, 512], P(('fsdp', 'dp')), may hold values from -0.125 to 0.125
- w_out: bfloat16 [2048, 2048], P(('fsdp', 'dp')), may hold values from -0.125 to 0.125
- a_query: bfloat16 [2048, 64], P(('fsdp', 'dp')), may hold values from -0.125 to 0.125
- b_query: bfloat16 [2048, 64], P(('fsdp', 'dp')), may hold values from -0.375 to 0.375
- a_value: bfloat16 [2048, 64], P(('fsdp', 'dp')), may hold values from -0.125 to 0.125
- b_value: bfloat16 [512, 64], P(('fsdp', 'dp')), may hold values from -0.375 to 0.375
Outputs:
- grad_a_query: float32 [2048, 64], P(('fsdp', 'dp'))
- grad_b_query: float32 [2048, 64], P(('fsdp', 'dp'))
- grad_a_value: float32 [2048, 64], P(('fsdp', 'dp'))
- grad_b_value: float32 [512, 64], P(('fsdp', 'dp'))
- dpo_loss: float32 [32], P(('fsdp', 'dp'))
Inputs may be any that keep to these rules, and one draw needn't show every extreme that they name: `resp_mask`: each sequence is 0 on a prompt of 64 to 256 positions and 1 on every later position; both sequences of a pair have the same prompt length.
All inputs are finite; a program needn't handle non-finite values.
Results may differ from a plain program's by a relative error of at most 0.029.
The roundings to bfloat16 on the way count: a program that leaves them out, or rounds other values in their place, can miss the bound.
Values may be sent and summed in bfloat16 or wider, within the bound.
No kernel may reach another device: no remote copies, remote signals or barrier semaphores. Data moves between devices by JAX's collectives and lax.ppermute only.
A program may use at most 64 MiB of HBM per device.

v0:
```python
import math

import jax
import jax.numpy as jnp
from jax import lax
from jax.experimental import pallas as pl
from jax.experimental.pallas import tpu as pltpu
from jax.sharding import Mesh
from jax.sharding import PartitionSpec as P

D = 2048
HQ = 16
HK = 4
HD = 128
RANK = 64
GROUP = HQ // HK
KVW = HK * HD
TOK = 64
ROWS = 2 * TOK
BLOCKS = 8
ALL = BLOCKS * ROWS
L = BLOCKS * TOK
PARTS = 2 * HK
QROWS = GROUP * TOK

EPS = 1e-05
BETA = 0.1
ADAPTER_SCALE = 2.0
THETA = 500000.0

BF = jnp.bfloat16
F32 = jnp.float32

AXES = ("z", "c", "y", "h", "x")
OWN = ("z", "c", "x")


def mm(a, b):
    return jnp.dot(a, b, preferred_element_type=F32)


def mm_t(a, b):
    return lax.dot_general(a, b, (((1,), (1,)), ((), ())), preferred_element_type=F32)


def turn(u, c, s):
    return u * c + pltpu.roll(u, HD // 2, 1) * s


def dot_rows(a, b):
    return jnp.sum(a * b, axis=-1, keepdims=True)


def local_kernel(own_ref, full, xa_in, kc, ks, bias, hid, ans, gain, sign, out,
                 xa, wn, wkv, wq, wo, low, bqm, bvm, keys, vref, vpol, qs, prob, probb, o32, heads, yp, by, bo, bq, vt, dn, sems):
    copies = [
        pltpu.make_async_copy(xa_in, xa, sems.at[0]),
        pltpu.make_async_copy(full.at[:, 5120:5376], wn, sems.at[1]),
        pltpu.make_async_copy(full.at[:, 2048:3072], wkv, sems.at[2]),
        pltpu.make_async_copy(full.at[:, 0:2048], wq, sems.at[3]),
        pltpu.make_async_copy(full.at[:, 3072:5120], wo, sems.at[4]),
    ]
    for copy in copies:
        copy.start()
    own = pl.multiple_of(own_ref[0] * ROWS, ROWS)

    copies[0].wait()
    copies[1].wait()
    lane = lax.broadcasted_iota(jnp.int32, (D, 2 * RANK), 1)
    bqm[...] = jnp.where(lane < RANK, wn[:, 2 * RANK :].astype(F32), 0.0).astype(BF)
    lane16 = lax.broadcasted_iota(jnp.int32, (16, 2 * RANK), 1)
    for d in range(32):
        bvm[16 * d : 16 * d + 16, :] = jnp.where(lane16 >= RANK, wn[64 * d : 64 * d + 16, 2 * RANK :].astype(F32), 0.0).astype(BF)
    copies[2].wait()

    @pl.loop(0, ALL // 256)
    def _(r):
        r0 = pl.multiple_of(r * 256, 256)
        x = xa[pl.ds(r0, 256), :]
        lw = mm(x, wn[:, : 2 * RANK]).astype(BF)
        low[pl.ds(r0, 256), :] = lw
        c, s = kc[pl.ds(r0, 256), :], ks[pl.ds(r0, 256), :]
        kv = mm(x, wkv[...])
        lift = mm_t(lw, bvm[...])
        for g in range(HK):
            cols = slice(HD * g, HD * g + HD)
            k = turn(kv[:, cols], c, s).astype(BF)
            vr = kv[:, KVW + HD * g : KVW + HD * g + HD].astype(BF)
            vp = (vr.astype(F32) + ADAPTER_SCALE * lift[:, cols]).astype(BF)
            for b in range(2):
                t0 = pl.multiple_of(r * 2 * TOK + b * TOK, TOK)
                for side in range(2):
                    src = slice(b * ROWS + side * TOK, b * ROWS + side * TOK + TOK)
                    at = side * HK + g
                    keys[at, pl.ds(t0, TOK), :] = k[src]
                    vref[at, pl.ds(t0, TOK), :] = vr[src]
                    vpol[at, pl.ds(t0, TOK), :] = vp[src]

    copies[3].wait()
    c_own, s_own = kc[pl.ds(own, ROWS), :], ks[pl.ds(own, ROWS), :]

    @pl.loop(0, HK)
    def _(g):
        w0 = pl.multiple_of(g * GROUP * HD, GROUP * HD)
        base = mm(xa[pl.ds(own, ROWS), :], wq[:, pl.ds(w0, GROUP * HD)])
        lift = mm_t(low[pl.ds(own, ROWS), :], bqm[pl.ds(w0, GROUP * HD), :])
        moved = base + ADAPTER_SCALE * lift
        for j in range(GROUP):
            cols = slice(HD * j, HD * j + HD)
            qr = turn(base[:, cols], c_own, s_own).astype(BF)
            qp = turn(moved[:, cols], c_own, s_own).astype(BF)
            for side in range(2):
                src = slice(side * TOK, side * TOK + TOK)
                qs[0, side * HK + g, j * TOK : j * TOK + TOK, :] = qr[src]
                qs[1, side * HK + g, j * TOK : j * TOK + TOK, :] = qp[src]

    scale = 1.0 / math.sqrt(HD)

    def soft(q, k):
        logits = mm_t(q, k) * scale
        logits = (logits.reshape(GROUP, TOK, L) + bias[...][None]).reshape(QROWS, L)
        raised = jnp.exp(logits - jnp.max(logits, axis=-1, keepdims=True))
        return raised * (1.0 / jnp.sum(raised, axis=-1, keepdims=True))

    @pl.loop(0, PARTS)
    def _(i):
        g, side = lax.rem(i, HK), lax.div(i, HK)
        k = keys[i]
        p0 = soft(qs[0, i], k)
        p1 = soft(qs[1, i], k)
        b1 = p1.astype(BF)
        prob[i] = p1
        probb[i] = b1
        m0 = mm(p0.astype(BF), vref[i])
        m1 = mm(b1, vpol[i])
        o32[i] = m1
        n0, n1 = m0.astype(BF), m1.astype(BF)
        r0 = pl.multiple_of(side * TOK, TOK)
        for j in range(GROUP):
            c0 = pl.multiple_of(g * GROUP * HD + j * HD, HD)
            heads[pl.ds(r0, TOK), pl.ds(c0, HD)] = n0[j * TOK : j * TOK + TOK]
            heads[pl.ds(r0 + ROWS, TOK), pl.ds(c0, HD)] = n1[j * TOK : j * TOK + TOK]

    copies[4].wait()
    tile = 512
    zero = jnp.zeros((ROWS, 1), F32)
    sq0, sq1, sc0, sc1 = zero, zero, zero, zero
    for n in range(D // tile):
        cols = slice(n * tile, n * tile + tile)
        y = mm(heads[...], wo[:, cols])
        x = hid[:, cols].astype(F32)
        ga = gain[:, cols] * ans[:, cols].astype(F32)
        y0, y1 = x + y[:ROWS], x + y[ROWS:]
        yp[:, cols] = y1
        sq0, sq1 = sq0 + dot_rows(y0, y0), sq1 + dot_rows(y1, y1)
        sc0, sc1 = sc0 + dot_rows(y0, ga), sc1 + dot_rows(y1, ga)
    inv0 = lax.rsqrt(sq0 * (1.0 / D) + EPS)
    inv1 = lax.rsqrt(sq1 * (1.0 / D) + EPS)
    score0, score1 = sc0 * inv0, sc1 * inv1
    sg = sign[...]
    margin = jnp.sum(sg * (score1 - score0), axis=0, keepdims=True)
    lead = inv1 * sg
    pull = inv1 * score1 * (1.0 / D)
    for n in range(D // tile):
        cols = slice(n * tile, n * tile + tile)
        ga = gain[:, cols] * ans[:, cols].astype(F32)
        by[:, cols] = (lead * (ga - yp[:, cols] * pull)).astype(BF)

    @pl.loop(0, HK)
    def _(g):
        w0 = pl.multiple_of(g * GROUP * HD, GROUP * HD)
        back = mm_t(by[...], wo[pl.ds(w0, GROUP * HD), :]).astype(BF)
        for j in range(GROUP):
            for side in range(2):
                bo[side * HK + g, j * TOK : j * TOK + TOK, :] = back[side * TOK : side * TOK + TOK, HD * j : HD * j + HD]

    @pl.loop(0, PARTS)
    def _(i):
        g, side = lax.rem(i, HK), lax.div(i, HK)
        b = bo[i]
        dp = mm_t(b, vpol[i])
        rd = dot_rows(b.astype(F32), o32[i])
        bl = (prob[i] * (dp - rd) * scale).astype(BF)
        dq = mm(bl, keys[i])
        term = mm(probb[i].T, b).astype(BF)
        r0 = pl.multiple_of(side * TOK, TOK)
        o0 = pl.multiple_of(own + side * TOK, TOK)
        c, s = kc[pl.ds(o0, TOK), :], ks[pl.ds(o0, TOK), :]
        for j in range(GROUP):
            c0 = pl.multiple_of(g * GROUP * HD + j * HD, HD)
            bq[pl.ds(r0, TOK), pl.ds(c0, HD)] = turn(dq[j * TOK : j * TOK + TOK], c, -s).astype(BF)
        for blk in range(BLOCKS):
            v0 = pl.multiple_of(side * TOK + blk * ROWS, TOK)
            vt[pl.ds(v0, TOK), pl.ds(pl.multiple_of(g * HD, HD), HD)] = term[blk * TOK : blk * TOK + TOK]

    dn[...] = mm(vt[...], bvm[...]).astype(BF)
    dq_low = mm(bq[...], bqm[...])
    dn[pl.ds(own, ROWS), :] = (dn[pl.ds(own, ROWS), :].astype(F32) + dq_low).astype(BF)
    dn_t = dn[...].T
    low_t = low[...].T
    low_own_t = low[pl.ds(own, ROWS), :].T
    lane64 = lax.broadcasted_iota(jnp.int32, (256, 2 * RANK), 1)
    for n in range(D // tile):
        cols = slice(n * tile, n * tile + tile)
        ga_t = (ADAPTER_SCALE * mm(dn_t, xa[:, cols])).T
        gb_t = (ADAPTER_SCALE * mm(low_own_t, bq[:, cols])).T
        for d in range(tile // TOK):
            for q in range(4):
                src = slice(d * TOK + q * 16, d * TOK + q * 16 + 16)
                out[q, n * (tile // TOK) + d, :, : 2 * RANK] = ga_t[src].astype(BF)
                out[q, n * (tile // TOK) + d, :, 2 * RANK :] = jnp.where(lane16 < RANK, gb_t[src], 0.0).astype(BF)
    gv_t = (ADAPTER_SCALE * mm(low_t, vt[...])).T
    for d in range(32):
        here = out[0, d, :, 2 * RANK :].astype(F32)
        out[0, d, :, 2 * RANK :] = jnp.where(lane16 < RANK, here, gv_t[16 * d : 16 * d + 16]).astype(BF)
    hi = margin.astype(BF).astype(F32)
    mid = (margin - hi).astype(BF).astype(F32)
    lo = margin - hi - mid
    lane_m = lax.broadcasted_iota(jnp.int32, (16, 4 * RANK), 1)
    riding = jnp.where(lane_m == 0, hi, jnp.where(lane_m == 1, mid, jnp.where(lane_m == 2, lo, 0.0))).astype(BF)
    for q in range(4):
        out[q, 32] = riding


def local_step(own_block, full, xa, kc, ks, bias, hid, ans, gain, sign):
    vm, anyspace = pl.BlockSpec(memory_space=pltpu.VMEM), pl.BlockSpec(memory_space=pl.ANY)
    bf, f32 = (lambda *s: pltpu.VMEM(s, BF)), (lambda *s: pltpu.VMEM(s, F32))
    return pl.pallas_call(
        local_kernel,
        out_shape=jax.ShapeDtypeStruct((4, 33, 16, 4 * RANK), BF),
        in_specs=[pl.BlockSpec(memory_space=pltpu.SMEM), anyspace, anyspace] + [vm] * 7,
        out_specs=vm,
        scratch_shapes=[
            bf(ALL, D), bf(D, 256), bf(D, 2 * KVW), bf(D, D), bf(D, D),
            bf(ALL, 2 * RANK), bf(D, 2 * RANK), bf(KVW, 2 * RANK),
            bf(PARTS, L, HD), bf(PARTS, L, HD), bf(PARTS, L, HD),
            bf(2, PARTS, QROWS, HD), f32(PARTS, QROWS, L), bf(PARTS, QROWS, L), f32(PARTS, QROWS, HD),
            bf(2 * ROWS, D), f32(ROWS, D), bf(ROWS, D), bf(PARTS, QROWS, HD), bf(ROWS, D), bf(ALL, KVW), bf(ALL, 2 * RANK),
            pltpu.SemaphoreType.DMA((5,)),
        ],
        compiler_params=pltpu.CompilerParams(vmem_limit_bytes=60 * 2**20),
        cost_estimate=pl.CostEstimate(flops=24_000_000_000, bytes_accessed=27_000_000, transcendentals=2_100_000),
    )(own_block, full, xa, kc, ks, bias, hid, ans, gain, sign)


def split3(value):
    hi = lax.reduce_precision(value, 8, 7)
    mid = lax.reduce_precision(value - hi, 8, 7)
    return jnp.stack([hi, mid, value - hi - mid], axis=-1)


def body(hidden, answer_rows, resp_mask, attn_gain, final_gain, w_query, w_key, w_value, w_out, a_query, b_query, a_value, b_value):
    hidden = hidden[0]
    y_pos, h_pos = lax.axis_index("y"), lax.axis_index("h")

    narrow_v = jnp.concatenate([b_value, jnp.zeros((TOK - b_value.shape[0], RANK), BF)], axis=0)
    packed = jnp.concatenate([w_query, w_key, w_value, w_out, a_query, a_value, b_query, narrow_v], axis=1)
    full = lax.all_gather(packed, OWN, axis=0, tiled=True)

    x32 = hidden.astype(F32)
    xn = (x32 * lax.rsqrt(jnp.mean(x32 * x32, axis=-1, keepdims=True) + EPS) * attn_gain).astype(BF).reshape(ROWS, D)
    other = lax.ppermute(xn, "h", [(0, 1), (1, 0)])
    two = jnp.concatenate([xn, other], axis=0)
    every = lax.all_to_all(jnp.broadcast_to(two[None], (4,) + two.shape), "y", 0, 0, tiled=True)
    xa = every.reshape(ALL, D)

    block = jnp.arange(BLOCKS, dtype=jnp.int32)
    source = (block // 2) * 2 + jnp.bitwise_xor(block % 2, h_pos)
    token = jnp.arange(TOK, dtype=jnp.int32)
    key_pos = source[:, None] * TOK + token[None, :]
    own_pos = (y_pos * 2 + h_pos) * TOK + token
    frequency = THETA ** (-(jnp.arange(HD // 2, dtype=F32) * 2.0) / HD)
    row_pos = jnp.broadcast_to(key_pos[:, None, :], (BLOCKS, 2, TOK)).reshape(ALL)
    angles = row_pos.astype(F32)[:, None] * frequency[None, :]
    cosine, sine = jnp.cos(angles), jnp.sin(angles)
    kc = jnp.concatenate([cosine, cosine], axis=1)
    ks = jnp.concatenate([-sine, sine], axis=1)
    bias = jnp.where(own_pos[:, None] >= key_pos.reshape(1, L), 0.0, -1e30).astype(F32)
    sign = (resp_mask[0].astype(F32) * jnp.array([1.0, -1.0], F32)[:, None]).reshape(ROWS, 1)
    own_block = jnp.full((1,), 2, jnp.int32) * y_pos

    mine = local_step(own_block, full, xa, kc, ks, bias, hidden.reshape(ROWS, D), answer_rows.reshape(ROWS, D), final_gain.reshape(1, D), sign)

    got = jnp.sum(lax.all_to_all(mine, "y", 0, 0, tiled=True).astype(F32), axis=0)
    first = jnp.sum(got[32, 0, :3]).reshape(1)
    sent = got.astype(BF)
    sent = jnp.concatenate([sent[:32], jnp.pad(split3(first).astype(BF).reshape(1, 1, 3), ((0, 0), (0, 15), (0, 253)))], axis=0)
    sent = lax.optimization_barrier(sent)
    met = lax.ppermute(sent, "h", [(0, 1), (1, 0)])
    margin = jnp.sum(sent[32, 0, :3].astype(F32)).reshape(1) + jnp.sum(met[32, 0, :3].astype(F32)).reshape(1)
    loss = jax.nn.softplus(-BETA * margin)
    weight = -BETA * jax.nn.sigmoid(-BETA * margin)
    scaled = (weight * (sent[:32].astype(F32) + met[:32].astype(F32))).astype(BF)
    shares = lax.all_to_all(scaled, OWN, 0, 0, tiled=True)
    piece = jnp.sum(shares.astype(F32), axis=0)
    total = lax.all_to_all(jnp.broadcast_to(piece[None], (4,) + piece.shape), "y", 0, 0, tiled=True).reshape(TOK, 4 * RANK)
    return total[:, :64], total[:, 128:192], total[:, 64:128], total[:16, 192:], loss


def solution(mesh):
    fine = Mesh(mesh.devices.reshape(4, 2, 4, 2, 4), AXES)
    seq = ("y", "h")
    weights = P(OWN, None)
    in_specs = (P(OWN, None, seq, None), P(OWN, None, seq, None), P(OWN, None, seq), P(), P()) + (weights,) * 8
    out_specs = (weights,) * 4 + (P(OWN),)
    return jax.shard_map(body, mesh=fine, in_specs=in_specs, out_specs=out_specs, check_vma=False)
```

profile of v0, /device:TPU:1, one launch (start us, length us, event | category | flops | bytes accessed | tf_op | source)
XLA Modules:
  0.0 270.7 jit_solution(2519268476389535878)
XLA Ops:
  7.2 0.0 copy-start
  7.2 0.0 copy-start.1
  7.2 0.0 all-gather.2.cloned.1.call-start
  7.2 0.7 concatenate.28
  8.0 2.0 concatenate.29
  10.0 0.0 all-gather.2.cloned.1.call-update
  10.0 0.0 copy-done
  10.0 0.2 multiply_reduce_fusion
  10.2 0.1 rsqrt.12
  10.3 0.0 copy-done.1
  10.3 0.2 multiply_convert_fusion
  10.5 7.8 %collective-permute-start = (bf16[128,2048]{1,0:T(8,128)(2,1)S(1)}, bf16[128,2048]{1,0:T(8,128)(2,1)S(1)}, u32[]{:S(2)}, u32[]{:S(2)}) collective-permute-start(bf16[128,2048]{1,0:T(8,128)(2,1)S(1)} %multiply_convert_fusion), channel_id=1, source_target_pairs={{0,4},{4,0},{1,5},{5,1},{2,6},{6,2},{3,7},{7,3},{8,12},{12,8},{9,1... | collective-permute-start | bytes 1572872 | tf_op jit(solution)/shard_map/ppermute | solution.py:262
  18.4 14.5 %collective-permute-done = bf16[128,2048]{1,0:T(8,128)(2,1)S(1)} collective-permute-done((bf16[128,2048]{1,0:T(8,128)(2,1)S(1)}, bf16[128,2048]{1,0:T(8,128)(2,1)S(1)}, u32[]{:S(2)}, u32[]{:S(2)}) %collective-permute-start) | collective-permute-done | bytes 524320 | tf_op jit(solution)/shard_map/ppermute | solution.py:262
  32.9 0.1 pad_maximum_fusion
  33.0 2.6 broadcast_in_dim.12
  35.6 0.0 copy-start.2
  35.6 0.0 copy-start.3
  35.6 5.0 %all-to-all-start = ((bf16[4,256,2048]{2,1,0:T(8,128)(2,1)}), bf16[4,256,2048]{2,1,0:T(8,128)(2,1)}, u32[]{:S(2)}, u32[]{:S(2)}) async-start(bf16[4,256,2048]{2,1,0:T(8,128)(2,1)} %broadcast_in_dim.12), calls=%async_computation | async-start | bytes 8388608 | tf_op jit(solution)/shard_map/all_to_all | solution.py:264
  40.6 0.1 iota_add_fusion
  40.7 0.1 convert_element_type.77
  40.8 0.1 add.99
  40.9 0.0 copy-done.2
  40.9 0.1 convert_element_type.79
  41.0 0.0 copy-done.3
  41.0 0.1 mul.115
  41.0 0.1 mul.116
  41.1 0.7 copy.23.sign
  41.9 1.9 fusion
  43.8 1.3 pad_maximum_fusion.1
  45.1 0.7 compare_select_fusion.bias
  45.9 36.7 %all-to-all-done = bf16[4,256,2048]{2,1,0:T(8,128)(2,1)} async-done(((bf16[4,256,2048]{2,1,0:T(8,128)(2,1)}), bf16[4,256,2048]{2,1,0:T(8,128)(2,1)}, u32[]{:S(2)}, u32[]{:S(2)}) %all-to-all-start) | async-done | bytes 4194336 | tf_op jit(solution)/shard_map/all_to_all | solution.py:264
  82.6 73.8 %all-gather.2.cloned.1.call-done.full = bf16[2048,5376]{1,0:T(8,128)(2,1)} async-done(((bf16[64,5376]{1,0:T(8,128)(2,1)}), bf16[2048,5376]{1,0:T(8,128)(2,1)}) %all-gather.2.cloned.1.call-update) | async-done | bytes 22020112 | tf_op jit(solution)/shard_map/all_gather | solution.py:258
  156.4 33.1 %shard_map.173 = bf16[4,33,16,256]{3,2,1,0:T(8,128)(2,1)} custom-call(s32[1]{0:T(128)} %bitcast.own_ref, bf16[2048,5376]{1,0:T(8,128)(2,1)} %all-gather.2.cloned.1.call-done.full, bf16[1024,2048]{1,0:T(8,128)(2,1)} %bitcast.2.xa_in, f32[1024,128]{1,0:T(8,128)} %get-tuple-element.13.kc, f32[1024,128]{1,0:T(8,128)} %get-tuple-element.14.ks, ...), custom_call_target="tpu_custom_call" | custom-call | flops 24000000000 | bytes 27000000 | tf_op jit(solution)/shard_map/pallas_call | solution.py:228
  189.5 16.5 %all_to_all.20 = bf16[4,33,16,256]{3,2,1,0:T(8,128)(2,1)S(1)} all-to-all(bf16[4,33,16,256]{3,2,1,0:T(8,128)(2,1)} %shard_map.173), channel_id=1, replica_groups=mesh['z'=4,'c'=2,'y'=4,'h'=2,'x'=4] {'y'}, dimensions={0} | all-to-all | bytes 2162688 | tf_op jit(solution)/shard_map/all_to_all | solution.py:284
  206.1 0.2 convert_reduce_fusion
  206.2 0.6 slice_reduce_fusion
  211.8 0.1 fusion.9
  211.9 0.8 collective-permute-start.1
  212.7 0.6 fusion.16
  213.3 7.9 %collective-permute-done.1 = bf16[33,16,256]{2,1,0:T(8,128)(2,1)S(1)} collective-permute-done((bf16[33,16,256]{2,1,0:T(8,128)(2,1)S(1)}, bf16[33,16,256]{2,1,0:T(8,128)(2,1)S(1)}, u32[]{:S(2)}, u32[]{:S(2)}) %collective-permute-start.1) | collective-permute-done | bytes 270368 | tf_op jit(solution)/shard_map/ppermute | solution.py:289
  221.2 0.6 fusion.15
  223.2 0.1 multiply_convert_fusion.1
  223.3 29.7 %all_to_all.21 = bf16[32,16,256]{2,1,0:T(8,128)(2,1)S(1)} all-to-all(bf16[32,16,256]{2,1,0:T(8,128)(2,1)S(1)} %multiply_convert_fusion.1), channel_id=1, replica_groups=mesh['z'=4,'c'=2,'y'=4,'h'=2,'x'=4] {'z','c','x'}, dimensions={0} | all-to-all | bytes 524288 | tf_op jit(solution)/shard_map/all_to_all | solution.py:294
  253.0 0.6 broadcast_in_dim.16
  253.6 3.3 %all-to-all-start.3 = ((f32[4,16,256]{2,1,0:T(8,128)}), f32[4,16,256]{2,1,0:T(8,128)S(1)}, u32[]{:S(2)}, u32[]{:S(2)}) async-start(f32[4,16,256]{2,1,0:T(8,128)} %broadcast_in_dim.16), calls=%async_computation.3 | async-start | bytes 131072 | tf_op jit(solution)/shard_map/all_to_all | solution.py:296
  257.0 4.3 %all-to-all-done.3 = f32[4,16,256]{2,1,0:T(8,128)S(1)} async-done(((f32[4,16,256]{2,1,0:T(8,128)}), f32[4,16,256]{2,1,0:T(8,128)S(1)}, u32[]{:S(2)}, u32[]{:S(2)}) %all-to-all-start.3) | async-done | bytes 65568 | tf_op jit(solution)/shard_map/all_to_all | solution.py:296
  261.4 0.7 fusion.17
  262.1 0.7 slice.49
  (10 shorter events, 0.2 us)
Async XLA Ops:
  7.2 2.9 %copy-start = (bf16[1,2,64,2048]{3,2,1,0:T(8,128)(2,1)S(1)}, bf16[1,2,64,2048]{3,2,1,0:T(8,128)(2,1)}, u32[]{:S(2)}) copy-start(bf16[1,2,64,2048]{3,2,1,0:T(8,128)(2,1)} %param.14) | copy-start | bytes 1572868
  7.2 3.2 %copy-start.1 = (f32[2048]{0:T(1024)S(1)}, f32[2048]{0:T(1024)}, u32[]{:S(2)}) copy-start(f32[2048]{0:T(1024)} %param.17) | copy-start | bytes 24580
  7.2 149.2 %all-gather.2.cloned.1.call-start = ((), (), s32[]{:S(2)}) async-start(), calls=%async_computation.4 | async-start | bytes 22708224 | tf_op jit(solution)/shard_map/all_gather | solution.py:258
  10.5 22.3 %collective-permute-start = (bf16[128,2048]{1,0:T(8,128)(2,1)S(1)}, bf16[128,2048]{1,0:T(8,128)(2,1)S(1)}, u32[]{:S(2)}, u32[]{:S(2)}) collective-permute-start(bf16[128,2048]{1,0:T(8,128)(2,1)S(1)} %multiply_convert_fusion), channel_id=1, source_target_pairs={{0,4},{4,0},{1,5},{5,1},{2,6},{6,2},{3,7},{7,3},{8,12},{12,8},{9,1... | collective-permute-start | bytes 1572872 | tf_op jit(solution)/shard_map/ppermute | solution.py:262
  35.6 5.3 %copy-start.2 = (s32[1,2,64]{2,1,0:T(2,128)S(1)}, s32[1,2,64]{2,1,0:T(2,128)}, u32[]{:S(2)}) copy-start(s32[1,2,64]{2,1,0:T(2,128)} %param.16) | copy-start | bytes 1540
  35.6 5.4 %copy-start.3 = (f32[2]{0:T(128)S(1)}, f32[2]{0:T(128)}, u32[]{:S(2)}) copy-start(f32[2]{0:T(128)} %constant.76.clone) | copy-start | bytes 28
  35.6 47.0 %all-to-all-start = ((bf16[4,256,2048]{2,1,0:T(8,128)(2,1)}), bf16[4,256,2048]{2,1,0:T(8,128)(2,1)}, u32[]{:S(2)}, u32[]{:S(2)}) async-start(bf16[4,256,2048]{2,1,0:T(8,128)(2,1)} %broadcast_in_dim.12), calls=%async_computation | async-start | bytes 8388608 | tf_op jit(solution)/shard_map/all_to_all | solution.py:264
  211.9 9.3 %collective-permute-start.1 = (bf16[33,16,256]{2,1,0:T(8,128)(2,1)S(1)}, bf16[33,16,256]{2,1,0:T(8,128)(2,1)S(1)}, u32[]{:S(2)}, u32[]{:S(2)}) collective-permute-start(bf16[33,16,256]{2,1,0:T(8,128)(2,1)S(1)} %pad_maximum_fusion.3), channel_id=1, source_target_pairs={{0,4},{4,0},{1,5},{5,1},{2,6},{6,2},{3,7},{7,3},{8,12},{12,8},{9,1... | collective-permute-start | bytes 811016 | tf_op jit(solution)/shard_map/ppermute | solution.py:289
  253.6 7.7 %all-to-all-start.3 = ((f32[4,16,256]{2,1,0:T(8,128)}), f32[4,16,256]{2,1,0:T(8,128)S(1)}, u32[]{:S(2)}, u32[]{:S(2)}) async-start(f32[4,16,256]{2,1,0:T(8,128)} %broadcast_in_dim.16), calls=%async_computation.3 | async-start | bytes 131072 | tf_op jit(solution)/shard_map/all_to_all | solution.py:296
Sparse Core Ops, SparseCore 0:
  10.2 146.2 all-gather.1
where the time goes:
time: 271 us
  waiting for transfers between devices  137 us (51%)
  blocking collectives  46.2 us (17%)
  Pallas kernels  33.1 us (12%)
  between operations  21.7 us (8%)
  starting transfers between devices  16.9 us (6%)
  local copies, waits for them, and re-layouts  8.66 us (3%)
  other arithmetic  6.77 us (2%)
    all_gather x1, waiting for transfers between devices, body(): full = lax.all_gather(packed, OWN, axis=0, tiled=True)  73.8 us
    all_to_all x1, waiting for transfers between devices, body(): lax.all_to_all(jnp.broadcast_to(two[None], (4,) + two.shape), 'y', 0, 0,...  36.7 us
    pallas_call x1, Pallas kernels, local_step(): pl.pallas_call(local_kernel, out_shape=jax.ShapeDtypeStruct((4, 33, 16, 4...  33.1 us
    all_to_all x1, blocking collectives, body(): shares = lax.all_to_all(scaled, OWN, 0, 0, tiled=True)  29.7 us
    all_to_all x1, blocking collectives, body(): lax.all_to_all(mine, 'y', 0, 0, tiled=True).astype(F32)  16.5 us
    ppermute x1, waiting for transfers between devices, body(): other = lax.ppermute(xn, 'h', [(0, 1), (1, 0)])  14.5 us
    ppermute x1, waiting for transfers between devices, body(): met = lax.ppermute(sent, 'h', [(0, 1), (1, 0)])  7.91 us
    ppermute x1, starting transfers between devices, body(): other = lax.ppermute(xn, 'h', [(0, 1), (1, 0)])  7.83 us
  transfers between devices with their start and end apart: 5, of which 5 were waited for; matrix products, arithmetic and copies ran while one was open for 3% of the time, Pallas kernels for 0%

commit v1 on v0

--- a/solution.py
+++ b/solution.py
@@ -51,27 +51,26 @@
     return jnp.sum(a * b, axis=-1, keepdims=True)
 
 
-def local_kernel(own_ref, full, xa_in, kc, ks, bias, hid, ans, gain, sign, out,
-                 xa, wn, wkv, wq, wo, low, bqm, bvm, keys, vref, vpol, qs, prob, probb, o32, heads, yp, by, bo, bq, vt, dn, sems):
+def local_kernel(own_ref, full, xa, kc, ks, bias, hid, ans, gain, sign, out,
+                 wn, wkv, wq, wo, low, bqm, bvm, keys, vref, vpol, qs, prob, probb, o32, heads, yp, by, bo, bq, vt, dn, sems):
     copies = [
-        pltpu.make_async_copy(xa_in, xa, sems.at[0]),
-        pltpu.make_async_copy(full.at[:, 5120:5376], wn, sems.at[1]),
-        pltpu.make_async_copy(full.at[:, 2048:3072], wkv, sems.at[2]),
-        pltpu.make_async_copy(full.at[:, 0:2048], wq, sems.at[3]),
-        pltpu.make_async_copy(full.at[:, 3072:5120], wo, sems.at[4]),
+        pltpu.make_async_copy(full.at[0, :, 0:256], wn, sems.at[0]),
+        pltpu.make_async_copy(full.at[1, :, 0:1024], wkv, sems.at[1]),
+        pltpu.make_async_copy(full.at[0, :, 256:2304], wq, sems.at[2]),
+        pltpu.make_async_copy(full.at[0, :, 2304:2688], wo.at[:, 0:384], sems.at[3]),
+        pltpu.make_async_copy(full.at[1, :, 1024:2688], wo.at[:, 384:2048], sems.at[4]),
     ]
     for copy in copies:
         copy.start()
     own = pl.multiple_of(own_ref[0] * ROWS, ROWS)
 
     copies[0].wait()
-    copies[1].wait()
     lane = lax.broadcasted_iota(jnp.int32, (D, 2 * RANK), 1)
     bqm[...] = jnp.where(lane < RANK, wn[:, 2 * RANK :].astype(F32), 0.0).astype(BF)
     lane16 = lax.broadcasted_iota(jnp.int32, (16, 2 * RANK), 1)
     for d in range(32):
         bvm[16 * d : 16 * d + 16, :] = jnp.where(lane16 >= RANK, wn[64 * d : 64 * d + 16, 2 * RANK :].astype(F32), 0.0).astype(BF)
-    copies[2].wait()
+    copies[1].wait()
 
     @pl.loop(0, ALL // 256)
     def _(r):
@@ -96,7 +95,7 @@
                     vref[at, pl.ds(t0, TOK), :] = vr[src]
                     vpol[at, pl.ds(t0, TOK), :] = vp[src]
 
-    copies[3].wait()
+    copies[2].wait()
     c_own, s_own = kc[pl.ds(own, ROWS), :], ks[pl.ds(own, ROWS), :]
 
     @pl.loop(0, HK)
@@ -141,6 +140,7 @@
             heads[pl.ds(r0, TOK), pl.ds(c0, HD)] = n0[j * TOK : j * TOK + TOK]
             heads[pl.ds(r0 + ROWS, TOK), pl.ds(c0, HD)] = n1[j * TOK : j * TOK + TOK]
 
+    copies[3].wait()
     copies[4].wait()
     tile = 512
     zero = jnp.zeros((ROWS, 1), F32)
@@ -199,27 +199,52 @@
     dn_t = dn[...].T
     low_t = low[...].T
     low_own_t = low[pl.ds(own, ROWS), :].T
-    lane64 = lax.broadcasted_iota(jnp.int32, (256, 2 * RANK), 1)
+    left = lane16 < RANK
     for n in range(D // tile):
         cols = slice(n * tile, n * tile + tile)
         ga_t = (ADAPTER_SCALE * mm(dn_t, xa[:, cols])).T
         gb_t = (ADAPTER_SCALE * mm(low_own_t, bq[:, cols])).T
         for d in range(tile // TOK):
+            at = n * (tile // TOK) + d
+            ga, gb = ga_t[d * TOK : d * TOK + TOK], gb_t[d * TOK : d * TOK + TOK]
             for q in range(4):
-                src = slice(d * TOK + q * 16, d * TOK + q * 16 + 16)
-                out[q, n * (tile // TOK) + d, :, : 2 * RANK] = ga_t[src].astype(BF)
-                out[q, n * (tile // TOK) + d, :, 2 * RANK :] = jnp.where(lane16 < RANK, gb_t[src], 0.0).astype(BF)
+                out[q, at] = ga[q * 16 : q * 16 + 16].astype(BF)
+            for q in range(2):
+                out[4 + q, at] = jnp.where(left, gb[q * 32 : q * 32 + 16], pltpu.roll(gb[q * 32 + 16 : q * 32 + 32], RANK, 1)).astype(BF)
     gv_t = (ADAPTER_SCALE * mm(low_t, vt[...])).T
     for d in range(32):
-        here = out[0, d, :, 2 * RANK :].astype(F32)
-        out[0, d, :, 2 * RANK :] = jnp.where(lane16 < RANK, here, gv_t[16 * d : 16 * d + 16]).astype(BF)
+        out[6, d] = jnp.where(left, pltpu.roll(gv_t[16 * d : 16 * d + 16], RANK, 1), 0.0).astype(BF)
+        out[7, d] = jnp.zeros((16, 2 * RANK), BF)
     hi = margin.astype(BF).astype(F32)
     mid = (margin - hi).astype(BF).astype(F32)
     lo = margin - hi - mid
-    lane_m = lax.broadcasted_iota(jnp.int32, (16, 4 * RANK), 1)
-    riding = jnp.where(lane_m == 0, hi, jnp.where(lane_m == 1, mid, jnp.where(lane_m == 2, lo, 0.0))).astype(BF)
-    for q in range(4):
+    riding = jnp.where(lane16 == 0, hi, jnp.where(lane16 == 1, mid, jnp.where(lane16 == 2, lo, 0.0))).astype(BF)
+    for q in range(8):
         out[q, 32] = riding
+
+
+def scale_kernel(got, scaled, margin_out):
+    ride = got[0, 32].astype(F32)
+    for q in range(1, 8):
+        ride = ride + got[q, 32].astype(F32)
+    margin = jnp.sum(ride[0:1, :], axis=-1, keepdims=True)
+    margin_out[...] = jnp.broadcast_to(margin, (8, 2 * RANK))
+    weight = -BETA / (1.0 + jnp.exp(BETA * margin))
+    total = got[0, 0:32].astype(F32)
+    for q in range(1, 8):
+        total = total + got[q, 0:32].astype(F32)
+    scaled[...] = (total * weight[None]).astype(BF)
+
+
+def scale_step(got):
+    vm = pl.BlockSpec(memory_space=pltpu.VMEM)
+    return pl.pallas_call(
+        scale_kernel,
+        out_shape=(jax.ShapeDtypeStruct((32, 16, 2 * RANK), BF), jax.ShapeDtypeStruct((8, 2 * RANK), F32)),
+        in_specs=[vm],
+        out_specs=(vm, vm),
+        compiler_params=pltpu.CompilerParams(vmem_limit_bytes=16 * 2**20),
+    )(got)
 
 
 def local_step(own_block, full, xa, kc, ks, bias, hid, ans, gain, sign):
@@ -227,26 +252,20 @@
     bf, f32 = (lambda *s: pltpu.VMEM(s, BF)), (lambda *s: pltpu.VMEM(s, F32))
     return pl.pallas_call(
         local_kernel,
-        out_shape=jax.ShapeDtypeStruct((4, 33, 16, 4 * RANK), BF),
-        in_specs=[pl.BlockSpec(memory_space=pltpu.SMEM), anyspace, anyspace] + [vm] * 7,
+        out_shape=jax.ShapeDtypeStruct((8, 33, 16, 2 * RANK), BF),
+        in_specs=[pl.BlockSpec(memory_space=pltpu.SMEM), anyspace] + [vm] * 8,
         out_specs=vm,
         scratch_shapes=[
-            bf(ALL, D), bf(D, 256), bf(D, 2 * KVW), bf(D, D), bf(D, D),
+            bf(D, 256), bf(D, 2 * KVW), bf(D, D), bf(D, D),
             bf(ALL, 2 * RANK), bf(D, 2 * RANK), bf(KVW, 2 * RANK),
             bf(PARTS, L, HD), bf(PARTS, L, HD), bf(PARTS, L, HD),
             bf(2, PARTS, QROWS, HD), f32(PARTS, QROWS, L), bf(PARTS, QROWS, L), f32(PARTS, QROWS, HD),
             bf(2 * ROWS, D), f32(ROWS, D), bf(ROWS, D), bf(PARTS, QROWS, HD), bf(ROWS, D), bf(ALL, KVW), bf(ALL, 2 * RANK),
             pltpu.SemaphoreType.DMA((5,)),
         ],
-        compiler_params=pltpu.CompilerParams(vmem_limit_bytes=60 * 2**20),
+        compiler_params=pltpu.CompilerParams(vmem_limit_bytes=50 * 2**20),
         cost_estimate=pl.CostEstimate(flops=24_000_000_000, bytes_accessed=27_000_000, transcendentals=2_100_000),
     )(own_block, full, xa, kc, ks, bias, hid, ans, gain, sign)
-
-
-def split3(value):
-    hi = lax.reduce_precision(value, 8, 7)
-    mid = lax.reduce_precision(value - hi, 8, 7)
-    return jnp.stack([hi, mid, value - hi - mid], axis=-1)
 
 
 def body(hidden, answer_rows, resp_mask, attn_gain, final_gain, w_query, w_key, w_value, w_out, a_query, b_query, a_value, b_value):
@@ -254,8 +273,10 @@
     y_pos, h_pos = lax.axis_index("y"), lax.axis_index("h")
 
     narrow_v = jnp.concatenate([b_value, jnp.zeros((TOK - b_value.shape[0], RANK), BF)], axis=0)
-    packed = jnp.concatenate([w_query, w_key, w_value, w_out, a_query, a_value, b_query, narrow_v], axis=1)
-    full = lax.all_gather(packed, OWN, axis=0, tiled=True)
+    half0 = jnp.concatenate([a_query, a_value, b_query, narrow_v, w_query, w_out[:, :384]], axis=1)
+    half1 = jnp.concatenate([w_key, w_value, w_out[:, 384:]], axis=1)
+    packed = jnp.where(h_pos == 0, half0, half1)
+    full = lax.all_gather(packed, ("h",) + OWN, axis=0, tiled=True).reshape(2, D, half0.shape[1])
 
     x32 = hidden.astype(F32)
     xn = (x32 * lax.rsqrt(jnp.mean(x32 * x32, axis=-1, keepdims=True) + EPS) * attn_gain).astype(BF).reshape(ROWS, D)
@@ -281,20 +302,16 @@
 
     mine = local_step(own_block, full, xa, kc, ks, bias, hidden.reshape(ROWS, D), answer_rows.reshape(ROWS, D), final_gain.reshape(1, D), sign)
 
-    got = jnp.sum(lax.all_to_all(mine, "y", 0, 0, tiled=True).astype(F32), axis=0)
-    first = jnp.sum(got[32, 0, :3]).reshape(1)
-    sent = got.astype(BF)
-    sent = jnp.concatenate([sent[:32], jnp.pad(split3(first).astype(BF).reshape(1, 1, 3), ((0, 0), (0, 15), (0, 253)))], axis=0)
-    sent = lax.optimization_barrier(sent)
-    met = lax.ppermute(sent, "h", [(0, 1), (1, 0)])
-    margin = jnp.sum(sent[32, 0, :3].astype(F32)).reshape(1) + jnp.sum(met[32, 0, :3].astype(F32)).reshape(1)
-    loss = jax.nn.softplus(-BETA * margin)
-    weight = -BETA * jax.nn.sigmoid(-BETA * margin)
-    scaled = (weight * (sent[:32].astype(F32) + met[:32].astype(F32))).astype(BF)
+    seq = ("y", "h")
+    scaled, margin = scale_step(lax.all_to_all(mine, seq, 0, 0, tiled=True))
     shares = lax.all_to_all(scaled, OWN, 0, 0, tiled=True)
+    loss = jax.nn.softplus(-BETA * margin[0, :1])
     piece = jnp.sum(shares.astype(F32), axis=0)
-    total = lax.all_to_all(jnp.broadcast_to(piece[None], (4,) + piece.shape), "y", 0, 0, tiled=True).reshape(TOK, 4 * RANK)
-    return total[:, :64], total[:, 128:192], total[:, 64:128], total[:16, 192:], loss
+    total = lax.all_to_all(jnp.broadcast_to(piece[None], (8,) + piece.shape), seq, 0, 0, tiled=True)
+    grad_a = total[:4].reshape(TOK, 2 * RANK)
+    low_half, high_half = total[4:6, :, :RANK], total[4:6, :, RANK:]
+    grad_b_q = jnp.stack([low_half, high_half], axis=1).reshape(TOK, RANK)
+    return grad_a[:, :RANK], grad_b_q, grad_a[:, RANK:], total[6, :, :RANK], loss
 
 
 def solution(mesh):

time: 271 us -> 242 us (0.89)
  waiting for transfers between devices: 137 us -> 112 us
  between operations: 21.7 us -> 16.1 us
  blocking collectives: 46.2 us -> 51.1 us
    all_gather x1, waiting for transfers between devices: 73.8 us -> 47.7 us  [body(): lax.all_gather(packed, ('h',) + OWN, axis=0, tiled=True)]
    all_to_all x1, blocking collectives: 16.5 us -> 28 us  [body(): scaled, margin = scale_step(lax.all_to_all(mine, seq, 0, 0, tiled=True))]
    ppermute x1 -> x0, waiting for transfers between devices: 7.91 us -> none  [body(): met = lax.ppermute(sent, 'h', [(0, 1), (1, 0)])]
    all_to_all x1, blocking collectives: 29.7 us -> 23.1 us  [body(): shares = lax.all_to_all(scaled, OWN, 0, 0, tiled=True)]
    all_to_all x1, waiting for transfers between devices: 36.7 us -> 41 us  [body(): lax.all_to_all(jnp.broadcast_to(two[None], (4,) + two.shape), 'y', 0, 0,...]
    all_to_all x1, waiting for transfers between devices: 4.35 us -> 7.77 us  [body(): lax.all_to_all(jnp.broadcast_to(piece[None], (8,) + piece.shape), seq, 0,...]
    pallas_call x1 -> x2, Pallas kernels: 33.1 us -> 32 us  [the longest x1 31.8 us: local_step(): pl.pallas_call(local_kernel, out_shape=jax.ShapeDtypeStruct((8, 33, 16, 2...]
  transfers between devices with their start and end apart: 5 -> 4, of which waited for: 5 -> 4; matrix products, arithmetic and copies ran while one was open for 3% -> 3% of each run, Pallas kernels for 0% -> 0%
where the time goes in v1:
time: 242 us
  waiting for transfers between devices  112 us (46%)
  blocking collectives  51.1 us (21%)
  Pallas kernels  32 us (13%)
  starting transfers between devices  16.2 us (7%)
  between operations  16.1 us (7%)
  local copies, waits for them, and re-layouts  9.38 us (4%)
  other arithmetic  5.24 us (2%)
    all_gather x1, waiting for transfers between devices, body(): lax.all_gather(packed, ('h',) + OWN, axis=0, tiled=True)  47.7 us
    all_to_all x1, waiting for transfers between devices, body(): lax.all_to_all(jnp.broadcast_to(two[None], (4,) + two.shape), 'y', 0, 0,...  41 us
    pallas_call x1, Pallas kernels, local_step(): pl.pallas_call(local_kernel, out_shape=jax.ShapeDtypeStruct((8, 33, 16, 2...  31.8 us
    all_to_all x1, blocking collectives, body(): scaled, margin = scale_step(lax.all_to_all(mine, seq, 0, 0, tiled=True))  28 us
    all_to_all x1, blocking collectives, body(): shares = lax.all_to_all(scaled, OWN, 0, 0, tiled=True)  23.1 us
    ppermute x1, waiting for transfers between devices, body(): other = lax.ppermute(xn, 'h', [(0, 1), (1, 0)])  15.1 us
    ppermute x1, starting transfers between devices, body(): other = lax.ppermute(xn, 'h', [(0, 1), (1, 0)])  7.83 us
    all_to_all x1, waiting for transfers between devices, body(): lax.all_to_all(jnp.broadcast_to(piece[None], (8,) + piece.shape), seq, 0,...  7.77 us
  transfers between devices with their start and end apart: 4, of which 4 were waited for; matrix products, arithmetic and copies ran while one was open for 3% of the time, Pallas kernels for 0%

profile of v1, /device:TPU:1, one launch (start us, length us, event | category | flops | bytes accessed | tf_op | source)
XLA Modules:
  0.0 241.5 jit_solution(7457506027831557564)
XLA Ops:
  7.2 0.0 copy-start
  7.2 0.0 copy-start.3
  7.2 0.0 all-gather.2.cloned.1.call-start
  7.2 0.9 slice.27
  8.1 0.9 slice.28
  9.0 0.7 concatenate.18
  9.7 1.1 concatenate.19
  10.8 1.7 maximum_select_fusion
  12.5 0.0 all-gather.2.cloned.1.call-update
  12.5 0.0 copy-done
  12.5 0.2 multiply_reduce_fusion
  12.7 0.1 rsqrt.12
  12.8 0.0 copy-done.3
  12.8 0.2 multiply_convert_fusion
  13.0 7.8 %collective-permute-start = (bf16[128,2048]{1,0:T(8,128)(2,1)S(1)}, bf16[128,2048]{1,0:T(8,128)(2,1)S(1)}, u32[]{:S(2)}, u32[]{:S(2)}) collective-permute-start(bf16[128,2048]{1,0:T(8,128)(2,1)S(1)} %multiply_convert_fusion), channel_id=1, source_target_pairs={{0,4},{4,0},{1,5},{5,1},{2,6},{6,2},{3,7},{7,3},{8,12},{12,8},{9,1... | collective-permute-start | bytes 1572872 | tf_op jit(solution)/shard_map/ppermute | solution.py:283
  20.9 15.1 %collective-permute-done = bf16[128,2048]{1,0:T(8,128)(2,1)S(1)} collective-permute-done((bf16[128,2048]{1,0:T(8,128)(2,1)S(1)}, bf16[128,2048]{1,0:T(8,128)(2,1)S(1)}, u32[]{:S(2)}, u32[]{:S(2)}) %collective-permute-start) | collective-permute-done | bytes 524320 | tf_op jit(solution)/shard_map/ppermute | solution.py:283
  35.9 0.1 pad_maximum_fusion
  36.1 2.6 %broadcast_in_dim.12 = bf16[4,256,2048]{2,1,0:T(8,128)(2,1)} broadcast(bf16[256,2048]{1,0:T(8,128)(2,1)S(1)} %pad_maximum_fusion), dimensions={1,2} | broadcast | bytes 5242880 | tf_op jit(solution)/shard_map/broadcast_in_dim | solution.py:285
  38.7 0.0 copy-start.4
  38.7 0.0 copy-start.5
  38.7 5.0 %all-to-all-start = ((bf16[4,256,2048]{2,1,0:T(8,128)(2,1)}), bf16[4,256,2048]{2,1,0:T(8,128)(2,1)}, u32[]{:S(2)}, u32[]{:S(2)}) async-start(bf16[4,256,2048]{2,1,0:T(8,128)(2,1)} %broadcast_in_dim.12), calls=%async_computation | async-start | bytes 8388608 | tf_op jit(solution)/shard_map/all_to_all | solution.py:285
  43.8 0.1 iota_add_fusion
  43.8 0.1 convert_element_type.42
  43.9 0.1 add.87
  44.0 0.0 copy-done.4
  44.0 0.1 convert_element_type.44
  44.1 0.0 copy-done.5
  44.1 0.1 mul.101
  44.2 0.1 mul.102
  44.3 0.1 copy.24.sign
  44.4 0.0 copy-start.1
  44.4 0.0 copy-start.2
  44.4 1.9 fusion
  46.3 0.3 pad_maximum_fusion.1
  46.7 0.1 compare_select_fusion.bias
  46.7 41.0 %all-to-all-done = bf16[4,256,2048]{2,1,0:T(8,128)(2,1)} async-done(((bf16[4,256,2048]{2,1,0:T(8,128)(2,1)}), bf16[4,256,2048]{2,1,0:T(8,128)(2,1)}, u32[]{:S(2)}, u32[]{:S(2)}) %all-to-all-start) | async-done | bytes 4194336 | tf_op jit(solution)/shard_map/all_to_all | solution.py:285
  87.8 47.7 %all-gather.2.cloned.1.call-done = bf16[4096,2688]{1,0:T(8,128)(2,1)} async-done(((bf16[64,2688]{1,0:T(8,128)(2,1)}), bf16[4096,2688]{1,0:T(8,128)(2,1)}) %all-gather.2.cloned.1.call-update) | async-done | bytes 22020112 | tf_op jit(solution)/shard_map/all_gather | solution.py:279
  135.4 0.0 copy-done.1
  135.4 0.0 copy-done.2
  135.4 31.8 %shard_map.173 = bf16[8,33,16,128]{3,2,1,0:T(8,128)(2,1)S(1)} custom-call(s32[1]{0:T(128)} %bitcast.own_ref, bf16[2,2048,2688]{2,1,0:T(8,128)(2,1)} %bitcast.23, bf16[1024,2048]{1,0:T(8,128)(2,1)} %bitcast.3.xa, f32[1024,128]{1,0:T(8,128)S(1)} %get-tuple-element.18.kc, f32[1024,128]{1,0:T(8,128)S(1)} %get-tuple-element.19.ks, ...), custom_call_target="tpu_custom_call" | custom-call | flops 24000000000 | bytes 27000000 | tf_op jit(solution)/shard_map/pallas_call | solution.py:253
  167.2 28.0 %all_to_all.20.got = bf16[8,33,16,128]{3,2,1,0:T(8,128)(2,1)S(1)} all-to-all(bf16[8,33,16,128]{3,2,1,0:T(8,128)(2,1)S(1)} %shard_map.173), channel_id=1, replica_groups=mesh['z'=4,'c'=2,'y'=4,'h'=2,'x'=4] {'y','h'}, dimensions={0} | all-to-all | bytes 2162688 | tf_op jit(solution)/shard_map/all_to_all | solution.py:306
  195.2 0.2 shard_map.174
  195.4 23.1 %all_to_all.21 = bf16[32,16,128]{2,1,0:T(8,128)(2,1)S(1)} all-to-all(bf16[32,16,128]{2,1,0:T(8,128)(2,1)S(1)} %get-tuple-element.7), channel_id=1, replica_groups=mesh['z'=4,'c'=2,'y'=4,'h'=2,'x'=4] {'z','c','x'}, dimensions={0} | all-to-all | bytes 262144 | tf_op jit(solution)/shard_map/all_to_all | solution.py:307
  218.5 0.6 broadcast_in_dim.16
  219.2 3.3 %all-to-all-start.3 = ((f32[8,16,128]{2,1,0:T(8,128)}), f32[8,16,128]{2,1,0:T(8,128)S(1)}, u32[]{:S(2)}, u32[]{:S(2)}) async-start(f32[8,16,128]{2,1,0:T(8,128)} %broadcast_in_dim.16), calls=%async_computation.3 | async-start | bytes 131072 | tf_op jit(solution)/shard_map/all_to_all | solution.py:310
  222.5 0.5 slice.35
  223.8 7.8 %all-to-all-done.3 = f32[8,16,128]{2,1,0:T(8,128)S(1)} async-done(((f32[8,16,128]{2,1,0:T(8,128)}), f32[8,16,128]{2,1,0:T(8,128)S(1)}, u32[]{:S(2)}, u32[]{:S(2)}) %all-to-all-start.3) | async-done | bytes 65568 | tf_op jit(solution)/shard_map/all_to_all | solution.py:310
  231.6 0.7 fusion.6
  232.2 0.1 slice_bitcast_fusion.1
  232.3 0.6 pad_maximum_fusion.3
  232.9 0.6 slice_bitcast_fusion.2
  (9 shorter events, 0.1 us)
Async XLA Ops:
  7.2 5.4 %copy-start = (bf16[1,2,64,2048]{3,2,1,0:T(8,128)(2,1)S(1)}, bf16[1,2,64,2048]{3,2,1,0:T(8,128)(2,1)}, u32[]{:S(2)}) copy-start(bf16[1,2,64,2048]{3,2,1,0:T(8,128)(2,1)} %param.14) | copy-start | bytes 1572868
  7.2 5.7 %copy-start.3 = (f32[2048]{0:T(1024)S(1)}, f32[2048]{0:T(1024)}, u32[]{:S(2)}) copy-start(f32[2048]{0:T(1024)} %param.17) | copy-start | bytes 24580
  7.2 128.2 %all-gather.2.cloned.1.call-start = ((), (), s32[]{:S(2)}) async-start(), calls=%async_computation.4 | async-start | bytes 22364160 | tf_op jit(solution)/shard_map/all_gather | solution.py:279
  13.0 22.9 %collective-permute-start = (bf16[128,2048]{1,0:T(8,128)(2,1)S(1)}, bf16[128,2048]{1,0:T(8,128)(2,1)S(1)}, u32[]{:S(2)}, u32[]{:S(2)}) collective-permute-start(bf16[128,2048]{1,0:T(8,128)(2,1)S(1)} %multiply_convert_fusion), channel_id=1, source_target_pairs={{0,4},{4,0},{1,5},{5,1},{2,6},{6,2},{3,7},{7,3},{8,12},{12,8},{9,1... | collective-permute-start | bytes 1572872 | tf_op jit(solution)/shard_map/ppermute | solution.py:283
  38.7 5.3 %copy-start.4 = (s32[1,2,64]{2,1,0:T(2,128)S(1)}, s32[1,2,64]{2,1,0:T(2,128)}, u32[]{:S(2)}) copy-start(s32[1,2,64]{2,1,0:T(2,128)} %param.16) | copy-start | bytes 1540
  38.7 5.4 %copy-start.5 = (f32[2]{0:T(128)S(1)}, f32[2]{0:T(128)}, u32[]{:S(2)}) copy-start(f32[2]{0:T(128)} %constant.72.clone) | copy-start | bytes 28
  38.7 49.1 %all-to-all-start = ((bf16[4,256,2048]{2,1,0:T(8,128)(2,1)}), bf16[4,256,2048]{2,1,0:T(8,128)(2,1)}, u32[]{:S(2)}, u32[]{:S(2)}) async-start(bf16[4,256,2048]{2,1,0:T(8,128)(2,1)} %broadcast_in_dim.12), calls=%async_computation | async-start | bytes 8388608 | tf_op jit(solution)/shard_map/all_to_all | solution.py:285
  44.4 91.0 %copy-start.1 = (bf16[1,2,64,2048]{3,2,1,0:T(8,128)(2,1)S(1)}, bf16[1,2,64,2048]{3,2,1,0:T(8,128)(2,1)}, u32[]{:S(2)}) copy-start(bf16[1,2,64,2048]{3,2,1,0:T(8,128)(2,1)} %param.15) | copy-start | bytes 1572868
  44.4 91.0 %copy-start.2 = (f32[2048]{0:T(1024)S(1)}, f32[2048]{0:T(1024)}, u32[]{:S(2)}) copy-start(f32[2048]{0:T(1024)} %param.18) | copy-start | bytes 24580
  219.2 12.4 %all-to-all-start.3 = ((f32[8,16,128]{2,1,0:T(8,128)}), f32[8,16,128]{2,1,0:T(8,128)S(1)}, u32[]{:S(2)}, u32[]{:S(2)}) async-start(f32[8,16,128]{2,1,0:T(8,128)} %broadcast_in_dim.16), calls=%async_computation.3 | async-start | bytes 131072 | tf_op jit(solution)/shard_map/all_to_all | solution.py:310
Sparse Core Ops, SparseCore 0:
  12.7 122.7 all-gather.1

commit v2 on v1

--- a/solution.py
+++ b/solution.py
@@ -22,6 +22,7 @@
 L = BLOCKS * TOK
 PARTS = 2 * HK
 QROWS = GROUP * TOK
+PIECES = 4
 
 EPS = 1e-05
 BETA = 0.1
@@ -51,36 +52,61 @@
     return jnp.sum(a * b, axis=-1, keepdims=True)
 
 
+def split3(margin):
+    lane = lax.broadcasted_iota(jnp.int32, (16, 2 * RANK), 1)
+    hi = margin.astype(BF).astype(F32)
+    mid = (margin - hi).astype(BF).astype(F32)
+    lo = margin - hi - mid
+    return jnp.where(lane == 0, hi, jnp.where(lane == 1, mid, jnp.where(lane == 2, lo, 0.0))).astype(BF)
+
+
 def local_kernel(own_ref, full, xa, kc, ks, bias, hid, ans, gain, sign, out,
-                 wn, wkv, wq, wo, low, bqm, bvm, keys, vref, vpol, qs, prob, probb, o32, heads, yp, by, bo, bq, vt, dn, sems):
+                 wn, wkv, wq, wo, low, bv, keys, vref, vpol, qs, prob, probb, o32, heads, yp, by, bo, bq, vt, dn, sems):
+    half = D // PIECES
+
+    def pieces(first, h, cols, dst, at):
+        made = []
+        for n in range(PIECES):
+            rows = pl.ds(n * half, half)
+            made.append(pltpu.make_async_copy(full.at[h, rows, cols[0] : cols[1]], dst.at[rows, at[0] : at[1]], sems.at[first, n]))
+        return made
+
     copies = [
-        pltpu.make_async_copy(full.at[0, :, 0:256], wn, sems.at[0]),
-        pltpu.make_async_copy(full.at[1, :, 0:1024], wkv, sems.at[1]),
-        pltpu.make_async_copy(full.at[0, :, 256:2304], wq, sems.at[2]),
-        pltpu.make_async_copy(full.at[0, :, 2304:2688], wo.at[:, 0:384], sems.at[3]),
-        pltpu.make_async_copy(full.at[1, :, 1024:2688], wo.at[:, 384:2048], sems.at[4]),
+        pieces(0, 0, (0, 256), wn, (0, 256)),
+        pieces(1, 1, (0, 1024), wkv, (0, 1024)),
+        pieces(2, 0, (256, 2304), wq, (0, 2048)),
+        pieces(3, 0, (2304, 2688), wo, (0, 384)),
+        pieces(4, 1, (1024, 2688), wo, (384, 2048)),
     ]
-    for copy in copies:
-        copy.start()
+    def begin(first):
+        for copy in copies[first]:
+            copy.start()
+
+    def arrived(first):
+        for copy in copies[first]:
+            copy.wait()
+
+    begin(0)
+    begin(1)
+
     own = pl.multiple_of(own_ref[0] * ROWS, ROWS)
 
-    copies[0].wait()
-    lane = lax.broadcasted_iota(jnp.int32, (D, 2 * RANK), 1)
-    bqm[...] = jnp.where(lane < RANK, wn[:, 2 * RANK :].astype(F32), 0.0).astype(BF)
-    lane16 = lax.broadcasted_iota(jnp.int32, (16, 2 * RANK), 1)
+    arrived(0)
+    lane_of = lambda n: lax.broadcasted_iota(jnp.int32, (n, 2 * RANK), 1)
     for d in range(32):
-        bvm[16 * d : 16 * d + 16, :] = jnp.where(lane16 >= RANK, wn[64 * d : 64 * d + 16, 2 * RANK :].astype(F32), 0.0).astype(BF)
-    copies[1].wait()
-
-    @pl.loop(0, ALL // 256)
+        bv[16 * d : 16 * d + 16, :] = wn[64 * d : 64 * d + 16, 2 * RANK :]
+    arrived(1)
+    begin(2)
+
+    @pl.loop(0, ALL // 256, unroll=2)
     def _(r):
         r0 = pl.multiple_of(r * 256, 256)
         x = xa[pl.ds(r0, 256), :]
-        lw = mm(x, wn[:, : 2 * RANK]).astype(BF)
-        low[pl.ds(r0, 256), :] = lw
+        lw = mm(x, wn[:, : 2 * RANK])
+        low[pl.ds(r0, 256), :] = lw.astype(BF)
         c, s = kc[pl.ds(r0, 256), :], ks[pl.ds(r0, 256), :]
         kv = mm(x, wkv[...])
-        lift = mm_t(lw, bvm[...])
+        lift = mm_t(jnp.where(lane_of(256) < RANK, 0.0, lw).astype(BF), bv[...])
         for g in range(HK):
             cols = slice(HD * g, HD * g + HD)
             k = turn(kv[:, cols], c, s).astype(BF)
@@ -95,14 +121,18 @@
                     vref[at, pl.ds(t0, TOK), :] = vr[src]
                     vpol[at, pl.ds(t0, TOK), :] = vp[src]
 
-    copies[2].wait()
+    arrived(2)
+    begin(3)
+    begin(4)
+    low_own = low[pl.ds(own, ROWS), :].astype(F32)
+    low_q = jnp.where(lane_of(ROWS) < RANK, low_own, 0.0).astype(BF)
     c_own, s_own = kc[pl.ds(own, ROWS), :], ks[pl.ds(own, ROWS), :]
 
-    @pl.loop(0, HK)
+    @pl.loop(0, HK, unroll=True)
     def _(g):
         w0 = pl.multiple_of(g * GROUP * HD, GROUP * HD)
         base = mm(xa[pl.ds(own, ROWS), :], wq[:, pl.ds(w0, GROUP * HD)])
-        lift = mm_t(low[pl.ds(own, ROWS), :], bqm[pl.ds(w0, GROUP * HD), :])
+        lift = mm_t(low_q, wn[pl.ds(w0, GROUP * HD), 2 * RANK :])
         moved = base + ADAPTER_SCALE * lift
         for j in range(GROUP):
             cols = slice(HD * j, HD * j + HD)
@@ -116,12 +146,12 @@
     scale = 1.0 / math.sqrt(HD)
 
     def soft(q, k):
-        logits = mm_t(q, k) * scale
-        logits = (logits.reshape(GROUP, TOK, L) + bias[...][None]).reshape(QROWS, L)
-        raised = jnp.exp(logits - jnp.max(logits, axis=-1, keepdims=True))
+        logits = mm_t(q, k).reshape(GROUP, TOK, L) * (scale * math.log2(math.e)) + bias[...][None]
+        logits = logits.reshape(QROWS, L)
+        raised = jnp.exp2(logits - jnp.max(logits, axis=-1, keepdims=True))
         return raised * (1.0 / jnp.sum(raised, axis=-1, keepdims=True))
 
-    @pl.loop(0, PARTS)
+    @pl.loop(0, PARTS, unroll=2)
     def _(i):
         g, side = lax.rem(i, HK), lax.div(i, HK)
         k = keys[i]
@@ -140,8 +170,8 @@
             heads[pl.ds(r0, TOK), pl.ds(c0, HD)] = n0[j * TOK : j * TOK + TOK]
             heads[pl.ds(r0 + ROWS, TOK), pl.ds(c0, HD)] = n1[j * TOK : j * TOK + TOK]
 
-    copies[3].wait()
-    copies[4].wait()
+    arrived(3)
+    arrived(4)
     tile = 512
     zero = jnp.zeros((ROWS, 1), F32)
     sq0, sq1, sc0, sc1 = zero, zero, zero, zero
@@ -166,21 +196,23 @@
         ga = gain[:, cols] * ans[:, cols].astype(F32)
         by[:, cols] = (lead * (ga - yp[:, cols] * pull)).astype(BF)
 
-    @pl.loop(0, HK)
+    by_t = by[...].T
+
+    @pl.loop(0, HK, unroll=True)
     def _(g):
         w0 = pl.multiple_of(g * GROUP * HD, GROUP * HD)
-        back = mm_t(by[...], wo[pl.ds(w0, GROUP * HD), :]).astype(BF)
+        back = mm(wo[pl.ds(w0, GROUP * HD), :], by_t).T.astype(BF)
         for j in range(GROUP):
             for side in range(2):
                 bo[side * HK + g, j * TOK : j * TOK + TOK, :] = back[side * TOK : side * TOK + TOK, HD * j : HD * j + HD]
 
-    @pl.loop(0, PARTS)
+    @pl.loop(0, PARTS, unroll=2)
     def _(i):
         g, side = lax.rem(i, HK), lax.div(i, HK)
         b = bo[i]
         dp = mm_t(b, vpol[i])
-        rd = dot_rows(b.astype(F32), o32[i])
-        bl = (prob[i] * (dp - rd) * scale).astype(BF)
+        rd = dot_rows(b.astype(F32), o32[i]) * scale
+        bl = (prob[i] * (dp * scale - rd)).astype(BF)
         dq = mm(bl, keys[i])
         term = mm(probb[i].T, b).astype(BF)
         r0 = pl.multiple_of(side * TOK, TOK)
@@ -193,12 +225,13 @@
             v0 = pl.multiple_of(side * TOK + blk * ROWS, TOK)
             vt[pl.ds(v0, TOK), pl.ds(pl.multiple_of(g * HD, HD), HD)] = term[blk * TOK : blk * TOK + TOK]
 
-    dn[...] = mm(vt[...], bvm[...]).astype(BF)
-    dq_low = mm(bq[...], bqm[...])
+    dn[...] = jnp.where(lane_of(ALL) < RANK, 0.0, mm(vt[...], bv[...])).astype(BF)
+    dq_low = jnp.where(lane_of(ROWS) < RANK, mm(bq[...], wn[:, 2 * RANK :]), 0.0)
     dn[pl.ds(own, ROWS), :] = (dn[pl.ds(own, ROWS), :].astype(F32) + dq_low).astype(BF)
     dn_t = dn[...].T
     low_t = low[...].T
     low_own_t = low[pl.ds(own, ROWS), :].T
+    lane16 = lane_of(16)
     left = lane16 < RANK
     for n in range(D // tile):
         cols = slice(n * tile, n * tile + tile)
@@ -215,36 +248,81 @@
     for d in range(32):
         out[6, d] = jnp.where(left, pltpu.roll(gv_t[16 * d : 16 * d + 16], RANK, 1), 0.0).astype(BF)
         out[7, d] = jnp.zeros((16, 2 * RANK), BF)
-    hi = margin.astype(BF).astype(F32)
-    mid = (margin - hi).astype(BF).astype(F32)
-    lo = margin - hi - mid
-    riding = jnp.where(lane16 == 0, hi, jnp.where(lane16 == 1, mid, jnp.where(lane16 == 2, lo, 0.0))).astype(BF)
+    riding = split3(margin)
     for q in range(8):
         out[q, 32] = riding
 
 
-def scale_kernel(got, scaled, margin_out):
-    ride = got[0, 32].astype(F32)
-    for q in range(1, 8):
-        ride = ride + got[q, 32].astype(F32)
-    margin = jnp.sum(ride[0:1, :], axis=-1, keepdims=True)
+def ride_of(block):
+    return jnp.sum(block[0:1, :], axis=-1, keepdims=True)
+
+
+def halves_kernel(h_ref, got, keep, send, margin_out):
+    h = h_ref[0]
+    ride = got[0, 0, 32].astype(F32)
+    kept, sent = got[0, h, 0:32].astype(F32), got[0, 1 - h, 0:32].astype(F32)
+    for q in range(1, 4):
+        ride = ride + got[q, 0, 32].astype(F32)
+        kept = kept + got[q, h, 0:32].astype(F32)
+        sent = sent + got[q, 1 - h, 0:32].astype(F32)
+    margin = ride_of(ride)
+    margin_out[...] = jnp.broadcast_to(margin, (8, 2 * RANK))
+    keep[...] = kept
+    send[0:32] = sent.astype(BF)
+    send[32] = split3(margin)
+
+
+def scale_kernel(keep, met, margin_in, scaled, margin_out):
+    margin = margin_in[0:1, 0:1] + ride_of(met[32].astype(F32))
     margin_out[...] = jnp.broadcast_to(margin, (8, 2 * RANK))
     weight = -BETA / (1.0 + jnp.exp(BETA * margin))
-    total = got[0, 0:32].astype(F32)
-    for q in range(1, 8):
-        total = total + got[q, 0:32].astype(F32)
-    scaled[...] = (total * weight[None]).astype(BF)
-
-
-def scale_step(got):
+    scaled[...] = ((keep[...] + met[0:32].astype(F32)) * weight[None]).astype(BF)
+
+
+def small_call(kernel, out_shape, args, scalars):
     vm = pl.BlockSpec(memory_space=pltpu.VMEM)
     return pl.pallas_call(
-        scale_kernel,
-        out_shape=(jax.ShapeDtypeStruct((32, 16, 2 * RANK), BF), jax.ShapeDtypeStruct((8, 2 * RANK), F32)),
-        in_specs=[vm],
-        out_specs=(vm, vm),
+        kernel,
+        out_shape=out_shape,
+        in_specs=[pl.BlockSpec(memory_space=pltpu.SMEM)] * scalars + [vm] * (len(args) - scalars),
+        out_specs=(vm,) * len(out_shape),
         compiler_params=pltpu.CompilerParams(vmem_limit_bytes=16 * 2**20),
-    )(got)
+    )(*args)
+
+
+def pack_kernel(h_ref, wq, wk, wv, wo, aq, av, bq, bv, out, narrow, sems):
+    narrow[:, 0:RANK] = aq[...]
+    narrow[:, RANK : 2 * RANK] = av[...]
+    narrow[:, 2 * RANK : 3 * RANK] = bq[...]
+    narrow[:, 3 * RANK : 4 * RANK] = jnp.zeros((TOK, RANK), BF)
+    narrow[0:16, 3 * RANK : 4 * RANK] = bv[...]
+
+    def move(parts):
+        copies = [pltpu.make_async_copy(src, out.at[:, lo:hi], sems.at[n]) for n, (src, lo, hi) in enumerate(parts)]
+        for copy in copies:
+            copy.start()
+        for copy in copies:
+            copy.wait()
+
+    @pl.when(h_ref[0] == 0)
+    def _():
+        move([(wq, 256, 2304), (wo.at[:, 0:384], 2304, 2688), (narrow, 0, 256)])
+
+    @pl.when(h_ref[0] == 1)
+    def _():
+        move([(wk, 0, 512), (wv, 512, 1024), (wo.at[:, 384:2048], 1024, 2688)])
+
+
+def pack(*args):
+    vm, anyspace = pl.BlockSpec(memory_space=pltpu.VMEM), pl.BlockSpec(memory_space=pl.ANY)
+    return pl.pallas_call(
+        pack_kernel,
+        out_shape=jax.ShapeDtypeStruct((TOK, 2688), BF),
+        in_specs=[pl.BlockSpec(memory_space=pltpu.SMEM)] + [anyspace] * 4 + [vm] * 4,
+        out_specs=anyspace,
+        scratch_shapes=[pltpu.VMEM((TOK, 4 * RANK), BF), pltpu.SemaphoreType.DMA((3,))],
+        compiler_params=pltpu.CompilerParams(vmem_limit_bytes=16 * 2**20),
+    )(*args)
 
 
 def local_step(own_block, full, xa, kc, ks, bias, hid, ans, gain, sign):
@@ -257,11 +335,11 @@
         out_specs=vm,
         scratch_shapes=[
             bf(D, 256), bf(D, 2 * KVW), bf(D, D), bf(D, D),
-            bf(ALL, 2 * RANK), bf(D, 2 * RANK), bf(KVW, 2 * RANK),
+            bf(ALL, 2 * RANK), bf(KVW, 2 * RANK),
             bf(PARTS, L, HD), bf(PARTS, L, HD), bf(PARTS, L, HD),
             bf(2, PARTS, QROWS, HD), f32(PARTS, QROWS, L), bf(PARTS, QROWS, L), f32(PARTS, QROWS, HD),
             bf(2 * ROWS, D), f32(ROWS, D), bf(ROWS, D), bf(PARTS, QROWS, HD), bf(ROWS, D), bf(ALL, KVW), bf(ALL, 2 * RANK),
-            pltpu.SemaphoreType.DMA((5,)),
+            pltpu.SemaphoreType.DMA((5, PIECES)),
         ],
         compiler_params=pltpu.CompilerParams(vmem_limit_bytes=50 * 2**20),
         cost_estimate=pl.CostEstimate(flops=24_000_000_000, bytes_accessed=27_000_000, transcendentals=2_100_000),
@@ -272,11 +350,9 @@
     hidden = hidden[0]
     y_pos, h_pos = lax.axis_index("y"), lax.axis_index("h")
 
-    narrow_v = jnp.concatenate([b_value, jnp.zeros((TOK - b_value.shape[0], RANK), BF)], axis=0)
-    half0 = jnp.concatenate([a_query, a_value, b_query, narrow_v, w_query, w_out[:, :384]], axis=1)
-    half1 = jnp.concatenate([w_key, w_value, w_out[:, 384:]], axis=1)
-    packed = jnp.where(h_pos == 0, half0, half1)
-    full = lax.all_gather(packed, ("h",) + OWN, axis=0, tiled=True).reshape(2, D, half0.shape[1])
+    h_one = jnp.full((1,), 1, jnp.int32) * h_pos
+    packed = pack(h_one, w_query, w_key, w_value, w_out, a_query, a_value, b_query, b_value)
+    full = lax.all_gather(packed, ("h",) + OWN, axis=0, tiled=True).reshape(2, D, packed.shape[1])
 
     x32 = hidden.astype(F32)
     xn = (x32 * lax.rsqrt(jnp.mean(x32 * x32, axis=-1, keepdims=True) + EPS) * attn_gain).astype(BF).reshape(ROWS, D)
@@ -303,7 +379,13 @@
     mine = local_step(own_block, full, xa, kc, ks, bias, hidden.reshape(ROWS, D), answer_rows.reshape(ROWS, D), final_gain.reshape(1, D), sign)
 
     seq = ("y", "h")
-    scaled, margin = scale_step(lax.all_to_all(mine, seq, 0, 0, tiled=True))
+    got = lax.all_to_all(mine.reshape(4, 2, 33, 16, 2 * RANK), "y", 0, 0, tiled=True)
+    quarter, vector = (16, 2 * RANK), jax.ShapeDtypeStruct((8, 2 * RANK), F32)
+    keep, send, part = small_call(
+        halves_kernel, (jax.ShapeDtypeStruct((32,) + quarter, F32), jax.ShapeDtypeStruct((33,) + quarter, BF), vector), (h_one, got), 1
+    )
+    met = lax.ppermute(send, "h", [(0, 1), (1, 0)])
+    scaled, margin = small_call(scale_kernel, (jax.ShapeDtypeStruct((32,) + quarter, BF), vector), (keep, met, part), 0)
     shares = lax.all_to_all(scaled, OWN, 0, 0, tiled=True)
     loss = jax.nn.softplus(-BETA * margin[0, :1])
     piece = jnp.sum(shares.astype(F32), axis=0)

time: 242 us -> 237 us (0.979)
  blocking collectives: 51.1 us -> 37.3 us
  waiting for transfers between devices: 112 us -> 117 us
  local copies, waits for them, and re-layouts: 9.38 us -> 12.2 us
  starting transfers between devices: 16.2 us -> 19 us
  Pallas kernels: 32 us -> 29.3 us
    all_to_all x1, blocking collectives: 28 us -> 18.8 us  [body(): lax.all_to_all(mine.reshape(4, 2, 33, 16, 2 * RANK), 'y', 0, 0, tiled=True)]
    unnamed x12 -> x26, local copies, waits for them, and re-layouts: 0.03 us -> 6.48 us
    ppermute x0 -> x1, waiting for transfers between devices: none -> 5.17 us  [body(): met = lax.ppermute(send, 'h', [(0, 1), (1, 0)])]
    all_to_all x1, blocking collectives: 23.1 us -> 18.5 us  [body(): shares = lax.all_to_all(scaled, OWN, 0, 0, tiled=True)]
    pallas_call x1, Pallas kernels: 31.8 us -> 28.2 us  [local_step(): pl.pallas_call(local_kernel, out_shape=jax.ShapeDtypeStruct((8, 33, 16, 2...]
    ppermute x0 -> x1, starting transfers between devices: none -> 2.74 us  [body(): met = lax.ppermute(send, 'h', [(0, 1), (1, 0)])]
  transfers between devices with their start and end apart: 4 -> 5, of which waited for: 4 -> 5; matrix products, arithmetic and copies ran while one was open for 3% -> 4% of each run, Pallas kernels for 0% -> 0%
where the time goes in v2:
time: 237 us; the launch traced here: 236 us
  waiting for transfers between devices  117 us (49%)
  blocking collectives  37.3 us (16%)
  Pallas kernels  29.3 us (12%)
  starting transfers between devices  19 us (8%)
  between operations  16.1 us (7%)
  local copies, waits for them, and re-layouts  12.2 us (5%)
  other arithmetic  5.31 us (2%)
    all_gather x1, waiting for transfers between devices, body(): lax.all_gather(packed, ('h',) + OWN, axis=0, tiled=True)  47.5 us
    all_to_all x1, waiting for transfers between devices, body(): lax.all_to_all(jnp.broadcast_to(two[None], (4,) + two.shape), 'y', 0, 0,...  40.9 us
    pallas_call x1, Pallas kernels, local_step(): pl.pallas_call(local_kernel, out_shape=jax.ShapeDtypeStruct((8, 33, 16, 2...  28.2 us
    all_to_all x1, blocking collectives, body(): lax.all_to_all(mine.reshape(4, 2, 33, 16, 2 * RANK), 'y', 0, 0, tiled=True)  18.8 us
    all_to_all x1, blocking collectives, body(): shares = lax.all_to_all(scaled, OWN, 0, 0, tiled=True)  18.5 us
    ppermute x1, waiting for transfers between devices, body(): other = lax.ppermute(xn, 'h', [(0, 1), (1, 0)])  15.3 us
    ppermute x1, starting transfers between devices, body(): other = lax.ppermute(xn, 'h', [(0, 1), (1, 0)])  7.9 us
    all_to_all x1, waiting for transfers between devices, body(): lax.all_to_all(jnp.broadcast_to(piece[None], (8,) + piece.shape), seq, 0,...  7.77 us
  transfers between devices with their start and end apart: 5, of which 5 were waited for; matrix products, arithmetic and copies ran while one was open for 4% of the time, Pallas kernels for 0%

profile of v2, /device:TPU:1, one launch (start us, length us, event | category | flops | bytes accessed | tf_op | source)
XLA Modules:
  0.0 235.9 jit_solution(12375639354085707411)
XLA Ops:
  7.2 0.0 copy-start
  7.2 0.0 all-gather.2.cloned.1.call-start
  7.2 0.0 copy-start.1
  7.2 1.0 copy-done.1
  8.2 0.0 copy-start.2
  8.2 0.9 copy-done.2
  9.2 0.0 copy-start.3
  9.2 0.8 copy-done.3
  10.0 0.0 copy-start.4
  10.0 0.8 copy-done.4
  10.9 0.0 copy-start.5
  10.9 0.7 copy-done.5
  11.6 0.0 copy-start.6
  11.6 0.7 copy-done.6
  12.3 0.0 copy-start.7
  12.3 0.7 copy-done.7
  13.0 0.0 copy-start.8
  13.0 0.7 copy-done.8
  13.7 0.8 shard_map.173
  14.5 0.0 all-gather.2.cloned.1.call-update
  14.5 1.2 multiply_reduce_fusion
  15.7 0.1 rsqrt.12
  15.8 0.0 copy-done
  15.8 0.9 multiply_convert_fusion
  16.7 7.9 %collective-permute-start = (bf16[128,2048]{1,0:T(8,128)(2,1)S(1)}, bf16[128,2048]{1,0:T(8,128)(2,1)S(1)}, u32[]{:S(2)}, u32[]{:S(2)}) collective-permute-start(bf16[128,2048]{1,0:T(8,128)(2,1)S(1)} %multiply_convert_fusion), channel_id=1, source_target_pairs={{0,4},{4,0},{1,5},{5,1},{2,6},{6,2},{3,7},{7,3},{8,12},{12,8},{9,1... | collective-permute-start | bytes 1572872 | tf_op jit(solution)/shard_map/ppermute | solution.py:359
  24.6 15.3 %collective-permute-done = bf16[128,2048]{1,0:T(8,128)(2,1)S(1)} collective-permute-done((bf16[128,2048]{1,0:T(8,128)(2,1)S(1)}, bf16[128,2048]{1,0:T(8,128)(2,1)S(1)}, u32[]{:S(2)}, u32[]{:S(2)}) %collective-permute-start) | collective-permute-done | bytes 524320 | tf_op jit(solution)/shard_map/ppermute | solution.py:359
  39.9 0.1 pad_maximum_fusion
  40.0 2.6 %broadcast_in_dim.12 = bf16[4,256,2048]{2,1,0:T(8,128)(2,1)} broadcast(bf16[256,2048]{1,0:T(8,128)(2,1)S(1)} %pad_maximum_fusion), dimensions={1,2} | broadcast | bytes 5242880 | tf_op jit(solution)/shard_map/broadcast_in_dim | solution.py:361
  42.7 0.0 copy-start.11
  42.7 0.0 copy-start.12
  42.7 5.0 %all-to-all-start = ((bf16[4,256,2048]{2,1,0:T(8,128)(2,1)}), bf16[4,256,2048]{2,1,0:T(8,128)(2,1)}, u32[]{:S(2)}, u32[]{:S(2)}) async-start(bf16[4,256,2048]{2,1,0:T(8,128)(2,1)} %broadcast_in_dim.12), calls=%async_computation | async-start | bytes 8388608 | tf_op jit(solution)/shard_map/all_to_all | solution.py:361
  47.7 0.1 iota_add_fusion
  47.7 0.1 convert_element_type.42
  47.8 0.1 add.85
  47.9 0.0 copy-done.11
  47.9 0.1 convert_element_type.44
  48.0 0.0 copy-done.12
  48.0 0.1 mul.105
  48.1 0.1 mul.106
  48.2 0.1 copy.24.sign
  48.3 0.0 copy-start.9
  48.3 0.0 copy-start.10
  48.3 1.9 fusion
  50.2 0.3 pad_maximum_fusion.1
  50.6 0.1 compare_select_fusion.bias
  50.7 40.9 %all-to-all-done = bf16[4,256,2048]{2,1,0:T(8,128)(2,1)} async-done(((bf16[4,256,2048]{2,1,0:T(8,128)(2,1)}), bf16[4,256,2048]{2,1,0:T(8,128)(2,1)}, u32[]{:S(2)}, u32[]{:S(2)}) %all-to-all-start) | async-done | bytes 4194336 | tf_op jit(solution)/shard_map/all_to_all | solution.py:361
  91.6 47.5 %all-gather.2.cloned.1.call-done = bf16[4096,2688]{1,0:T(8,128)(2,1)} async-done(((bf16[64,2688]{1,0:T(8,128)(2,1)}), bf16[4096,2688]{1,0:T(8,128)(2,1)}) %all-gather.2.cloned.1.call-update) | async-done | bytes 22020112 | tf_op jit(solution)/shard_map/all_gather | solution.py:355
  139.1 0.0 copy-done.9
  139.1 0.0 copy-done.10
  139.1 28.2 %shard_map.174 = bf16[8,33,16,128]{3,2,1,0:T(8,128)(2,1)S(1)} custom-call(s32[1]{0:T(128)} %bitcast.1.own_ref, bf16[2,2048,2688]{2,1,0:T(8,128)(2,1)} %bitcast.26, bf16[1024,2048]{1,0:T(8,128)(2,1)} %bitcast.4.xa, f32[1024,128]{1,0:T(8,128)S(1)} %get-tuple-element.24.kc, f32[1024,128]{1,0:T(8,128)S(1)} %get-tuple-element.25.ks, ...), custom_call_target="tpu_custom_call" | custom-call | flops 24000000000 | bytes 27000000 | tf_op jit(solution)/shard_map/pallas_call | solution.py:331
  167.2 18.8 %all_to_all.20.got = bf16[4,2,33,16,128]{4,3,2,1,0:T(8,128)(2,1)S(1)} all-to-all(bf16[4,2,33,16,128]{4,3,2,1,0:T(8,128)(2,1)S(1)} %bitcast.21), channel_id=1, replica_groups=mesh['z'=4,'c'=2,'y'=4,'h'=2,'x'=4] {'y'}, dimensions={0} | all-to-all | bytes 2162688 | tf_op jit(solution)/shard_map/all_to_all | solution.py:382
  186.0 0.2 shard_map.175
  186.3 2.7 %collective-permute-start.1 = (bf16[33,16,128]{2,1,0:T(8,128)(2,1)S(1)}, bf16[33,16,128]{2,1,0:T(8,128)(2,1)S(1)}, u32[]{:S(2)}, u32[]{:S(2)}) collective-permute-start(bf16[33,16,128]{2,1,0:T(8,128)(2,1)S(1)} %get-tuple-element.11), channel_id=1, source_target_pairs={{0,4},{4,0},{1,5},{5,1},{2,6},{6,2},{3,7},{7,3},{8,12},{12,8},{9,1... | collective-permute-start | bytes 405512 | tf_op jit(solution)/shard_map/ppermute | solution.py:387
  189.0 5.2 %collective-permute-done.1.met = bf16[33,16,128]{2,1,0:T(8,128)(2,1)S(1)} collective-permute-done((bf16[33,16,128]{2,1,0:T(8,128)(2,1)S(1)}, bf16[33,16,128]{2,1,0:T(8,128)(2,1)S(1)}, u32[]{:S(2)}, u32[]{:S(2)}) %collective-permute-start.1) | collective-permute-done | bytes 135200 | tf_op jit(solution)/shard_map/ppermute | solution.py:387
  194.2 0.1 shard_map.176
  194.3 18.5 %all_to_all.21 = bf16[32,16,128]{2,1,0:T(8,128)(2,1)S(1)} all-to-all(bf16[32,16,128]{2,1,0:T(8,128)(2,1)S(1)} %get-tuple-element.13), channel_id=1, replica_groups=mesh['z'=4,'c'=2,'y'=4,'h'=2,'x'=4] {'z','c','x'}, dimensions={0} | all-to-all | bytes 262144 | tf_op jit(solution)/shard_map/all_to_all | solution.py:389
  212.9 0.6 broadcast_in_dim.16
  213.5 3.3 %all-to-all-start.3 = ((f32[8,16,128]{2,1,0:T(8,128)}), f32[8,16,128]{2,1,0:T(8,128)S(1)}, u32[]{:S(2)}, u32[]{:S(2)}) async-start(f32[8,16,128]{2,1,0:T(8,128)} %broadcast_in_dim.16), calls=%async_computation.3 | async-start | bytes 131072 | tf_op jit(solution)/shard_map/all_to_all | solution.py:392
  216.9 0.5 slice.27
  218.1 7.8 %all-to-all-done.3 = f32[8,16,128]{2,1,0:T(8,128)S(1)} async-done(((f32[8,16,128]{2,1,0:T(8,128)}), f32[8,16,128]{2,1,0:T(8,128)S(1)}, u32[]{:S(2)}, u32[]{:S(2)}) %all-to-all-start.3) | async-done | bytes 65568 | tf_op jit(solution)/shard_map/all_to_all | solution.py:392
  225.9 0.7 fusion.6
  226.6 0.1 slice_bitcast_fusion.1
  226.7 0.6 pad_maximum_fusion.3
  227.3 0.6 slice_bitcast_fusion.2
  (9 shorter events, 0.1 us)
Async XLA Ops:
  7.2 8.7 %copy-start = (bf16[1,2,64,2048]{3,2,1,0:T(8,128)(2,1)S(1)}, bf16[1,2,64,2048]{3,2,1,0:T(8,128)(2,1)}, u32[]{:S(2)}) copy-start(bf16[1,2,64,2048]{3,2,1,0:T(8,128)(2,1)} %param.14) | copy-start | bytes 1572868
  7.2 131.9 %all-gather.2.cloned.1.call-start = ((), (), s32[]{:S(2)}) async-start(), calls=%async_computation.4 | async-start | bytes 22364160 | tf_op jit(solution)/shard_map/all_gather | solution.py:355
  7.2 1.0 copy-start.1
  8.2 0.9 copy-start.2
  9.2 0.8 copy-start.3
  10.0 0.8 copy-start.4
  10.9 0.7 copy-start.5
  11.6 0.7 copy-start.6
  12.3 0.7 copy-start.7
  13.0 0.7 copy-start.8
  16.7 23.2 %collective-permute-start = (bf16[128,2048]{1,0:T(8,128)(2,1)S(1)}, bf16[128,2048]{1,0:T(8,128)(2,1)S(1)}, u32[]{:S(2)}, u32[]{:S(2)}) collective-permute-start(bf16[128,2048]{1,0:T(8,128)(2,1)S(1)} %multiply_convert_fusion), channel_id=1, source_target_pairs={{0,4},{4,0},{1,5},{5,1},{2,6},{6,2},{3,7},{7,3},{8,12},{12,8},{9,1... | collective-permute-start | bytes 1572872 | tf_op jit(solution)/shard_map/ppermute | solution.py:359
  42.7 5.3 %copy-start.11 = (s32[1,2,64]{2,1,0:T(2,128)S(1)}, s32[1,2,64]{2,1,0:T(2,128)}, u32[]{:S(2)}) copy-start(s32[1,2,64]{2,1,0:T(2,128)} %param.16) | copy-start | bytes 1540
  42.7 5.3 %copy-start.12 = (f32[2]{0:T(128)S(1)}, f32[2]{0:T(128)}, u32[]{:S(2)}) copy-start(f32[2]{0:T(128)} %constant.69.clone) | copy-start | bytes 28
  42.7 48.9 %all-to-all-start = ((bf16[4,256,2048]{2,1,0:T(8,128)(2,1)}), bf16[4,256,2048]{2,1,0:T(8,128)(2,1)}, u32[]{:S(2)}, u32[]{:S(2)}) async-start(bf16[4,256,2048]{2,1,0:T(8,128)(2,1)} %broadcast_in_dim.12), calls=%async_computation | async-start | bytes 8388608 | tf_op jit(solution)/shard_map/all_to_all | solution.py:361
  48.3 90.8 %copy-start.9 = (bf16[1,2,64,2048]{3,2,1,0:T(8,128)(2,1)S(1)}, bf16[1,2,64,2048]{3,2,1,0:T(8,128)(2,1)}, u32[]{:S(2)}) copy-start(bf16[1,2,64,2048]{3,2,1,0:T(8,128)(2,1)} %param.15) | copy-start | bytes 1572868
  48.3 90.7 %copy-start.10 = (f32[2048]{0:T(1024)S(1)}, f32[2048]{0:T(1024)}, u32[]{:S(2)}) copy-start(f32[2048]{0:T(1024)} %param.18) | copy-start | bytes 24580
  186.3 7.9 %collective-permute-start.1 = (bf16[33,16,128]{2,1,0:T(8,128)(2,1)S(1)}, bf16[33,16,128]{2,1,0:T(8,128)(2,1)S(1)}, u32[]{:S(2)}, u32[]{:S(2)}) collective-permute-start(bf16[33,16,128]{2,1,0:T(8,128)(2,1)S(1)} %get-tuple-element.11), channel_id=1, source_target_pairs={{0,4},{4,0},{1,5},{5,1},{2,6},{6,2},{3,7},{7,3},{8,12},{12,8},{9,1... | collective-permute-start | bytes 405512 | tf_op jit(solution)/shard_map/ppermute | solution.py:387
  213.5 12.4 %all-to-all-start.3 = ((f32[8,16,128]{2,1,0:T(8,128)}), f32[8,16,128]{2,1,0:T(8,128)S(1)}, u32[]{:S(2)}, u32[]{:S(2)}) async-start(f32[8,16,128]{2,1,0:T(8,128)} %broadcast_in_dim.16), calls=%async_computation.3 | async-start | bytes 131072 | tf_op jit(solution)/shard_map/all_to_all | solution.py:392
Sparse Core Ops, SparseCore 0:
  14.6 124.3 all-gather.1

commit v3 on v2

--- a/solution.py
+++ b/solution.py
@@ -151,7 +151,7 @@
         raised = jnp.exp2(logits - jnp.max(logits, axis=-1, keepdims=True))
         return raised * (1.0 / jnp.sum(raised, axis=-1, keepdims=True))
 
-    @pl.loop(0, PARTS, unroll=2)
+    @pl.loop(0, PARTS, unroll=4)
     def _(i):
         g, side = lax.rem(i, HK), lax.div(i, HK)
         k = keys[i]
@@ -206,7 +206,7 @@
             for side in range(2):
                 bo[side * HK + g, j * TOK : j * TOK + TOK, :] = back[side * TOK : side * TOK + TOK, HD * j : HD * j + HD]
 
-    @pl.loop(0, PARTS, unroll=2)
+    @pl.loop(0, PARTS, unroll=4)
     def _(i):
         g, side = lax.rem(i, HK), lax.div(i, HK)
         b = bo[i]
@@ -257,71 +257,95 @@
     return jnp.sum(block[0:1, :], axis=-1, keepdims=True)
 
 
-def halves_kernel(h_ref, got, keep, send, margin_out):
-    h = h_ref[0]
-    ride = got[0, 0, 32].astype(F32)
-    kept, sent = got[0, h, 0:32].astype(F32), got[0, 1 - h, 0:32].astype(F32)
+def quarter_kernel(got, send):
+    total = got[0].astype(F32)
     for q in range(1, 4):
-        ride = ride + got[q, 0, 32].astype(F32)
-        kept = kept + got[q, h, 0:32].astype(F32)
-        sent = sent + got[q, 1 - h, 0:32].astype(F32)
-    margin = ride_of(ride)
-    margin_out[...] = jnp.broadcast_to(margin, (8, 2 * RANK))
-    keep[...] = kept
-    send[0:32] = sent.astype(BF)
-    send[32] = split3(margin)
-
-
-def scale_kernel(keep, met, margin_in, scaled, margin_out):
-    margin = margin_in[0:1, 0:1] + ride_of(met[32].astype(F32))
+        total = total + got[q].astype(F32)
+    send[...] = total.astype(BF)
+    ride = split3(ride_of(total[0, 32]))
+    send[0, 32] = ride
+
+
+def scale_kernel(sent, met, scaled, margin_out):
+    margin = ride_of(sent[0, 32].astype(F32)) + ride_of(met[0, 32].astype(F32))
     margin_out[...] = jnp.broadcast_to(margin, (8, 2 * RANK))
     weight = -BETA / (1.0 + jnp.exp(BETA * margin))
-    scaled[...] = ((keep[...] + met[0:32].astype(F32)) * weight[None]).astype(BF)
-
-
-def small_call(kernel, out_shape, args, scalars):
+    for e in range(2):
+        scaled[:, e] = ((sent[e, 0:32].astype(F32) + met[e, 0:32].astype(F32)) * weight[None]).astype(BF)
+
+
+def sum_kernel(shares, spread):
+    total = shares[0].astype(F32)
+    for q in range(1, 32):
+        total = total + shares[q].astype(F32)
+    for q in range(4):
+        spread[q] = total
+
+
+def finish_kernel(total, a_q, b_q, a_v, b_v):
+    for e in range(4):
+        at = slice(16 * e, 16 * e + 16)
+        a_q[at, :] = total[e, :, 0:RANK]
+        a_v[at, :] = total[e, :, RANK : 2 * RANK]
+    for e in range(2):
+        b_q[32 * e : 32 * e + 16, :] = total[4 + e, :, 0:RANK]
+        b_q[32 * e + 16 : 32 * e + 32, :] = total[4 + e, :, RANK : 2 * RANK]
+    b_v[...] = total[6, :, 0:RANK]
+
+
+def small_call(kernel, out_shape, *args):
     vm = pl.BlockSpec(memory_space=pltpu.VMEM)
     return pl.pallas_call(
         kernel,
         out_shape=out_shape,
-        in_specs=[pl.BlockSpec(memory_space=pltpu.SMEM)] * scalars + [vm] * (len(args) - scalars),
+        in_specs=[vm] * len(args),
         out_specs=(vm,) * len(out_shape),
         compiler_params=pltpu.CompilerParams(vmem_limit_bytes=16 * 2**20),
     )(*args)
 
 
-def pack_kernel(h_ref, wq, wk, wv, wo, aq, av, bq, bv, out, narrow, sems):
-    narrow[:, 0:RANK] = aq[...]
-    narrow[:, RANK : 2 * RANK] = av[...]
-    narrow[:, 2 * RANK : 3 * RANK] = bq[...]
-    narrow[:, 3 * RANK : 4 * RANK] = jnp.zeros((TOK, RANK), BF)
-    narrow[0:16, 3 * RANK : 4 * RANK] = bv[...]
-
+def pack_kernel(h_ref, wq, wk, wv, wo, aq, av, bq, bv, out, thin, thin_v, narrow, sems, thin_sems):
     def move(parts):
-        copies = [pltpu.make_async_copy(src, out.at[:, lo:hi], sems.at[n]) for n, (src, lo, hi) in enumerate(parts)]
-        for copy in copies:
-            copy.start()
-        for copy in copies:
-            copy.wait()
+        return [pltpu.make_async_copy(src, out.at[:, lo:hi], sems.at[n]) for n, (src, lo, hi) in enumerate(parts)]
 
     @pl.when(h_ref[0] == 0)
     def _():
-        move([(wq, 256, 2304), (wo.at[:, 0:384], 2304, 2688), (narrow, 0, 256)])
+        small = [pltpu.make_async_copy(src, thin.at[n], thin_sems.at[n]) for n, src in enumerate((aq, av, bq))]
+        small.append(pltpu.make_async_copy(bv, thin_v, thin_sems.at[3]))
+        large = move([(wq, 256, 2304), (wo.at[:, 0:384], 2304, 2688), (narrow, 0, 256)])
+        for copy in small + large[:2]:
+            copy.start()
+        for copy in small:
+            copy.wait()
+        for n in range(3):
+            narrow[:, n * RANK : n * RANK + RANK] = thin[n]
+        narrow[:, 3 * RANK : 4 * RANK] = jnp.zeros((TOK, RANK), BF)
+        narrow[0:16, 3 * RANK : 4 * RANK] = thin_v[...]
+        large[2].start()
+        for copy in large:
+            copy.wait()
 
     @pl.when(h_ref[0] == 1)
     def _():
-        move([(wk, 0, 512), (wv, 512, 1024), (wo.at[:, 384:2048], 1024, 2688)])
+        large = move([(wk, 0, 512), (wv, 512, 1024), (wo.at[:, 384:2048], 1024, 2688)])
+        for copy in large:
+            copy.start()
+        for copy in large:
+            copy.wait()
 
 
 def pack(*args):
-    vm, anyspace = pl.BlockSpec(memory_space=pltpu.VMEM), pl.BlockSpec(memory_space=pl.ANY)
+    anyspace = pl.BlockSpec(memory_space=pl.ANY)
     return pl.pallas_call(
         pack_kernel,
         out_shape=jax.ShapeDtypeStruct((TOK, 2688), BF),
-        in_specs=[pl.BlockSpec(memory_space=pltpu.SMEM)] + [anyspace] * 4 + [vm] * 4,
+        in_specs=[pl.BlockSpec(memory_space=pltpu.SMEM)] + [anyspace] * 8,
         out_specs=anyspace,
-        scratch_shapes=[pltpu.VMEM((TOK, 4 * RANK), BF), pltpu.SemaphoreType.DMA((3,))],
-        compiler_params=pltpu.CompilerParams(vmem_limit_bytes=16 * 2**20),
+        scratch_shapes=[
+            pltpu.VMEM((3, TOK, RANK), BF), pltpu.VMEM((16, RANK), BF), pltpu.VMEM((TOK, 4 * RANK), BF),
+            pltpu.SemaphoreType.DMA((3,)), pltpu.SemaphoreType.DMA((4,)),
+        ],
+        compiler_params=pltpu.CompilerParams(vmem_limit_bytes=62 * 2**20),
     )(*args)
 
 
@@ -378,22 +402,18 @@
 
     mine = local_step(own_block, full, xa, kc, ks, bias, hidden.reshape(ROWS, D), answer_rows.reshape(ROWS, D), final_gain.reshape(1, D), sign)
 
-    seq = ("y", "h")
     got = lax.all_to_all(mine.reshape(4, 2, 33, 16, 2 * RANK), "y", 0, 0, tiled=True)
-    quarter, vector = (16, 2 * RANK), jax.ShapeDtypeStruct((8, 2 * RANK), F32)
-    keep, send, part = small_call(
-        halves_kernel, (jax.ShapeDtypeStruct((32,) + quarter, F32), jax.ShapeDtypeStruct((33,) + quarter, BF), vector), (h_one, got), 1
-    )
+    tile, vector = (16, 2 * RANK), jax.ShapeDtypeStruct((8, 2 * RANK), F32)
+    (send,) = small_call(quarter_kernel, (jax.ShapeDtypeStruct((2, 33) + tile, BF),), got)
     met = lax.ppermute(send, "h", [(0, 1), (1, 0)])
-    scaled, margin = small_call(scale_kernel, (jax.ShapeDtypeStruct((32,) + quarter, BF), vector), (keep, met, part), 0)
+    scaled, margin = small_call(scale_kernel, (jax.ShapeDtypeStruct((32, 2) + tile, BF), vector), send, met)
     shares = lax.all_to_all(scaled, OWN, 0, 0, tiled=True)
     loss = jax.nn.softplus(-BETA * margin[0, :1])
-    piece = jnp.sum(shares.astype(F32), axis=0)
-    total = lax.all_to_all(jnp.broadcast_to(piece[None], (8,) + piece.shape), seq, 0, 0, tiled=True)
-    grad_a = total[:4].reshape(TOK, 2 * RANK)
-    low_half, high_half = total[4:6, :, :RANK], total[4:6, :, RANK:]
-    grad_b_q = jnp.stack([low_half, high_half], axis=1).reshape(TOK, RANK)
-    return grad_a[:, :RANK], grad_b_q, grad_a[:, RANK:], total[6, :, :RANK], loss
+    (spread,) = small_call(sum_kernel, (jax.ShapeDtypeStruct((4, 2) + tile, F32),), shares)
+    total = lax.all_to_all(spread, "y", 0, 0, tiled=True).reshape((8,) + tile)
+    square = jax.ShapeDtypeStruct((TOK, RANK), F32)
+    grads = small_call(finish_kernel, (square, square, square, jax.ShapeDtypeStruct((16, RANK), F32)), total)
+    return tuple(grads) + (loss,)
 
 
 def solution(mesh):

time: 237 us -> 242 us (1.021)
  Pallas kernels: 29.3 us -> 39.8 us
  local copies, waits for them, and re-layouts: 12.2 us -> 3.78 us
  blocking collectives: 37.3 us -> 40.3 us
    pallas_call x1, Pallas kernels: 0.77 us -> 10.6 us  [pack(): pl.pallas_call(pack_kernel, out_shape=jax.ShapeDtypeStruct((TOK, 2688), B...]
    unnamed x26 -> x10, local copies, waits for them, and re-layouts: 6.48 us -> 0.03 us
    ppermute x1, waiting for transfers between devices: 5.17 us -> 10.3 us  [body(): met = lax.ppermute(send, 'h', [(0, 1), (1, 0)])]
    all_to_all x1, waiting for transfers between devices: 7.77 us -> 3.18 us  [body(): total = lax.all_to_all(spread, 'y', 0, 0, tiled=True).reshape((8,) + tile)]
    all_to_all x1, blocking collectives: 18.5 us -> 21.6 us  [body(): shares = lax.all_to_all(scaled, OWN, 0, 0, tiled=True)]
  transfers between devices with their start and end apart: 5 -> 5, of which waited for: 5 -> 5; matrix products, arithmetic and copies ran while one was open for 4% -> 3% of each run, Pallas kernels for 0% -> 0%
where the time goes in v3:
time: 242 us; the launch traced here: 241 us
  waiting for transfers between devices  117 us (48%)
  blocking collectives  40.3 us (17%)
  Pallas kernels  39.8 us (16%)
  starting transfers between devices  20 us (8%)
  between operations  16 us (7%)
  other arithmetic  4.65 us (2%)
  local copies, waits for them, and re-layouts  3.78 us (2%)
    all_gather x1, waiting for transfers between devices, body(): lax.all_gather(packed, ('h',) + OWN, axis=0, tiled=True)  47.1 us
    all_to_all x1, waiting for transfers between devices, body(): lax.all_to_all(jnp.broadcast_to(two[None], (4,) + two.shape), 'y', 0, 0,...  40.8 us
    pallas_call x1, Pallas kernels, local_step(): pl.pallas_call(local_kernel, out_shape=jax.ShapeDtypeStruct((8, 33, 16, 2...  27.4 us
    all_to_all x1, blocking collectives, body(): shares = lax.all_to_all(scaled, OWN, 0, 0, tiled=True)  21.6 us
    all_to_all x1, blocking collectives, body(): lax.all_to_all(mine.reshape(4, 2, 33, 16, 2 * RANK), 'y', 0, 0, tiled=True)  18.7 us
    ppermute x1, waiting for transfers between devices, body(): other = lax.ppermute(xn, 'h', [(0, 1), (1, 0)])  15.3 us
    pallas_call x1, Pallas kernels, pack(): pl.pallas_call(pack_kernel, out_shape=jax.ShapeDtypeStruct((TOK, 2688), B...  10.6 us
    ppermute x1, waiting for transfers between devices, body(): met = lax.ppermute(send, 'h', [(0, 1), (1, 0)])  10.3 us
  transfers between devices with their start and end apart: 5, of which 5 were waited for; matrix products, arithmetic and copies ran while one was open for 3% of the time, Pallas kernels for 0%

profile of v3, /device:TPU:1, one launch (start us, length us, event | category | flops | bytes accessed | tf_op | source)
XLA Modules:
  0.0 241.4 jit_solution(9598662539640017059)
XLA Ops:
  7.2 0.0 copy-start
  7.2 0.0 all-gather.2.cloned.1.call-start
  7.2 10.6 %shard_map.173 = bf16[64,2688]{1,0:T(8,128)(2,1)} custom-call(s32[1]{0:T(128)} %bitcast.1.h_ref, bf16[64,2048]{1,0:T(8,128)(2,1)} %wq.1, bf16[64,512]{1,0:T(8,128)(2,1)} %wk.1, bf16[64,512]{1,0:T(8,128)(2,1)} %wv.1, bf16[64,2048]{1,0:T(8,128)(2,1)} %wo.1, bf16[64,64]{1,0:T(8,128)(2,1)} %aq.1, bf16[64,64]{1,0:T(8,128)(2,1)} %av.1, bf16[64,64]{1,0:T(8,128)(2,1)} %bq.1, ...), custom_call_target="tpu_custom_call" | custom-call | tf_op jit(solution)/shard_map/pallas_call | solution.py:339
  17.8 0.0 all-gather.2.cloned.1.call-update
  17.9 1.2 multiply_reduce_fusion
  19.1 0.1 rsqrt.12
  19.2 0.0 copy-done
  19.2 0.9 multiply_convert_fusion
  20.1 8.8 %collective-permute-start = (bf16[128,2048]{1,0:T(8,128)(2,1)S(1)}, bf16[128,2048]{1,0:T(8,128)(2,1)S(1)}, u32[]{:S(2)}, u32[]{:S(2)}) collective-permute-start(bf16[128,2048]{1,0:T(8,128)(2,1)S(1)} %multiply_convert_fusion), channel_id=1, source_target_pairs={{0,4},{4,0},{1,5},{5,1},{2,6},{6,2},{3,7},{7,3},{8,12},{12,8},{9,1... | collective-permute-start | bytes 1572872 | tf_op jit(solution)/shard_map/ppermute | solution.py:383
  28.9 15.3 %collective-permute-done = bf16[128,2048]{1,0:T(8,128)(2,1)S(1)} collective-permute-done((bf16[128,2048]{1,0:T(8,128)(2,1)S(1)}, bf16[128,2048]{1,0:T(8,128)(2,1)S(1)}, u32[]{:S(2)}, u32[]{:S(2)}) %collective-permute-start) | collective-permute-done | bytes 524320 | tf_op jit(solution)/shard_map/ppermute | solution.py:383
  44.2 0.1 pad_maximum_fusion
  44.3 2.6 %broadcast_in_dim.10 = bf16[4,256,2048]{2,1,0:T(8,128)(2,1)} broadcast(bf16[256,2048]{1,0:T(8,128)(2,1)S(1)} %pad_maximum_fusion), dimensions={1,2} | broadcast | bytes 5242880 | tf_op jit(solution)/shard_map/broadcast_in_dim | solution.py:385
  46.9 0.0 copy-start.3
  46.9 0.0 copy-start.4
  46.9 5.0 %all-to-all-start = ((bf16[4,256,2048]{2,1,0:T(8,128)(2,1)}), bf16[4,256,2048]{2,1,0:T(8,128)(2,1)}, u32[]{:S(2)}, u32[]{:S(2)}) async-start(bf16[4,256,2048]{2,1,0:T(8,128)(2,1)} %broadcast_in_dim.10), calls=%async_computation | async-start | bytes 8388608 | tf_op jit(solution)/shard_map/all_to_all | solution.py:385
  52.0 0.1 iota_add_fusion
  52.0 0.1 convert_element_type.39
  52.1 0.1 add.85
  52.2 0.0 copy-done.3
  52.2 0.1 convert_element_type.41
  52.3 0.0 copy-done.4
  52.3 0.1 mul.105
  52.4 0.1 mul.106
  52.5 0.1 copy.21.sign
  52.6 0.0 copy-start.1
  52.6 0.0 copy-start.2
  52.6 1.9 fusion
  54.5 0.3 pad_maximum_fusion.1
  54.9 0.1 compare_select_fusion.bias
  55.0 40.8 %all-to-all-done = bf16[4,256,2048]{2,1,0:T(8,128)(2,1)} async-done(((bf16[4,256,2048]{2,1,0:T(8,128)(2,1)}), bf16[4,256,2048]{2,1,0:T(8,128)(2,1)}, u32[]{:S(2)}, u32[]{:S(2)}) %all-to-all-start) | async-done | bytes 4194336 | tf_op jit(solution)/shard_map/all_to_all | solution.py:385
  95.8 47.1 %all-gather.2.cloned.1.call-done = bf16[4096,2688]{1,0:T(8,128)(2,1)} async-done(((bf16[64,2688]{1,0:T(8,128)(2,1)}), bf16[4096,2688]{1,0:T(8,128)(2,1)}) %all-gather.2.cloned.1.call-update) | async-done | bytes 22020112 | tf_op jit(solution)/shard_map/all_gather | solution.py:379
  142.9 0.0 copy-done.1
  142.9 0.0 copy-done.2
  142.9 27.4 %shard_map.174 = bf16[8,33,16,128]{3,2,1,0:T(8,128)(2,1)S(1)} custom-call(s32[1]{0:T(128)} %bitcast.own_ref, bf16[2,2048,2688]{2,1,0:T(8,128)(2,1)} %bitcast.16, bf16[1024,2048]{1,0:T(8,128)(2,1)} %bitcast.4.xa, f32[1024,128]{1,0:T(8,128)S(1)} %get-tuple-element.22.kc, f32[1024,128]{1,0:T(8,128)S(1)} %get-tuple-element.23.ks, ...), custom_call_target="tpu_custom_call" | custom-call | flops 24000000000 | bytes 27000000 | tf_op jit(solution)/shard_map/pallas_call | solution.py:355
  170.3 18.7 %all_to_all.20.got = bf16[4,2,33,16,128]{4,3,2,1,0:T(8,128)(2,1)S(1)} all-to-all(bf16[4,2,33,16,128]{4,3,2,1,0:T(8,128)(2,1)S(1)} %bitcast.12), channel_id=1, replica_groups=mesh['z'=4,'c'=2,'y'=4,'h'=2,'x'=4] {'y'}, dimensions={0} | all-to-all | bytes 2162688 | tf_op jit(solution)/shard_map/all_to_all | solution.py:405
  189.0 0.3 shard_map.175.sent
  189.3 2.9 %collective-permute-start.1 = (bf16[2,33,16,128]{3,2,1,0:T(8,128)(2,1)S(1)}, bf16[2,33,16,128]{3,2,1,0:T(8,128)(2,1)S(1)}, u32[]{:S(2)}, u32[]{:S(2)}) collective-permute-start(bf16[2,33,16,128]{3,2,1,0:T(8,128)(2,1)S(1)} %shard_map.175.sent), channel_id=1, source_target_pairs={{0,4},{4,0},{1,5},{5,1},{2,6},{6,2},{3,7},{7,3},{8,12},{12,8},{9,1... | collective-permute-start | bytes 811016 | tf_op jit(solution)/shard_map/ppermute | solution.py:408
  192.2 10.3 %collective-permute-done.1.met = bf16[2,33,16,128]{3,2,1,0:T(8,128)(2,1)S(1)} collective-permute-done((bf16[2,33,16,128]{3,2,1,0:T(8,128)(2,1)S(1)}, bf16[2,33,16,128]{3,2,1,0:T(8,128)(2,1)S(1)}, u32[]{:S(2)}, u32[]{:S(2)}) %collective-permute-start.1) | collective-permute-done | bytes 270368 | tf_op jit(solution)/shard_map/ppermute | solution.py:408
  202.5 0.1 shard_map.176
  202.7 21.6 %all_to_all.21.shares = bf16[32,2,16,128]{3,2,1,0:T(8,128)(2,1)S(1)} all-to-all(bf16[32,2,16,128]{3,2,1,0:T(8,128)(2,1)S(1)} %get-tuple-element.11), channel_id=1, replica_groups=mesh['z'=4,'c'=2,'y'=4,'h'=2,'x'=4] {'z','c','x'}, dimensions={0} | all-to-all | bytes 524288 | tf_op jit(solution)/shard_map/all_to_all | solution.py:410
  224.3 0.7 shard_map.177
  225.0 3.3 %all-to-all-start.3 = ((f32[4,2,16,128]{3,2,1,0:T(8,128)}), f32[4,2,16,128]{3,2,1,0:T(8,128)S(1)}, u32[]{:S(2)}, u32[]{:S(2)}) async-start(f32[4,2,16,128]{3,2,1,0:T(8,128)} %shard_map.177), calls=%async_computation.3 | async-start | bytes 131072 | tf_op jit(solution)/shard_map/all_to_all | solution.py:413
  228.3 0.5 slice.3
  229.5 3.2 %all-to-all-done.3 = f32[4,2,16,128]{3,2,1,0:T(8,128)S(1)} async-done(((f32[4,2,16,128]{3,2,1,0:T(8,128)}), f32[4,2,16,128]{3,2,1,0:T(8,128)S(1)}, u32[]{:S(2)}, u32[]{:S(2)}) %all-to-all-start.3) | async-done | bytes 65568 | tf_op jit(solution)/shard_map/all_to_all | solution.py:413
  232.7 0.7 shard_map.178
  (7 shorter events, 0.0 us)
Async XLA Ops:
  7.2 12.0 %copy-start = (bf16[1,2,64,2048]{3,2,1,0:T(8,128)(2,1)S(1)}, bf16[1,2,64,2048]{3,2,1,0:T(8,128)(2,1)}, u32[]{:S(2)}) copy-start(bf16[1,2,64,2048]{3,2,1,0:T(8,128)(2,1)} %param.14) | copy-start | bytes 1572868
  7.2 135.7 %all-gather.2.cloned.1.call-start = ((), (), s32[]{:S(2)}) async-start(), calls=%async_computation.4 | async-start | bytes 22364160 | tf_op jit(solution)/shard_map/all_gather | solution.py:379
  20.1 24.1 %collective-permute-start = (bf16[128,2048]{1,0:T(8,128)(2,1)S(1)}, bf16[128,2048]{1,0:T(8,128)(2,1)S(1)}, u32[]{:S(2)}, u32[]{:S(2)}) collective-permute-start(bf16[128,2048]{1,0:T(8,128)(2,1)S(1)} %multiply_convert_fusion), channel_id=1, source_target_pairs={{0,4},{4,0},{1,5},{5,1},{2,6},{6,2},{3,7},{7,3},{8,12},{12,8},{9,1... | collective-permute-start | bytes 1572872 | tf_op jit(solution)/shard_map/ppermute | solution.py:383
  46.9 5.3 %copy-start.3 = (s32[1,2,64]{2,1,0:T(2,128)S(1)}, s32[1,2,64]{2,1,0:T(2,128)}, u32[]{:S(2)}) copy-start(s32[1,2,64]{2,1,0:T(2,128)} %param.16) | copy-start | bytes 1540
  46.9 5.4 %copy-start.4 = (f32[2]{0:T(128)S(1)}, f32[2]{0:T(128)}, u32[]{:S(2)}) copy-start(f32[2]{0:T(128)} %constant.69.clone) | copy-start | bytes 28
  46.9 48.9 %all-to-all-start = ((bf16[4,256,2048]{2,1,0:T(8,128)(2,1)}), bf16[4,256,2048]{2,1,0:T(8,128)(2,1)}, u32[]{:S(2)}, u32[]{:S(2)}) async-start(bf16[4,256,2048]{2,1,0:T(8,128)(2,1)} %broadcast_in_dim.10), calls=%async_computation | async-start | bytes 8388608 | tf_op jit(solution)/shard_map/all_to_all | solution.py:385
  52.6 90.3 %copy-start.1 = (bf16[1,2,64,2048]{3,2,1,0:T(8,128)(2,1)S(1)}, bf16[1,2,64,2048]{3,2,1,0:T(8,128)(2,1)}, u32[]{:S(2)}) copy-start(bf16[1,2,64,2048]{3,2,1,0:T(8,128)(2,1)} %param.15) | copy-start | bytes 1572868
  52.6 90.3 %copy-start.2 = (f32[2048]{0:T(1024)S(1)}, f32[2048]{0:T(1024)}, u32[]{:S(2)}) copy-start(f32[2048]{0:T(1024)} %param.18) | copy-start | bytes 24580
  189.3 13.2 %collective-permute-start.1 = (bf16[2,33,16,128]{3,2,1,0:T(8,128)(2,1)S(1)}, bf16[2,33,16,128]{3,2,1,0:T(8,128)(2,1)S(1)}, u32[]{:S(2)}, u32[]{:S(2)}) collective-permute-start(bf16[2,33,16,128]{3,2,1,0:T(8,128)(2,1)S(1)} %shard_map.175.sent), channel_id=1, source_target_pairs={{0,4},{4,0},{1,5},{5,1},{2,6},{6,2},{3,7},{7,3},{8,12},{12,8},{9,1... | collective-permute-start | bytes 811016 | tf_op jit(solution)/shard_map/ppermute | solution.py:408
  225.0 7.7 %all-to-all-start.3 = ((f32[4,2,16,128]{3,2,1,0:T(8,128)}), f32[4,2,16,128]{3,2,1,0:T(8,128)S(1)}, u32[]{:S(2)}, u32[]{:S(2)}) async-start(f32[4,2,16,128]{3,2,1,0:T(8,128)} %shard_map.177), calls=%async_computation.3 | async-start | bytes 131072 | tf_op jit(solution)/shard_map/all_to_all | solution.py:413
Sparse Core Ops, SparseCore 0:
  18.0 124.8 all-gather.1

commit v4 on v2

--- a/solution.py
+++ b/solution.py
@@ -151,7 +151,7 @@
         raised = jnp.exp2(logits - jnp.max(logits, axis=-1, keepdims=True))
         return raised * (1.0 / jnp.sum(raised, axis=-1, keepdims=True))
 
-    @pl.loop(0, PARTS, unroll=2)
+    @pl.loop(0, PARTS, unroll=4)
     def _(i):
         g, side = lax.rem(i, HK), lax.div(i, HK)
         k = keys[i]
@@ -206,7 +206,7 @@
             for side in range(2):
                 bo[side * HK + g, j * TOK : j * TOK + TOK, :] = back[side * TOK : side * TOK + TOK, HD * j : HD * j + HD]
 
-    @pl.loop(0, PARTS, unroll=2)
+    @pl.loop(0, PARTS, unroll=4)
     def _(i):
         g, side = lax.rem(i, HK), lax.div(i, HK)
         b = bo[i]
@@ -279,7 +279,26 @@
     scaled[...] = ((keep[...] + met[0:32].astype(F32)) * weight[None]).astype(BF)
 
 
-def small_call(kernel, out_shape, args, scalars):
+def sum_kernel(shares, spread):
+    total = shares[0].astype(F32)
+    for q in range(1, 32):
+        total = total + shares[q].astype(F32)
+    for q in range(8):
+        spread[q] = total
+
+
+def finish_kernel(total, a_q, b_q, a_v, b_v):
+    for e in range(4):
+        at = slice(16 * e, 16 * e + 16)
+        a_q[at, :] = total[e, :, 0:RANK]
+        a_v[at, :] = total[e, :, RANK : 2 * RANK]
+    for e in range(2):
+        b_q[32 * e : 32 * e + 16, :] = total[4 + e, :, 0:RANK]
+        b_q[32 * e + 16 : 32 * e + 32, :] = total[4 + e, :, RANK : 2 * RANK]
+    b_v[...] = total[6, :, 0:RANK]
+
+
+def small_call(kernel, out_shape, *args, scalars=0):
     vm = pl.BlockSpec(memory_space=pltpu.VMEM)
     return pl.pallas_call(
         kernel,
@@ -290,38 +309,54 @@
     )(*args)
 
 
-def pack_kernel(h_ref, wq, wk, wv, wo, aq, av, bq, bv, out, narrow, sems):
-    narrow[:, 0:RANK] = aq[...]
-    narrow[:, RANK : 2 * RANK] = av[...]
-    narrow[:, 2 * RANK : 3 * RANK] = bq[...]
-    narrow[:, 3 * RANK : 4 * RANK] = jnp.zeros((TOK, RANK), BF)
-    narrow[0:16, 3 * RANK : 4 * RANK] = bv[...]
-
-    def move(parts):
-        copies = [pltpu.make_async_copy(src, out.at[:, lo:hi], sems.at[n]) for n, (src, lo, hi) in enumerate(parts)]
+def pack_kernel(h_ref, wq, wk, wv, wo, aq, av, bq, bv, hidden, gain, out, xn, thin, thin_v, flat, hid, sems, out_sem):
+    hid_copy = pltpu.make_async_copy(hidden, hid, sems.at[6])
+    hid_copy.start()
+
+    def fetch(parts):
+        copies = [pltpu.make_async_copy(src, dst, sems.at[n]) for n, (src, dst) in enumerate(parts)]
         for copy in copies:
             copy.start()
-        for copy in copies:
-            copy.wait()
+        return copies
 
     @pl.when(h_ref[0] == 0)
     def _():
-        move([(wq, 256, 2304), (wo.at[:, 0:384], 2304, 2688), (narrow, 0, 256)])
+        small = [(aq, thin.at[0]), (av, thin.at[1]), (bq, thin.at[2]), (bv, thin_v)]
+        copies = fetch(small + [(wq, flat.at[:, 256:2304]), (wo.at[:, 0:384], flat.at[:, 2304:2688])])
+        for copy in copies[:4]:
+            copy.wait()
+        for n in range(3):
+            flat[:, n * RANK : n * RANK + RANK] = thin[n]
+        flat[:, 3 * RANK : 4 * RANK] = jnp.zeros((TOK, RANK), BF)
+        flat[0:16, 3 * RANK : 4 * RANK] = thin_v[...]
+        for copy in copies[4:]:
+            copy.wait()
 
     @pl.when(h_ref[0] == 1)
     def _():
-        move([(wk, 0, 512), (wv, 512, 1024), (wo.at[:, 384:2048], 1024, 2688)])
+        for copy in fetch([(wk, flat.at[:, 0:512]), (wv, flat.at[:, 512:1024]), (wo.at[:, 384:2048], flat.at[:, 1024:2688])]):
+            copy.wait()
+
+    done = pltpu.make_async_copy(flat, out, out_sem)
+    done.start()
+    hid_copy.wait()
+    x = hid[...].astype(F32)
+    xn[...] = (x * lax.rsqrt(jnp.mean(x * x, axis=-1, keepdims=True) + EPS) * gain[...]).astype(BF)
+    done.wait()
 
 
 def pack(*args):
     vm, anyspace = pl.BlockSpec(memory_space=pltpu.VMEM), pl.BlockSpec(memory_space=pl.ANY)
     return pl.pallas_call(
         pack_kernel,
-        out_shape=jax.ShapeDtypeStruct((TOK, 2688), BF),
-        in_specs=[pl.BlockSpec(memory_space=pltpu.SMEM)] + [anyspace] * 4 + [vm] * 4,
-        out_specs=anyspace,
-        scratch_shapes=[pltpu.VMEM((TOK, 4 * RANK), BF), pltpu.SemaphoreType.DMA((3,))],
-        compiler_params=pltpu.CompilerParams(vmem_limit_bytes=16 * 2**20),
+        out_shape=(jax.ShapeDtypeStruct((TOK, 2688), BF), jax.ShapeDtypeStruct((ROWS, D), BF)),
+        in_specs=[pl.BlockSpec(memory_space=pltpu.SMEM)] + [anyspace] * 9 + [vm],
+        out_specs=(anyspace, vm),
+        scratch_shapes=[
+            pltpu.VMEM((3, TOK, RANK), BF), pltpu.VMEM((16, RANK), BF), pltpu.VMEM((TOK, 2688), BF), pltpu.VMEM((ROWS, D), BF),
+            pltpu.SemaphoreType.DMA((7,)), pltpu.SemaphoreType.DMA,
+        ],
+        compiler_params=pltpu.CompilerParams(vmem_limit_bytes=60 * 2**20),
     )(*args)
 
 
@@ -351,12 +386,12 @@
     y_pos, h_pos = lax.axis_index("y"), lax.axis_index("h")
 
     h_one = jnp.full((1,), 1, jnp.int32) * h_pos
-    packed = pack(h_one, w_query, w_key, w_value, w_out, a_query, a_value, b_query, b_value)
+    packed, xn = pack(
+        h_one, w_query, w_key, w_value, w_out, a_query, a_value, b_query, b_value, hidden.reshape(ROWS, D), attn_gain.reshape(1, D)
+    )
+    other = lax.ppermute(xn, "h", [(0, 1), (1, 0)])
     full = lax.all_gather(packed, ("h",) + OWN, axis=0, tiled=True).reshape(2, D, packed.shape[1])
 
-    x32 = hidden.astype(F32)
-    xn = (x32 * lax.rsqrt(jnp.mean(x32 * x32, axis=-1, keepdims=True) + EPS) * attn_gain).astype(BF).reshape(ROWS, D)
-    other = lax.ppermute(xn, "h", [(0, 1), (1, 0)])
     two = jnp.concatenate([xn, other], axis=0)
     every = lax.all_to_all(jnp.broadcast_to(two[None], (4,) + two.shape), "y", 0, 0, tiled=True)
     xa = every.reshape(ALL, D)
@@ -378,22 +413,20 @@
 
     mine = local_step(own_block, full, xa, kc, ks, bias, hidden.reshape(ROWS, D), answer_rows.reshape(ROWS, D), final_gain.reshape(1, D), sign)
 
-    seq = ("y", "h")
     got = lax.all_to_all(mine.reshape(4, 2, 33, 16, 2 * RANK), "y", 0, 0, tiled=True)
-    quarter, vector = (16, 2 * RANK), jax.ShapeDtypeStruct((8, 2 * RANK), F32)
+    tile, vector = (16, 2 * RANK), jax.ShapeDtypeStruct((8, 2 * RANK), F32)
     keep, send, part = small_call(
-        halves_kernel, (jax.ShapeDtypeStruct((32,) + quarter, F32), jax.ShapeDtypeStruct((33,) + quarter, BF), vector), (h_one, got), 1
+        halves_kernel, (jax.ShapeDtypeStruct((32,) + tile, F32), jax.ShapeDtypeStruct((33,) + tile, BF), vector), h_one, got, scalars=1
     )
     met = lax.ppermute(send, "h", [(0, 1), (1, 0)])
-    scaled, margin = small_call(scale_kernel, (jax.ShapeDtypeStruct((32,) + quarter, BF), vector), (keep, met, part), 0)
+    scaled, margin = small_call(scale_kernel, (jax.ShapeDtypeStruct((32,) + tile, BF), vector), keep, met, part)
     shares = lax.all_to_all(scaled, OWN, 0, 0, tiled=True)
     loss = jax.nn.softplus(-BETA * margin[0, :1])
-    piece = jnp.sum(shares.astype(F32), axis=0)
-    total = lax.all_to_all(jnp.broadcast_to(piece[None], (8,) + piece.shape), seq, 0, 0, tiled=True)
-    grad_a = total[:4].reshape(TOK, 2 * RANK)
-    low_half, high_half = total[4:6, :, :RANK], total[4:6, :, RANK:]
-    grad_b_q = jnp.stack([low_half, high_half], axis=1).reshape(TOK, RANK)
-    return grad_a[:, :RANK], grad_b_q, grad_a[:, RANK:], total[6, :, :RANK], loss
+    (spread,) = small_call(sum_kernel, (jax.ShapeDtypeStruct((8,) + tile, F32),), shares)
+    total = lax.all_to_all(spread, ("y", "h"), 0, 0, tiled=True)
+    square = jax.ShapeDtypeStruct((TOK, RANK), F32)
+    grads = small_call(finish_kernel, (square, square, square, jax.ShapeDtypeStruct((16, RANK), F32)), total)
+    return tuple(grads) + (loss,)
 
 
 def solution(mesh):

time: 237 us -> 228 us (0.962)
  local copies, waits for them, and re-layouts: 12.2 us -> 3.7 us
  Pallas kernels: 29.3 us -> 32.6 us
    unnamed x26 -> x10, local copies, waits for them, and re-layouts: 6.48 us -> 0.03 us
    pallas_call x1, Pallas kernels: 0.77 us -> 3.49 us  [pack(): pl.pallas_call(pack_kernel, out_shape=(jax.ShapeDtypeStruct((TOK, 2688),...]
  transfers between devices with their start and end apart: 5 -> 5, of which waited for: 5 -> 5; matrix products, arithmetic and copies ran while one was open for 4% -> 3% of each run, Pallas kernels for 0% -> 0%
where the time goes in v4:
time: 228 us
  waiting for transfers between devices  116 us (51%)
  blocking collectives  37.3 us (16%)
  Pallas kernels  32.6 us (14%)
  starting transfers between devices  19.1 us (8%)
  between operations  16 us (7%)
  local copies, waits for them, and re-layouts  3.7 us (2%)
  other arithmetic  3.56 us (2%)
    all_gather x1, waiting for transfers between devices, body(): lax.all_gather(packed, ('h',) + OWN, axis=0, tiled=True)  46.9 us
    all_to_all x1, waiting for transfers between devices, body(): lax.all_to_all(jnp.broadcast_to(two[None], (4,) + two.shape), 'y', 0, 0,...  40.7 us
    pallas_call x1, Pallas kernels, local_step(): pl.pallas_call(local_kernel, out_shape=jax.ShapeDtypeStruct((8, 33, 16, 2...  27.4 us
    all_to_all x1, blocking collectives, body(): lax.all_to_all(mine.reshape(4, 2, 33, 16, 2 * RANK), 'y', 0, 0, tiled=True)  18.7 us
    all_to_all x1, blocking collectives, body(): shares = lax.all_to_all(scaled, OWN, 0, 0, tiled=True)  18.6 us
    ppermute x1, waiting for transfers between devices, body(): other = lax.ppermute(xn, 'h', [(0, 1), (1, 0)])  15.2 us
    ppermute x1, starting transfers between devices, body(): other = lax.ppermute(xn, 'h', [(0, 1), (1, 0)])  7.78 us
    all_to_all x1, waiting for transfers between devices, body(): total = lax.all_to_all(spread, ('y', 'h'), 0, 0, tiled=True)  7.77 us
  transfers between devices with their start and end apart: 5, of which 5 were waited for; matrix products, arithmetic and copies ran while one was open for 3% of the time, Pallas kernels for 0%

profile of v4, /device:TPU:1, one launch (start us, length us, event | category | flops | bytes accessed | tf_op | source)
XLA Modules:
  0.0 227.9 jit_solution(16336331550517375643)
XLA Ops:
  7.2 0.0 all-gather.2.cloned.1.call-start
  7.2 3.5 %shard_map.173 = (bf16[64,2688]{1,0:T(8,128)(2,1)}, bf16[128,2048]{1,0:T(8,128)(2,1)}) custom-call(s32[1]{0:T(128)} %bitcast.h_ref, bf16[64,2048]{1,0:T(8,128)(2,1)} %wq.1, bf16[64,512]{1,0:T(8,128)(2,1)} %wk.1, bf16[64,512]{1,0:T(8,128)(2,1)} %wv.1, bf16[64,2048]{1,0:T(8,128)(2,1)} %wo.1, bf16[64,64]{1,0:T(8,128)(2,1)} %aq.1, bf16[64,64]{1,0:T(8,128)(2,1)} %av.1, ...), custom_call_target="tpu_custom_call" | custom-call | tf_op jit(solution)/shard_map/pallas_call | solution.py:350
  10.7 0.0 all-gather.2.cloned.1.call-update
  10.7 7.8 %collective-permute-start = (bf16[128,2048]{1,0:T(8,128)(2,1)}, bf16[128,2048]{1,0:T(8,128)(2,1)S(1)}, u32[]{:S(2)}, u32[]{:S(2)}) collective-permute-start(bf16[128,2048]{1,0:T(8,128)(2,1)} %get-tuple-element.17), channel_id=1, source_target_pairs={{0,4},{4,0},{1,5},{5,1},{2,6},{6,2},{3,7},{7,3},{8,12},{12,8},{9,1... | collective-permute-start | bytes 1572872 | tf_op jit(solution)/shard_map/ppermute | solution.py:392
  18.5 15.2 %collective-permute-done = bf16[128,2048]{1,0:T(8,128)(2,1)S(1)} collective-permute-done((bf16[128,2048]{1,0:T(8,128)(2,1)}, bf16[128,2048]{1,0:T(8,128)(2,1)S(1)}, u32[]{:S(2)}, u32[]{:S(2)}) %collective-permute-start) | collective-permute-done | bytes 524320 | tf_op jit(solution)/shard_map/ppermute | solution.py:392
  33.8 1.1 pad_maximum_fusion
  34.9 2.6 %broadcast_in_dim.10 = bf16[4,256,2048]{2,1,0:T(8,128)(2,1)} broadcast(bf16[256,2048]{1,0:T(8,128)(2,1)S(1)} %pad_maximum_fusion), dimensions={1,2} | broadcast | bytes 5242880 | tf_op jit(solution)/shard_map/broadcast_in_dim | solution.py:396
  37.5 0.0 copy-start.3
  37.5 0.0 copy-start.4
  37.5 5.0 %all-to-all-start = ((bf16[4,256,2048]{2,1,0:T(8,128)(2,1)}), bf16[4,256,2048]{2,1,0:T(8,128)(2,1)}, u32[]{:S(2)}, u32[]{:S(2)}) async-start(bf16[4,256,2048]{2,1,0:T(8,128)(2,1)} %broadcast_in_dim.10), calls=%async_computation | async-start | bytes 8388608 | tf_op jit(solution)/shard_map/all_to_all | solution.py:396
  42.6 0.1 iota_add_fusion
  42.7 0.1 convert_element_type.25
  42.7 0.1 add.71
  42.8 0.0 copy-done.3
  42.8 0.1 convert_element_type.27
  42.9 0.0 copy-done.4
  42.9 0.1 mul.78
  43.0 0.1 mul.79
  43.1 0.1 copy.21.sign
  43.2 0.0 copy-start
  43.2 0.0 copy-start.1
  43.2 0.0 copy-start.2
  43.2 1.9 fusion
  45.1 0.3 pad_maximum_fusion.1
  45.5 0.1 compare_select_fusion.bias
  45.6 40.7 %all-to-all-done = bf16[4,256,2048]{2,1,0:T(8,128)(2,1)} async-done(((bf16[4,256,2048]{2,1,0:T(8,128)(2,1)}), bf16[4,256,2048]{2,1,0:T(8,128)(2,1)}, u32[]{:S(2)}, u32[]{:S(2)}) %all-to-all-start) | async-done | bytes 4194336 | tf_op jit(solution)/shard_map/all_to_all | solution.py:396
  86.3 46.9 %all-gather.2.cloned.1.call-done = bf16[4096,2688]{1,0:T(8,128)(2,1)} async-done(((bf16[64,2688]{1,0:T(8,128)(2,1)}), bf16[4096,2688]{1,0:T(8,128)(2,1)}) %all-gather.2.cloned.1.call-update) | async-done | bytes 22020112 | tf_op jit(solution)/shard_map/all_gather | solution.py:393
  133.2 0.0 copy-done
  133.2 0.0 copy-done.1
  133.2 0.0 copy-done.2
  133.2 27.4 %shard_map.174 = bf16[8,33,16,128]{3,2,1,0:T(8,128)(2,1)S(1)} custom-call(s32[1]{0:T(128)} %bitcast.1.own_ref, bf16[2,2048,2688]{2,1,0:T(8,128)(2,1)} %bitcast.16, bf16[1024,2048]{1,0:T(8,128)(2,1)} %bitcast.5.xa, f32[1024,128]{1,0:T(8,128)S(1)} %get-tuple-element.32.kc, f32[1024,128]{1,0:T(8,128)S(1)} %get-tuple-element.33.ks, ...), custom_call_target="tpu_custom_call" | custom-call | flops 24000000000 | bytes 27000000 | tf_op jit(solution)/shard_map/pallas_call | solution.py:366
  160.6 18.7 %all_to_all.20.got = bf16[4,2,33,16,128]{4,3,2,1,0:T(8,128)(2,1)S(1)} all-to-all(bf16[4,2,33,16,128]{4,3,2,1,0:T(8,128)(2,1)S(1)} %bitcast.10), channel_id=1, replica_groups=mesh['z'=4,'c'=2,'y'=4,'h'=2,'x'=4] {'y'}, dimensions={0} | all-to-all | bytes 2162688 | tf_op jit(solution)/shard_map/all_to_all | solution.py:416
  179.3 0.2 shard_map.175
  179.5 2.9 %collective-permute-start.1 = (bf16[33,16,128]{2,1,0:T(8,128)(2,1)S(1)}, bf16[33,16,128]{2,1,0:T(8,128)(2,1)S(1)}, u32[]{:S(2)}, u32[]{:S(2)}) collective-permute-start(bf16[33,16,128]{2,1,0:T(8,128)(2,1)S(1)} %get-tuple-element.19), channel_id=1, source_target_pairs={{0,4},{4,0},{1,5},{5,1},{2,6},{6,2},{3,7},{7,3},{8,12},{12,8},{9,1... | collective-permute-start | bytes 405512 | tf_op jit(solution)/shard_map/ppermute | solution.py:421
  182.4 5.0 %collective-permute-done.1.met = bf16[33,16,128]{2,1,0:T(8,128)(2,1)S(1)} collective-permute-done((bf16[33,16,128]{2,1,0:T(8,128)(2,1)S(1)}, bf16[33,16,128]{2,1,0:T(8,128)(2,1)S(1)}, u32[]{:S(2)}, u32[]{:S(2)}) %collective-permute-start.1) | collective-permute-done | bytes 135200 | tf_op jit(solution)/shard_map/ppermute | solution.py:421
  187.4 0.1 shard_map.176
  187.6 18.6 %all_to_all.21.shares = bf16[32,16,128]{2,1,0:T(8,128)(2,1)S(1)} all-to-all(bf16[32,16,128]{2,1,0:T(8,128)(2,1)S(1)} %get-tuple-element.21), channel_id=1, replica_groups=mesh['z'=4,'c'=2,'y'=4,'h'=2,'x'=4] {'z','c','x'}, dimensions={0} | all-to-all | bytes 262144 | tf_op jit(solution)/shard_map/all_to_all | solution.py:423
  206.2 0.7 shard_map.177
  206.8 3.3 %all-to-all-start.3 = ((f32[8,16,128]{2,1,0:T(8,128)}), f32[8,16,128]{2,1,0:T(8,128)S(1)}, u32[]{:S(2)}, u32[]{:S(2)}) async-start(f32[8,16,128]{2,1,0:T(8,128)} %shard_map.177), calls=%async_computation.3 | async-start | bytes 131072 | tf_op jit(solution)/shard_map/all_to_all | solution.py:426
  210.2 0.5 slice.3
  211.4 7.8 %all-to-all-done.3.total = f32[8,16,128]{2,1,0:T(8,128)S(1)} async-done(((f32[8,16,128]{2,1,0:T(8,128)}), f32[8,16,128]{2,1,0:T(8,128)S(1)}, u32[]{:S(2)}, u32[]{:S(2)}) %all-to-all-start.3) | async-done | bytes 65568 | tf_op jit(solution)/shard_map/all_to_all | solution.py:426
  219.2 0.7 shard_map.178
  (6 shorter events, 0.0 us)
Async XLA Ops:
  7.2 126.0 %all-gather.2.cloned.1.call-start = ((), (), s32[]{:S(2)}) async-start(), calls=%async_computation.4 | async-start | bytes 22364160 | tf_op jit(solution)/shard_map/all_gather | solution.py:393
  10.7 23.0 %collective-permute-start = (bf16[128,2048]{1,0:T(8,128)(2,1)}, bf16[128,2048]{1,0:T(8,128)(2,1)S(1)}, u32[]{:S(2)}, u32[]{:S(2)}) collective-permute-start(bf16[128,2048]{1,0:T(8,128)(2,1)} %get-tuple-element.17), channel_id=1, source_target_pairs={{0,4},{4,0},{1,5},{5,1},{2,6},{6,2},{3,7},{7,3},{8,12},{12,8},{9,1... | collective-permute-start | bytes 1572872 | tf_op jit(solution)/shard_map/ppermute | solution.py:392
  37.5 5.3 %copy-start.3 = (s32[1,2,64]{2,1,0:T(2,128)S(1)}, s32[1,2,64]{2,1,0:T(2,128)}, u32[]{:S(2)}) copy-start(s32[1,2,64]{2,1,0:T(2,128)} %param.16) | copy-start | bytes 1540
  37.5 5.4 %copy-start.4 = (f32[2]{0:T(128)S(1)}, f32[2]{0:T(128)}, u32[]{:S(2)}) copy-start(f32[2]{0:T(128)} %constant.64.clone) | copy-start | bytes 28
  37.5 48.8 %all-to-all-start = ((bf16[4,256,2048]{2,1,0:T(8,128)(2,1)}), bf16[4,256,2048]{2,1,0:T(8,128)(2,1)}, u32[]{:S(2)}, u32[]{:S(2)}) async-start(bf16[4,256,2048]{2,1,0:T(8,128)(2,1)} %broadcast_in_dim.10), calls=%async_computation | async-start | bytes 8388608 | tf_op jit(solution)/shard_map/all_to_all | solution.py:396
  43.2 90.0 %copy-start = (bf16[1,2,64,2048]{3,2,1,0:T(8,128)(2,1)S(1)}, bf16[1,2,64,2048]{3,2,1,0:T(8,128)(2,1)}, u32[]{:S(2)}) copy-start(bf16[1,2,64,2048]{3,2,1,0:T(8,128)(2,1)} %param.14) | copy-start | bytes 1572868
  43.2 90.0 %copy-start.1 = (bf16[1,2,64,2048]{3,2,1,0:T(8,128)(2,1)S(1)}, bf16[1,2,64,2048]{3,2,1,0:T(8,128)(2,1)}, u32[]{:S(2)}) copy-start(bf16[1,2,64,2048]{3,2,1,0:T(8,128)(2,1)} %param.15) | copy-start | bytes 1572868
  43.2 89.9 %copy-start.2 = (f32[2048]{0:T(1024)S(1)}, f32[2048]{0:T(1024)}, u32[]{:S(2)}) copy-start(f32[2048]{0:T(1024)} %param.18) | copy-start | bytes 24580
  179.5 7.9 %collective-permute-start.1 = (bf16[33,16,128]{2,1,0:T(8,128)(2,1)S(1)}, bf16[33,16,128]{2,1,0:T(8,128)(2,1)S(1)}, u32[]{:S(2)}, u32[]{:S(2)}) collective-permute-start(bf16[33,16,128]{2,1,0:T(8,128)(2,1)S(1)} %get-tuple-element.19), channel_id=1, source_target_pairs={{0,4},{4,0},{1,5},{5,1},{2,6},{6,2},{3,7},{7,3},{8,12},{12,8},{9,1... | collective-permute-start | bytes 405512 | tf_op jit(solution)/shard_map/ppermute | solution.py:421
  206.8 12.4 %all-to-all-start.3 = ((f32[8,16,128]{2,1,0:T(8,128)}), f32[8,16,128]{2,1,0:T(8,128)S(1)}, u32[]{:S(2)}, u32[]{:S(2)}) async-start(f32[8,16,128]{2,1,0:T(8,128)} %shard_map.177), calls=%async_computation.3 | async-start | bytes 131072 | tf_op jit(solution)/shard_map/all_to_all | solution.py:426
Sparse Core Ops, SparseCore 0:
  10.9 122.2 all-gather.1

commit v5 on v4

--- a/solution.py
+++ b/solution.py
@@ -231,44 +231,57 @@
     dn_t = dn[...].T
     low_t = low[...].T
     low_own_t = low[pl.ds(own, ROWS), :].T
-    lane16 = lane_of(16)
-    left = lane16 < RANK
+    left = lane_of(8) < RANK
     for n in range(D // tile):
         cols = slice(n * tile, n * tile + tile)
-        ga_t = (ADAPTER_SCALE * mm(dn_t, xa[:, cols])).T
-        gb_t = (ADAPTER_SCALE * mm(low_own_t, bq[:, cols])).T
+        ga = (ADAPTER_SCALE * mm(dn_t, xa[:, cols])).astype(BF).T
+        gb = (ADAPTER_SCALE * mm(low_own_t, bq[:, cols])).T
         for d in range(tile // TOK):
-            at = n * (tile // TOK) + d
-            ga, gb = ga_t[d * TOK : d * TOK + TOK], gb_t[d * TOK : d * TOK + TOK]
             for q in range(4):
-                out[q, at] = ga[q * 16 : q * 16 + 16].astype(BF)
-            for q in range(2):
-                out[4 + q, at] = jnp.where(left, gb[q * 32 : q * 32 + 16], pltpu.roll(gb[q * 32 + 16 : q * 32 + 32], RANK, 1)).astype(BF)
-    gv_t = (ADAPTER_SCALE * mm(low_t, vt[...])).T
-    for d in range(32):
-        out[6, d] = jnp.where(left, pltpu.roll(gv_t[16 * d : 16 * d + 16], RANK, 1), 0.0).astype(BF)
-        out[7, d] = jnp.zeros((16, 2 * RANK), BF)
+                r0 = d * TOK + 16 * q
+                out[q, n * (tile // TOK) + d] = ga[r0 : r0 + 16]
+        for pair in range(tile // TOK // 2):
+            for q in range(4):
+                both = []
+                for r0 in (2 * pair * TOK + 16 * q, (2 * pair + 1) * TOK + 16 * q):
+                    both.append(jnp.where(left, gb[r0 : r0 + 8], pltpu.roll(gb[r0 + 8 : r0 + 16], RANK, 1)))
+                out[q, 32 + n * (tile // TOK // 2) + pair] = jnp.concatenate(both, axis=0).astype(BF)
+    gv = (ADAPTER_SCALE * mm(low_t, vt[...])).T
+    for quad in range(8):
+        for q in range(2):
+            v = [gv[16 * (4 * quad + j) + 8 * q : 16 * (4 * quad + j) + 8 * q + 8] for j in range(4)]
+            both = [jnp.where(left, pltpu.roll(v[j], RANK, 1), v[j + 1]) for j in (0, 2)]
+            out[q, 48 + quad] = jnp.concatenate(both, axis=0).astype(BF)
+            out[2 + q, 48 + quad] = jnp.zeros((16, 2 * RANK), BF)
     riding = split3(margin)
-    for q in range(8):
-        out[q, 32] = riding
+    for q in range(4):
+        out[q, 56] = riding
 
 
 def ride_of(block):
     return jnp.sum(block[0:1, :], axis=-1, keepdims=True)
 
 
-def halves_kernel(h_ref, got, keep, send, margin_out):
+def halves_kernel(h_ref, got, keep, send, margin_out, both):
     h = h_ref[0]
-    ride = got[0, 0, 32].astype(F32)
-    kept, sent = got[0, h, 0:32].astype(F32), got[0, 1 - h, 0:32].astype(F32)
+    total = got[0].astype(F32)
     for q in range(1, 4):
-        ride = ride + got[q, 0, 32].astype(F32)
-        kept = kept + got[q, h, 0:32].astype(F32)
-        sent = sent + got[q, 1 - h, 0:32].astype(F32)
-    margin = ride_of(ride)
+        total = total + got[q].astype(F32)
+    left = lax.broadcasted_iota(jnp.int32, (8, 2 * RANK), 1) < RANK
+    for d in range(32):
+        b0, v0 = 8 * (d % 2), 8 * (d % 4 // 2)
+        b = total[32 + d // 2, b0 : b0 + 8]
+        v = total[48 + d // 4, v0 : v0 + 8]
+        if d % 2 == 0:
+            v = pltpu.roll(v, RANK, 1)
+        both[0, d, 0:8] = total[d, 0:8]
+        both[0, d, 8:16] = jnp.where(left, b, v)
+        both[1, d, 0:8] = total[d, 8:16]
+        both[1, d, 8:16] = jnp.where(left, pltpu.roll(b, RANK, 1), 0.0)
+    margin = ride_of(total[56])
     margin_out[...] = jnp.broadcast_to(margin, (8, 2 * RANK))
-    keep[...] = kept
-    send[0:32] = sent.astype(BF)
+    keep[...] = both[h]
+    send[0:32] = both[1 - h].astype(BF)
     send[32] = split3(margin)
 
 
@@ -288,23 +301,23 @@
 
 
 def finish_kernel(total, a_q, b_q, a_v, b_v):
-    for e in range(4):
-        at = slice(16 * e, 16 * e + 16)
-        a_q[at, :] = total[e, :, 0:RANK]
-        a_v[at, :] = total[e, :, RANK : 2 * RANK]
-    for e in range(2):
-        b_q[32 * e : 32 * e + 16, :] = total[4 + e, :, 0:RANK]
-        b_q[32 * e + 16 : 32 * e + 32, :] = total[4 + e, :, RANK : 2 * RANK]
-    b_v[...] = total[6, :, 0:RANK]
-
-
-def small_call(kernel, out_shape, *args, scalars=0):
+    for e in range(8):
+        at = slice(8 * e, 8 * e + 8)
+        a_q[at, :] = total[e, 0:8, 0:RANK]
+        a_v[at, :] = total[e, 0:8, RANK : 2 * RANK]
+        b_q[at, :] = total[e, 8:16, 0:RANK]
+    for q in range(2):
+        b_v[8 * q : 8 * q + 8, :] = total[2 * q, 8:16, RANK : 2 * RANK]
+
+
+def small_call(kernel, out_shape, *args, scalars=0, scratch=()):
     vm = pl.BlockSpec(memory_space=pltpu.VMEM)
     return pl.pallas_call(
         kernel,
         out_shape=out_shape,
         in_specs=[pl.BlockSpec(memory_space=pltpu.SMEM)] * scalars + [vm] * (len(args) - scalars),
         out_specs=(vm,) * len(out_shape),
+        scratch_shapes=scratch,
         compiler_params=pltpu.CompilerParams(vmem_limit_bytes=16 * 2**20),
     )(*args)
 
@@ -365,7 +378,7 @@
     bf, f32 = (lambda *s: pltpu.VMEM(s, BF)), (lambda *s: pltpu.VMEM(s, F32))
     return pl.pallas_call(
         local_kernel,
-        out_shape=jax.ShapeDtypeStruct((8, 33, 16, 2 * RANK), BF),
+        out_shape=jax.ShapeDtypeStruct((4, 57, 16, 2 * RANK), BF),
         in_specs=[pl.BlockSpec(memory_space=pltpu.SMEM), anyspace] + [vm] * 8,
         out_specs=vm,
         scratch_shapes=[
@@ -413,10 +426,11 @@
 
     mine = local_step(own_block, full, xa, kc, ks, bias, hidden.reshape(ROWS, D), answer_rows.reshape(ROWS, D), final_gain.reshape(1, D), sign)
 
-    got = lax.all_to_all(mine.reshape(4, 2, 33, 16, 2 * RANK), "y", 0, 0, tiled=True)
+    got = lax.all_to_all(mine, "y", 0, 0, tiled=True)
     tile, vector = (16, 2 * RANK), jax.ShapeDtypeStruct((8, 2 * RANK), F32)
     keep, send, part = small_call(
-        halves_kernel, (jax.ShapeDtypeStruct((32,) + tile, F32), jax.ShapeDtypeStruct((33,) + tile, BF), vector), h_one, got, scalars=1
+        halves_kernel, (jax.ShapeDtypeStruct((32,) + tile, F32), jax.ShapeDtypeStruct((33,) + tile, BF), vector), h_one, got, scalars=1,
+        scratch=(pltpu.VMEM((2, 32) + tile, F32),),
     )
     met = lax.ppermute(send, "h", [(0, 1), (1, 0)])
     scaled, margin = small_call(scale_kernel, (jax.ShapeDtypeStruct((32,) + tile, BF), vector), keep, met, part)

time: 228 us -> 227 us (level)
  no operation moved by 1% of the time
where the time goes in v5:
time: 227 us; the launch traced here: 226 us
  waiting for transfers between devices  116 us (51%)
  blocking collectives  35.7 us (16%)
  Pallas kernels  32.5 us (14%)
  starting transfers between devices  19.1 us (8%)
  between operations  16 us (7%)
  local copies, waits for them, and re-layouts  3.7 us (2%)
  other arithmetic  3.56 us (2%)
    all_gather x1, waiting for transfers between devices, body(): lax.all_gather(packed, ('h',) + OWN, axis=0, tiled=True)  46.9 us
    all_to_all x1, waiting for transfers between devices, body(): lax.all_to_all(jnp.broadcast_to(two[None], (4,) + two.shape), 'y', 0, 0,...  40.7 us
    pallas_call x1, Pallas kernels, local_step(): pl.pallas_call(local_kernel, out_shape=jax.ShapeDtypeStruct((4, 57, 16, 2...  27.3 us
    all_to_all x1, blocking collectives, body(): shares = lax.all_to_all(scaled, OWN, 0, 0, tiled=True)  18.6 us
    all_to_all x1, blocking collectives, body(): got = lax.all_to_all(mine, 'y', 0, 0, tiled=True)  17.1 us
    ppermute x1, waiting for transfers between devices, body(): other = lax.ppermute(xn, 'h', [(0, 1), (1, 0)])  15.2 us
    ppermute x1, starting transfers between devices, body(): other = lax.ppermute(xn, 'h', [(0, 1), (1, 0)])  7.78 us
    all_to_all x1, waiting for transfers between devices, body(): total = lax.all_to_all(spread, ('y', 'h'), 0, 0, tiled=True)  7.77 us
  transfers between devices with their start and end apart: 5, of which 5 were waited for; matrix products, arithmetic and copies ran while one was open for 3% of the time, Pallas kernels for 0%

profile of v5, /device:TPU:1, one launch (start us, length us, event | category | flops | bytes accessed | tf_op | source)
XLA Modules:
  0.0 226.2 jit_solution(17851095101724594521)
XLA Ops:
  7.2 0.0 all-gather.2.cloned.1.call-start
  7.2 3.5 %shard_map.173 = (bf16[64,2688]{1,0:T(8,128)(2,1)}, bf16[128,2048]{1,0:T(8,128)(2,1)}) custom-call(s32[1]{0:T(128)} %bitcast.h_ref, bf16[64,2048]{1,0:T(8,128)(2,1)} %wq.1, bf16[64,512]{1,0:T(8,128)(2,1)} %wk.1, bf16[64,512]{1,0:T(8,128)(2,1)} %wv.1, bf16[64,2048]{1,0:T(8,128)(2,1)} %wo.1, bf16[64,64]{1,0:T(8,128)(2,1)} %aq.1, bf16[64,64]{1,0:T(8,128)(2,1)} %av.1, ...), custom_call_target="tpu_custom_call" | custom-call | tf_op jit(solution)/shard_map/pallas_call | solution.py:363
  10.7 0.0 all-gather.2.cloned.1.call-update
  10.7 7.8 %collective-permute-start = (bf16[128,2048]{1,0:T(8,128)(2,1)}, bf16[128,2048]{1,0:T(8,128)(2,1)S(1)}, u32[]{:S(2)}, u32[]{:S(2)}) collective-permute-start(bf16[128,2048]{1,0:T(8,128)(2,1)} %get-tuple-element.17), channel_id=1, source_target_pairs={{0,4},{4,0},{1,5},{5,1},{2,6},{6,2},{3,7},{7,3},{8,12},{12,8},{9,1... | collective-permute-start | bytes 1572872 | tf_op jit(solution)/shard_map/ppermute | solution.py:405
  18.5 15.2 %collective-permute-done = bf16[128,2048]{1,0:T(8,128)(2,1)S(1)} collective-permute-done((bf16[128,2048]{1,0:T(8,128)(2,1)}, bf16[128,2048]{1,0:T(8,128)(2,1)S(1)}, u32[]{:S(2)}, u32[]{:S(2)}) %collective-permute-start) | collective-permute-done | bytes 524320 | tf_op jit(solution)/shard_map/ppermute | solution.py:405
  33.8 1.1 pad_maximum_fusion
  34.9 2.6 %broadcast_in_dim.10 = bf16[4,256,2048]{2,1,0:T(8,128)(2,1)} broadcast(bf16[256,2048]{1,0:T(8,128)(2,1)S(1)} %pad_maximum_fusion), dimensions={1,2} | broadcast | bytes 5242880 | tf_op jit(solution)/shard_map/broadcast_in_dim | solution.py:409
  37.5 0.0 copy-start.3
  37.5 0.0 copy-start.4
  37.5 5.0 %all-to-all-start = ((bf16[4,256,2048]{2,1,0:T(8,128)(2,1)}), bf16[4,256,2048]{2,1,0:T(8,128)(2,1)}, u32[]{:S(2)}, u32[]{:S(2)}) async-start(bf16[4,256,2048]{2,1,0:T(8,128)(2,1)} %broadcast_in_dim.10), calls=%async_computation | async-start | bytes 8388608 | tf_op jit(solution)/shard_map/all_to_all | solution.py:409
  42.6 0.0 copy-start
  42.6 0.0 copy-start.1
  42.6 0.0 copy-start.2
  42.6 0.1 iota_add_fusion
  42.7 0.1 convert_element_type.25
  42.8 0.1 add.71
  42.8 0.0 copy-done.3
  42.9 0.1 convert_element_type.27
  42.9 0.0 copy-done.4
  42.9 0.1 mul.78
  43.0 0.1 mul.79
  43.1 0.1 copy.21.sign
  43.2 1.9 fusion
  45.1 0.3 pad_maximum_fusion.1
  45.5 0.1 compare_select_fusion.bias
  45.6 40.7 %all-to-all-done = bf16[4,256,2048]{2,1,0:T(8,128)(2,1)} async-done(((bf16[4,256,2048]{2,1,0:T(8,128)(2,1)}), bf16[4,256,2048]{2,1,0:T(8,128)(2,1)}, u32[]{:S(2)}, u32[]{:S(2)}) %all-to-all-start) | async-done | bytes 4194336 | tf_op jit(solution)/shard_map/all_to_all | solution.py:409
  86.3 46.9 %all-gather.2.cloned.1.call-done = bf16[4096,2688]{1,0:T(8,128)(2,1)} async-done(((bf16[64,2688]{1,0:T(8,128)(2,1)}), bf16[4096,2688]{1,0:T(8,128)(2,1)}) %all-gather.2.cloned.1.call-update) | async-done | bytes 22020112 | tf_op jit(solution)/shard_map/all_gather | solution.py:406
  133.2 0.0 copy-done
  133.2 0.0 copy-done.1
  133.2 0.0 copy-done.2
  133.2 27.3 %shard_map.174 = bf16[4,57,16,128]{3,2,1,0:T(8,128)(2,1)S(1)} custom-call(s32[1]{0:T(128)} %bitcast.1.own_ref, bf16[2,2048,2688]{2,1,0:T(8,128)(2,1)} %bitcast.14, bf16[1024,2048]{1,0:T(8,128)(2,1)} %bitcast.5.xa, f32[1024,128]{1,0:T(8,128)S(1)} %get-tuple-element.32.kc, f32[1024,128]{1,0:T(8,128)S(1)} %get-tuple-element.33.ks, ...), custom_call_target="tpu_custom_call" | custom-call | flops 24000000000 | bytes 27000000 | tf_op jit(solution)/shard_map/pallas_call | solution.py:379
  160.5 17.1 %all_to_all.20.got = bf16[4,57,16,128]{3,2,1,0:T(8,128)(2,1)S(1)} all-to-all(bf16[4,57,16,128]{3,2,1,0:T(8,128)(2,1)S(1)} %shard_map.174), channel_id=1, replica_groups=mesh['z'=4,'c'=2,'y'=4,'h'=2,'x'=4] {'y'}, dimensions={0} | all-to-all | bytes 1867776 | tf_op jit(solution)/shard_map/all_to_all | solution.py:429
  177.6 0.2 shard_map.175
  177.8 3.0 %collective-permute-start.1 = (bf16[33,16,128]{2,1,0:T(8,128)(2,1)S(1)}, bf16[33,16,128]{2,1,0:T(8,128)(2,1)S(1)}, u32[]{:S(2)}, u32[]{:S(2)}) collective-permute-start(bf16[33,16,128]{2,1,0:T(8,128)(2,1)S(1)} %get-tuple-element.19), channel_id=1, source_target_pairs={{0,4},{4,0},{1,5},{5,1},{2,6},{6,2},{3,7},{7,3},{8,12},{12,8},{9,1... | collective-permute-start | bytes 405512 | tf_op jit(solution)/shard_map/ppermute | solution.py:435
  180.8 5.0 %collective-permute-done.1.met = bf16[33,16,128]{2,1,0:T(8,128)(2,1)S(1)} collective-permute-done((bf16[33,16,128]{2,1,0:T(8,128)(2,1)S(1)}, bf16[33,16,128]{2,1,0:T(8,128)(2,1)S(1)}, u32[]{:S(2)}, u32[]{:S(2)}) %collective-permute-start.1) | collective-permute-done | bytes 135200 | tf_op jit(solution)/shard_map/ppermute | solution.py:435
  185.7 0.1 shard_map.176
  185.9 18.6 %all_to_all.21.shares = bf16[32,16,128]{2,1,0:T(8,128)(2,1)S(1)} all-to-all(bf16[32,16,128]{2,1,0:T(8,128)(2,1)S(1)} %get-tuple-element.21), channel_id=1, replica_groups=mesh['z'=4,'c'=2,'y'=4,'h'=2,'x'=4] {'z','c','x'}, dimensions={0} | all-to-all | bytes 262144 | tf_op jit(solution)/shard_map/all_to_all | solution.py:437
  204.5 0.7 shard_map.177
  205.2 3.3 %all-to-all-start.3 = ((f32[8,16,128]{2,1,0:T(8,128)}), f32[8,16,128]{2,1,0:T(8,128)S(1)}, u32[]{:S(2)}, u32[]{:S(2)}) async-start(f32[8,16,128]{2,1,0:T(8,128)} %shard_map.177), calls=%async_computation.3 | async-start | bytes 131072 | tf_op jit(solution)/shard_map/all_to_all | solution.py:440
  208.5 0.5 slice.3
  209.8 7.8 %all-to-all-done.3.total = f32[8,16,128]{2,1,0:T(8,128)S(1)} async-done(((f32[8,16,128]{2,1,0:T(8,128)}), f32[8,16,128]{2,1,0:T(8,128)S(1)}, u32[]{:S(2)}, u32[]{:S(2)}) %all-to-all-start.3) | async-done | bytes 65568 | tf_op jit(solution)/shard_map/all_to_all | solution.py:440
  217.5 0.7 shard_map.178
  (6 shorter events, 0.0 us)
Async XLA Ops:
  7.2 126.0 %all-gather.2.cloned.1.call-start = ((), (), s32[]{:S(2)}) async-start(), calls=%async_computation.4 | async-start | bytes 22364160 | tf_op jit(solution)/shard_map/all_gather | solution.py:406
  10.7 23.0 %collective-permute-start = (bf16[128,2048]{1,0:T(8,128)(2,1)}, bf16[128,2048]{1,0:T(8,128)(2,1)S(1)}, u32[]{:S(2)}, u32[]{:S(2)}) collective-permute-start(bf16[128,2048]{1,0:T(8,128)(2,1)} %get-tuple-element.17), channel_id=1, source_target_pairs={{0,4},{4,0},{1,5},{5,1},{2,6},{6,2},{3,7},{7,3},{8,12},{12,8},{9,1... | collective-permute-start | bytes 1572872 | tf_op jit(solution)/shard_map/ppermute | solution.py:405
  37.5 5.3 %copy-start.3 = (s32[1,2,64]{2,1,0:T(2,128)S(1)}, s32[1,2,64]{2,1,0:T(2,128)}, u32[]{:S(2)}) copy-start(s32[1,2,64]{2,1,0:T(2,128)} %param.16) | copy-start | bytes 1540
  37.5 5.4 %copy-start.4 = (f32[2]{0:T(128)S(1)}, f32[2]{0:T(128)}, u32[]{:S(2)}) copy-start(f32[2]{0:T(128)} %constant.64.clone) | copy-start | bytes 28
  37.5 48.8 %all-to-all-start = ((bf16[4,256,2048]{2,1,0:T(8,128)(2,1)}), bf16[4,256,2048]{2,1,0:T(8,128)(2,1)}, u32[]{:S(2)}, u32[]{:S(2)}) async-start(bf16[4,256,2048]{2,1,0:T(8,128)(2,1)} %broadcast_in_dim.10), calls=%async_computation | async-start | bytes 8388608 | tf_op jit(solution)/shard_map/all_to_all | solution.py:409
  42.6 90.6 %copy-start = (bf16[1,2,64,2048]{3,2,1,0:T(8,128)(2,1)S(1)}, bf16[1,2,64,2048]{3,2,1,0:T(8,128)(2,1)}, u32[]{:S(2)}) copy-start(bf16[1,2,64,2048]{3,2,1,0:T(8,128)(2,1)} %param.14) | copy-start | bytes 1572868
  42.6 90.6 %copy-start.1 = (bf16[1,2,64,2048]{3,2,1,0:T(8,128)(2,1)S(1)}, bf16[1,2,64,2048]{3,2,1,0:T(8,128)(2,1)}, u32[]{:S(2)}) copy-start(bf16[1,2,64,2048]{3,2,1,0:T(8,128)(2,1)} %param.15) | copy-start | bytes 1572868
  42.6 90.6 %copy-start.2 = (f32[2048]{0:T(1024)S(1)}, f32[2048]{0:T(1024)}, u32[]{:S(2)}) copy-start(f32[2048]{0:T(1024)} %param.18) | copy-start | bytes 24580
  177.8 8.0 %collective-permute-start.1 = (bf16[33,16,128]{2,1,0:T(8,128)(2,1)S(1)}, bf16[33,16,128]{2,1,0:T(8,128)(2,1)S(1)}, u32[]{:S(2)}, u32[]{:S(2)}) collective-permute-start(bf16[33,16,128]{2,1,0:T(8,128)(2,1)S(1)} %get-tuple-element.19), channel_id=1, source_target_pairs={{0,4},{4,0},{1,5},{5,1},{2,6},{6,2},{3,7},{7,3},{8,12},{12,8},{9,1... | collective-permute-start | bytes 405512 | tf_op jit(solution)/shard_map/ppermute | solution.py:435
  205.2 12.4 %all-to-all-start.3 = ((f32[8,16,128]{2,1,0:T(8,128)}), f32[8,16,128]{2,1,0:T(8,128)S(1)}, u32[]{:S(2)}, u32[]{:S(2)}) async-start(f32[8,16,128]{2,1,0:T(8,128)} %shard_map.177), calls=%async_computation.3 | async-start | bytes 131072 | tf_op jit(solution)/shard_map/all_to_all | solution.py:440
Sparse Core Ops, SparseCore 0:
  10.9 122.2 all-gather.1

commit v6 on v5

--- a/solution.py
+++ b/solution.py
@@ -72,8 +72,8 @@
         return made
 
     copies = [
-        pieces(0, 0, (0, 256), wn, (0, 256)),
-        pieces(1, 1, (0, 1024), wkv, (0, 1024)),
+        pieces(0, 1, (0, KVW), wkv, (0, KVW)),
+        pieces(1, 0, (0, 256), wn, (0, 256)) + pieces(5, 1, (KVW, 2 * KVW), wkv, (KVW, 2 * KVW)),
         pieces(2, 0, (256, 2304), wq, (0, 2048)),
         pieces(3, 0, (2304, 2688), wo, (0, 384)),
         pieces(4, 1, (1024, 2688), wo, (384, 2048)),
@@ -88,15 +88,30 @@
 
     begin(0)
     begin(1)
+    begin(2)
 
     own = pl.multiple_of(own_ref[0] * ROWS, ROWS)
 
+    lane_of = lambda n: lax.broadcasted_iota(jnp.int32, (n, 2 * RANK), 1)
     arrived(0)
-    lane_of = lambda n: lax.broadcasted_iota(jnp.int32, (n, 2 * RANK), 1)
+
+    def spread_rows(ref, g, r, value):
+        for b in range(2):
+            t0 = pl.multiple_of(r * 2 * TOK + b * TOK, TOK)
+            for side in range(2):
+                ref[side * HK + g, pl.ds(t0, TOK), :] = value[b * ROWS + side * TOK : b * ROWS + side * TOK + TOK]
+
+    @pl.loop(0, ALL // 256, unroll=2)
+    def _(r):
+        r0 = pl.multiple_of(r * 256, 256)
+        c, s = kc[pl.ds(r0, 256), :], ks[pl.ds(r0, 256), :]
+        k = mm(xa[pl.ds(r0, 256), :], wkv[:, :KVW])
+        for g in range(HK):
+            spread_rows(keys, g, r, turn(k[:, HD * g : HD * g + HD], c, s).astype(BF))
+
+    arrived(1)
     for d in range(32):
         bv[16 * d : 16 * d + 16, :] = wn[64 * d : 64 * d + 16, 2 * RANK :]
-    arrived(1)
-    begin(2)
 
     @pl.loop(0, ALL // 256, unroll=2)
     def _(r):
@@ -104,22 +119,13 @@
         x = xa[pl.ds(r0, 256), :]
         lw = mm(x, wn[:, : 2 * RANK])
         low[pl.ds(r0, 256), :] = lw.astype(BF)
-        c, s = kc[pl.ds(r0, 256), :], ks[pl.ds(r0, 256), :]
-        kv = mm(x, wkv[...])
+        v = mm(x, wkv[:, KVW:])
         lift = mm_t(jnp.where(lane_of(256) < RANK, 0.0, lw).astype(BF), bv[...])
         for g in range(HK):
             cols = slice(HD * g, HD * g + HD)
-            k = turn(kv[:, cols], c, s).astype(BF)
-            vr = kv[:, KVW + HD * g : KVW + HD * g + HD].astype(BF)
-            vp = (vr.astype(F32) + ADAPTER_SCALE * lift[:, cols]).astype(BF)
-            for b in range(2):
-                t0 = pl.multiple_of(r * 2 * TOK + b * TOK, TOK)
-                for side in range(2):
-                    src = slice(b * ROWS + side * TOK, b * ROWS + side * TOK + TOK)
-                    at = side * HK + g
-                    keys[at, pl.ds(t0, TOK), :] = k[src]
-                    vref[at, pl.ds(t0, TOK), :] = vr[src]
-                    vpol[at, pl.ds(t0, TOK), :] = vp[src]
+            vr = v[:, cols].astype(BF)
+            spread_rows(vref, g, r, vr)
+            spread_rows(vpol, g, r, (vr.astype(F32) + ADAPTER_SCALE * lift[:, cols]).astype(BF))
 
     arrived(2)
     begin(3)
@@ -387,7 +393,7 @@
             bf(PARTS, L, HD), bf(PARTS, L, HD), bf(PARTS, L, HD),
             bf(2, PARTS, QROWS, HD), f32(PARTS, QROWS, L), bf(PARTS, QROWS, L), f32(PARTS, QROWS, HD),
             bf(2 * ROWS, D), f32(ROWS, D), bf(ROWS, D), bf(PARTS, QROWS, HD), bf(ROWS, D), bf(ALL, KVW), bf(ALL, 2 * RANK),
-            pltpu.SemaphoreType.DMA((5, PIECES)),
+            pltpu.SemaphoreType.DMA((6, PIECES)),
         ],
         compiler_params=pltpu.CompilerParams(vmem_limit_bytes=50 * 2**20),
         cost_estimate=pl.CostEstimate(flops=24_000_000_000, bytes_accessed=27_000_000, transcendentals=2_100_000),

time: 227 us -> 226 us (level)
  no operation moved by 1% of the time
where the time goes in v6:
time: 226 us
  waiting for transfers between devices  116 us (51%)
  blocking collectives  35.8 us (16%)
  Pallas kernels  32.1 us (14%)
  starting transfers between devices  18.8 us (8%)
  between operations  16 us (7%)
  local copies, waits for them, and re-layouts  3.7 us (2%)
  other arithmetic  3.56 us (2%)
    all_gather x1, waiting for transfers between devices, body(): lax.all_gather(packed, ('h',) + OWN, axis=0, tiled=True)  46.9 us
    all_to_all x1, waiting for transfers between devices, body(): lax.all_to_all(jnp.broadcast_to(two[None], (4,) + two.shape), 'y', 0, 0,...  40.7 us
    pallas_call x1, Pallas kernels, local_step(): pl.pallas_call(local_kernel, out_shape=jax.ShapeDtypeStruct((4, 57, 16, 2...  26.9 us
    all_to_all x1, blocking collectives, body(): shares = lax.all_to_all(scaled, OWN, 0, 0, tiled=True)  18.4 us
    all_to_all x1, blocking collectives, body(): got = lax.all_to_all(mine, 'y', 0, 0, tiled=True)  17.4 us
    ppermute x1, waiting for transfers between devices, body(): other = lax.ppermute(xn, 'h', [(0, 1), (1, 0)])  15.2 us
    ppermute x1, starting transfers between devices, body(): other = lax.ppermute(xn, 'h', [(0, 1), (1, 0)])  7.78 us
    all_to_all x1, waiting for transfers between devices, body(): total = lax.all_to_all(spread, ('y', 'h'), 0, 0, tiled=True)  7.77 us
  transfers between devices with their start and end apart: 5, of which 5 were waited for; matrix products, arithmetic and copies ran while one was open for 3% of the time, Pallas kernels for 0%

profile of v6, /device:TPU:1, one launch (start us, length us, event | category | flops | bytes accessed | tf_op | source)
XLA Modules:
  0.0 225.9 jit_solution(11693038681987692855)
XLA Ops:
  7.2 0.0 all-gather.2.cloned.1.call-start
  7.2 3.5 %shard_map.173 = (bf16[64,2688]{1,0:T(8,128)(2,1)}, bf16[128,2048]{1,0:T(8,128)(2,1)}) custom-call(s32[1]{0:T(128)} %bitcast.h_ref, bf16[64,2048]{1,0:T(8,128)(2,1)} %wq.1, bf16[64,512]{1,0:T(8,128)(2,1)} %wk.1, bf16[64,512]{1,0:T(8,128)(2,1)} %wv.1, bf16[64,2048]{1,0:T(8,128)(2,1)} %wo.1, bf16[64,64]{1,0:T(8,128)(2,1)} %aq.1, bf16[64,64]{1,0:T(8,128)(2,1)} %av.1, ...), custom_call_target="tpu_custom_call" | custom-call | tf_op jit(solution)/shard_map/pallas_call | solution.py:369
  10.7 0.0 all-gather.2.cloned.1.call-update
  10.7 7.8 %collective-permute-start = (bf16[128,2048]{1,0:T(8,128)(2,1)}, bf16[128,2048]{1,0:T(8,128)(2,1)S(1)}, u32[]{:S(2)}, u32[]{:S(2)}) collective-permute-start(bf16[128,2048]{1,0:T(8,128)(2,1)} %get-tuple-element.17), channel_id=1, source_target_pairs={{0,4},{4,0},{1,5},{5,1},{2,6},{6,2},{3,7},{7,3},{8,12},{12,8},{9,1... | collective-permute-start | bytes 1572872 | tf_op jit(solution)/shard_map/ppermute | solution.py:411
  18.5 15.2 %collective-permute-done = bf16[128,2048]{1,0:T(8,128)(2,1)S(1)} collective-permute-done((bf16[128,2048]{1,0:T(8,128)(2,1)}, bf16[128,2048]{1,0:T(8,128)(2,1)S(1)}, u32[]{:S(2)}, u32[]{:S(2)}) %collective-permute-start) | collective-permute-done | bytes 524320 | tf_op jit(solution)/shard_map/ppermute | solution.py:411
  33.8 1.1 pad_maximum_fusion
  34.9 2.6 %broadcast_in_dim.10 = bf16[4,256,2048]{2,1,0:T(8,128)(2,1)} broadcast(bf16[256,2048]{1,0:T(8,128)(2,1)S(1)} %pad_maximum_fusion), dimensions={1,2} | broadcast | bytes 5242880 | tf_op jit(solution)/shard_map/broadcast_in_dim | solution.py:415
  37.5 0.0 copy-start.3
  37.5 0.0 copy-start.4
  37.5 5.0 %all-to-all-start = ((bf16[4,256,2048]{2,1,0:T(8,128)(2,1)}), bf16[4,256,2048]{2,1,0:T(8,128)(2,1)}, u32[]{:S(2)}, u32[]{:S(2)}) async-start(bf16[4,256,2048]{2,1,0:T(8,128)(2,1)} %broadcast_in_dim.10), calls=%async_computation | async-start | bytes 8388608 | tf_op jit(solution)/shard_map/all_to_all | solution.py:415
  42.6 0.0 copy-start
  42.6 0.0 copy-start.1
  42.6 0.0 copy-start.2
  42.6 0.1 iota_add_fusion
  42.7 0.1 convert_element_type.25
  42.8 0.1 add.71
  42.8 0.0 copy-done.3
  42.9 0.1 convert_element_type.27
  42.9 0.0 copy-done.4
  42.9 0.1 mul.78
  43.0 0.1 mul.79
  43.1 0.1 copy.21.sign
  43.2 1.9 fusion
  45.1 0.3 pad_maximum_fusion.1
  45.5 0.1 compare_select_fusion.bias
  45.6 40.7 %all-to-all-done = bf16[4,256,2048]{2,1,0:T(8,128)(2,1)} async-done(((bf16[4,256,2048]{2,1,0:T(8,128)(2,1)}), bf16[4,256,2048]{2,1,0:T(8,128)(2,1)}, u32[]{:S(2)}, u32[]{:S(2)}) %all-to-all-start) | async-done | bytes 4194336 | tf_op jit(solution)/shard_map/all_to_all | solution.py:415
  86.3 46.9 %all-gather.2.cloned.1.call-done = bf16[4096,2688]{1,0:T(8,128)(2,1)} async-done(((bf16[64,2688]{1,0:T(8,128)(2,1)}), bf16[4096,2688]{1,0:T(8,128)(2,1)}) %all-gather.2.cloned.1.call-update) | async-done | bytes 22020112 | tf_op jit(solution)/shard_map/all_gather | solution.py:412
  133.2 0.0 copy-done
  133.2 0.0 copy-done.1
  133.2 0.0 copy-done.2
  133.2 26.9 %shard_map.174 = bf16[4,57,16,128]{3,2,1,0:T(8,128)(2,1)S(1)} custom-call(s32[1]{0:T(128)} %bitcast.1.own_ref, bf16[2,2048,2688]{2,1,0:T(8,128)(2,1)} %bitcast.14, bf16[1024,2048]{1,0:T(8,128)(2,1)} %bitcast.5.xa, f32[1024,128]{1,0:T(8,128)S(1)} %get-tuple-element.32.kc, f32[1024,128]{1,0:T(8,128)S(1)} %get-tuple-element.33.ks, ...), custom_call_target="tpu_custom_call" | custom-call | flops 24000000000 | bytes 27000000 | tf_op jit(solution)/shard_map/pallas_call | solution.py:385
  160.1 17.4 %all_to_all.20.got = bf16[4,57,16,128]{3,2,1,0:T(8,128)(2,1)S(1)} all-to-all(bf16[4,57,16,128]{3,2,1,0:T(8,128)(2,1)S(1)} %shard_map.174), channel_id=1, replica_groups=mesh['z'=4,'c'=2,'y'=4,'h'=2,'x'=4] {'y'}, dimensions={0} | all-to-all | bytes 1867776 | tf_op jit(solution)/shard_map/all_to_all | solution.py:435
  177.4 0.2 shard_map.175
  177.7 2.6 %collective-permute-start.1 = (bf16[33,16,128]{2,1,0:T(8,128)(2,1)S(1)}, bf16[33,16,128]{2,1,0:T(8,128)(2,1)S(1)}, u32[]{:S(2)}, u32[]{:S(2)}) collective-permute-start(bf16[33,16,128]{2,1,0:T(8,128)(2,1)S(1)} %get-tuple-element.19), channel_id=1, source_target_pairs={{0,4},{4,0},{1,5},{5,1},{2,6},{6,2},{3,7},{7,3},{8,12},{12,8},{9,1... | collective-permute-start | bytes 405512 | tf_op jit(solution)/shard_map/ppermute | solution.py:441
  180.2 5.4 %collective-permute-done.1.met = bf16[33,16,128]{2,1,0:T(8,128)(2,1)S(1)} collective-permute-done((bf16[33,16,128]{2,1,0:T(8,128)(2,1)S(1)}, bf16[33,16,128]{2,1,0:T(8,128)(2,1)S(1)}, u32[]{:S(2)}, u32[]{:S(2)}) %collective-permute-start.1) | collective-permute-done | bytes 135200 | tf_op jit(solution)/shard_map/ppermute | solution.py:441
  185.6 0.1 shard_map.176
  185.8 18.4 %all_to_all.21.shares = bf16[32,16,128]{2,1,0:T(8,128)(2,1)S(1)} all-to-all(bf16[32,16,128]{2,1,0:T(8,128)(2,1)S(1)} %get-tuple-element.21), channel_id=1, replica_groups=mesh['z'=4,'c'=2,'y'=4,'h'=2,'x'=4] {'z','c','x'}, dimensions={0} | all-to-all | bytes 262144 | tf_op jit(solution)/shard_map/all_to_all | solution.py:443
  204.2 0.7 shard_map.177
  204.8 3.3 %all-to-all-start.3 = ((f32[8,16,128]{2,1,0:T(8,128)}), f32[8,16,128]{2,1,0:T(8,128)S(1)}, u32[]{:S(2)}, u32[]{:S(2)}) async-start(f32[8,16,128]{2,1,0:T(8,128)} %shard_map.177), calls=%async_computation.3 | async-start | bytes 131072 | tf_op jit(solution)/shard_map/all_to_all | solution.py:446
  208.2 0.5 slice.3
  209.5 7.8 %all-to-all-done.3.total = f32[8,16,128]{2,1,0:T(8,128)S(1)} async-done(((f32[8,16,128]{2,1,0:T(8,128)}), f32[8,16,128]{2,1,0:T(8,128)S(1)}, u32[]{:S(2)}, u32[]{:S(2)}) %all-to-all-start.3) | async-done | bytes 65568 | tf_op jit(solution)/shard_map/all_to_all | solution.py:446
  217.2 0.7 shard_map.178
  (6 shorter events, 0.0 us)
Async XLA Ops:
  7.2 126.0 %all-gather.2.cloned.1.call-start = ((), (), s32[]{:S(2)}) async-start(), calls=%async_computation.4 | async-start | bytes 22364160 | tf_op jit(solution)/shard_map/all_gather | solution.py:412
  10.7 23.0 %collective-permute-start = (bf16[128,2048]{1,0:T(8,128)(2,1)}, bf16[128,2048]{1,0:T(8,128)(2,1)S(1)}, u32[]{:S(2)}, u32[]{:S(2)}) collective-permute-start(bf16[128,2048]{1,0:T(8,128)(2,1)} %get-tuple-element.17), channel_id=1, source_target_pairs={{0,4},{4,0},{1,5},{5,1},{2,6},{6,2},{3,7},{7,3},{8,12},{12,8},{9,1... | collective-permute-start | bytes 1572872 | tf_op jit(solution)/shard_map/ppermute | solution.py:411
  37.5 5.3 %copy-start.3 = (s32[1,2,64]{2,1,0:T(2,128)S(1)}, s32[1,2,64]{2,1,0:T(2,128)}, u32[]{:S(2)}) copy-start(s32[1,2,64]{2,1,0:T(2,128)} %param.16) | copy-start | bytes 1540
  37.5 5.4 %copy-start.4 = (f32[2]{0:T(128)S(1)}, f32[2]{0:T(128)}, u32[]{:S(2)}) copy-start(f32[2]{0:T(128)} %constant.64.clone) | copy-start | bytes 28
  37.5 48.8 %all-to-all-start = ((bf16[4,256,2048]{2,1,0:T(8,128)(2,1)}), bf16[4,256,2048]{2,1,0:T(8,128)(2,1)}, u32[]{:S(2)}, u32[]{:S(2)}) async-start(bf16[4,256,2048]{2,1,0:T(8,128)(2,1)} %broadcast_in_dim.10), calls=%async_computation | async-start | bytes 8388608 | tf_op jit(solution)/shard_map/all_to_all | solution.py:415
  42.6 90.6 %copy-start = (bf16[1,2,64,2048]{3,2,1,0:T(8,128)(2,1)S(1)}, bf16[1,2,64,2048]{3,2,1,0:T(8,128)(2,1)}, u32[]{:S(2)}) copy-start(bf16[1,2,64,2048]{3,2,1,0:T(8,128)(2,1)} %param.14) | copy-start | bytes 1572868
  42.6 90.6 %copy-start.1 = (bf16[1,2,64,2048]{3,2,1,0:T(8,128)(2,1)S(1)}, bf16[1,2,64,2048]{3,2,1,0:T(8,128)(2,1)}, u32[]{:S(2)}) copy-start(bf16[1,2,64,2048]{3,2,1,0:T(8,128)(2,1)} %param.15) | copy-start | bytes 1572868
  42.6 90.6 %copy-start.2 = (f32[2048]{0:T(1024)S(1)}, f32[2048]{0:T(1024)}, u32[]{:S(2)}) copy-start(f32[2048]{0:T(1024)} %param.18) | copy-start | bytes 24580
  177.7 8.0 %collective-permute-start.1 = (bf16[33,16,128]{2,1,0:T(8,128)(2,1)S(1)}, bf16[33,16,128]{2,1,0:T(8,128)(2,1)S(1)}, u32[]{:S(2)}, u32[]{:S(2)}) collective-permute-start(bf16[33,16,128]{2,1,0:T(8,128)(2,1)S(1)} %get-tuple-element.19), channel_id=1, source_target_pairs={{0,4},{4,0},{1,5},{5,1},{2,6},{6,2},{3,7},{7,3},{8,12},{12,8},{9,1... | collective-permute-start | bytes 405512 | tf_op jit(solution)/shard_map/ppermute | solution.py:441
  204.8 12.4 %all-to-all-start.3 = ((f32[8,16,128]{2,1,0:T(8,128)}), f32[8,16,128]{2,1,0:T(8,128)S(1)}, u32[]{:S(2)}, u32[]{:S(2)}) async-start(f32[8,16,128]{2,1,0:T(8,128)} %shard_map.177), calls=%async_computation.3 | async-start | bytes 131072 | tf_op jit(solution)/shard_map/all_to_all | solution.py:446
Sparse Core Ops, SparseCore 0:
  10.9 122.2 all-gather.1

commit v7 on v6

--- a/solution.py
+++ b/solution.py
@@ -101,7 +101,7 @@
             for side in range(2):
                 ref[side * HK + g, pl.ds(t0, TOK), :] = value[b * ROWS + side * TOK : b * ROWS + side * TOK + TOK]
 
-    @pl.loop(0, ALL // 256, unroll=2)
+    @pl.loop(0, ALL // 256, unroll=4)
     def _(r):
         r0 = pl.multiple_of(r * 256, 256)
         c, s = kc[pl.ds(r0, 256), :], ks[pl.ds(r0, 256), :]
@@ -113,7 +113,7 @@
     for d in range(32):
         bv[16 * d : 16 * d + 16, :] = wn[64 * d : 64 * d + 16, 2 * RANK :]
 
-    @pl.loop(0, ALL // 256, unroll=2)
+    @pl.loop(0, ALL // 256, unroll=4)
     def _(r):
         r0 = pl.multiple_of(r * 256, 256)
         x = xa[pl.ds(r0, 256), :]

time: 226 us -> 226 us (level)
  no operation moved by 1% of the time
where the time goes in v7:
time: 226 us; the launch traced here: 225 us
  waiting for transfers between devices  116 us (51%)
  blocking collectives  35.8 us (16%)
  Pallas kernels  31.6 us (14%)
  starting transfers between devices  18.9 us (8%)
  between operations  16 us (7%)
  local copies, waits for them, and re-layouts  3.7 us (2%)
  other arithmetic  3.56 us (2%)
    all_gather x1, waiting for transfers between devices, body(): lax.all_gather(packed, ('h',) + OWN, axis=0, tiled=True)  46.9 us
    all_to_all x1, waiting for transfers between devices, body(): lax.all_to_all(jnp.broadcast_to(two[None], (4,) + two.shape), 'y', 0, 0,...  40.7 us
    pallas_call x1, Pallas kernels, local_step(): pl.pallas_call(local_kernel, out_shape=jax.ShapeDtypeStruct((4, 57, 16, 2...  26.4 us
    all_to_all x1, blocking collectives, body(): shares = lax.all_to_all(scaled, OWN, 0, 0, tiled=True)  18.5 us
    all_to_all x1, blocking collectives, body(): got = lax.all_to_all(mine, 'y', 0, 0, tiled=True)  17.2 us
    ppermute x1, waiting for transfers between devices, body(): other = lax.ppermute(xn, 'h', [(0, 1), (1, 0)])  15.2 us
    ppermute x1, starting transfers between devices, body(): other = lax.ppermute(xn, 'h', [(0, 1), (1, 0)])  7.78 us
    all_to_all x1, waiting for transfers between devices, body(): total = lax.all_to_all(spread, ('y', 'h'), 0, 0, tiled=True)  7.77 us
  transfers between devices with their start and end apart: 5, of which 5 were waited for; matrix products, arithmetic and copies ran while one was open for 3% of the time, Pallas kernels for 0%

profile of v7, /device:TPU:1, one launch (start us, length us, event | category | flops | bytes accessed | tf_op | source)
XLA Modules:
  0.0 225.4 jit_solution(6124979851385806654)
XLA Ops:
  7.2 0.0 all-gather.2.cloned.1.call-start
  7.2 3.5 %shard_map.173 = (bf16[64,2688]{1,0:T(8,128)(2,1)}, bf16[128,2048]{1,0:T(8,128)(2,1)}) custom-call(s32[1]{0:T(128)} %bitcast.h_ref, bf16[64,2048]{1,0:T(8,128)(2,1)} %wq.1, bf16[64,512]{1,0:T(8,128)(2,1)} %wk.1, bf16[64,512]{1,0:T(8,128)(2,1)} %wv.1, bf16[64,2048]{1,0:T(8,128)(2,1)} %wo.1, bf16[64,64]{1,0:T(8,128)(2,1)} %aq.1, bf16[64,64]{1,0:T(8,128)(2,1)} %av.1, ...), custom_call_target="tpu_custom_call" | custom-call | tf_op jit(solution)/shard_map/pallas_call | solution.py:369
  10.7 0.0 all-gather.2.cloned.1.call-update
  10.7 7.8 %collective-permute-start = (bf16[128,2048]{1,0:T(8,128)(2,1)}, bf16[128,2048]{1,0:T(8,128)(2,1)S(1)}, u32[]{:S(2)}, u32[]{:S(2)}) collective-permute-start(bf16[128,2048]{1,0:T(8,128)(2,1)} %get-tuple-element.17), channel_id=1, source_target_pairs={{0,4},{4,0},{1,5},{5,1},{2,6},{6,2},{3,7},{7,3},{8,12},{12,8},{9,1... | collective-permute-start | bytes 1572872 | tf_op jit(solution)/shard_map/ppermute | solution.py:411
  18.5 15.2 %collective-permute-done = bf16[128,2048]{1,0:T(8,128)(2,1)S(1)} collective-permute-done((bf16[128,2048]{1,0:T(8,128)(2,1)}, bf16[128,2048]{1,0:T(8,128)(2,1)S(1)}, u32[]{:S(2)}, u32[]{:S(2)}) %collective-permute-start) | collective-permute-done | bytes 524320 | tf_op jit(solution)/shard_map/ppermute | solution.py:411
  33.8 1.1 pad_maximum_fusion
  34.9 2.6 %broadcast_in_dim.10 = bf16[4,256,2048]{2,1,0:T(8,128)(2,1)} broadcast(bf16[256,2048]{1,0:T(8,128)(2,1)S(1)} %pad_maximum_fusion), dimensions={1,2} | broadcast | bytes 5242880 | tf_op jit(solution)/shard_map/broadcast_in_dim | solution.py:415
  37.5 0.0 copy-start.3
  37.5 0.0 copy-start.4
  37.5 5.0 %all-to-all-start = ((bf16[4,256,2048]{2,1,0:T(8,128)(2,1)}), bf16[4,256,2048]{2,1,0:T(8,128)(2,1)}, u32[]{:S(2)}, u32[]{:S(2)}) async-start(bf16[4,256,2048]{2,1,0:T(8,128)(2,1)} %broadcast_in_dim.10), calls=%async_computation | async-start | bytes 8388608 | tf_op jit(solution)/shard_map/all_to_all | solution.py:415
  42.6 0.0 copy-start
  42.6 0.0 copy-start.1
  42.6 0.0 copy-start.2
  42.6 0.1 iota_add_fusion
  42.7 0.1 convert_element_type.25
  42.8 0.1 add.71
  42.8 0.0 copy-done.3
  42.9 0.1 convert_element_type.27
  42.9 0.0 copy-done.4
  42.9 0.1 mul.78
  43.0 0.1 mul.79
  43.1 0.1 copy.21.sign
  43.2 1.9 fusion
  45.1 0.3 pad_maximum_fusion.1
  45.5 0.1 compare_select_fusion.bias
  45.6 40.7 %all-to-all-done = bf16[4,256,2048]{2,1,0:T(8,128)(2,1)} async-done(((bf16[4,256,2048]{2,1,0:T(8,128)(2,1)}), bf16[4,256,2048]{2,1,0:T(8,128)(2,1)}, u32[]{:S(2)}, u32[]{:S(2)}) %all-to-all-start) | async-done | bytes 4194336 | tf_op jit(solution)/shard_map/all_to_all | solution.py:415
  86.3 46.9 %all-gather.2.cloned.1.call-done = bf16[4096,2688]{1,0:T(8,128)(2,1)} async-done(((bf16[64,2688]{1,0:T(8,128)(2,1)}), bf16[4096,2688]{1,0:T(8,128)(2,1)}) %all-gather.2.cloned.1.call-update) | async-done | bytes 22020112 | tf_op jit(solution)/shard_map/all_gather | solution.py:412
  133.2 0.0 copy-done
  133.2 0.0 copy-done.1
  133.2 0.0 copy-done.2
  133.2 26.4 %shard_map.174 = bf16[4,57,16,128]{3,2,1,0:T(8,128)(2,1)S(1)} custom-call(s32[1]{0:T(128)} %bitcast.1.own_ref, bf16[2,2048,2688]{2,1,0:T(8,128)(2,1)} %bitcast.14, bf16[1024,2048]{1,0:T(8,128)(2,1)} %bitcast.5.xa, f32[1024,128]{1,0:T(8,128)S(1)} %get-tuple-element.32.kc, f32[1024,128]{1,0:T(8,128)S(1)} %get-tuple-element.33.ks, ...), custom_call_target="tpu_custom_call" | custom-call | flops 24000000000 | bytes 27000000 | tf_op jit(solution)/shard_map/pallas_call | solution.py:385
  159.6 17.2 %all_to_all.20.got = bf16[4,57,16,128]{3,2,1,0:T(8,128)(2,1)S(1)} all-to-all(bf16[4,57,16,128]{3,2,1,0:T(8,128)(2,1)S(1)} %shard_map.174), channel_id=1, replica_groups=mesh['z'=4,'c'=2,'y'=4,'h'=2,'x'=4] {'y'}, dimensions={0} | all-to-all | bytes 1867776 | tf_op jit(solution)/shard_map/all_to_all | solution.py:435
  176.8 0.2 shard_map.175
  177.1 2.7 %collective-permute-start.1 = (bf16[33,16,128]{2,1,0:T(8,128)(2,1)S(1)}, bf16[33,16,128]{2,1,0:T(8,128)(2,1)S(1)}, u32[]{:S(2)}, u32[]{:S(2)}) collective-permute-start(bf16[33,16,128]{2,1,0:T(8,128)(2,1)S(1)} %get-tuple-element.19), channel_id=1, source_target_pairs={{0,4},{4,0},{1,5},{5,1},{2,6},{6,2},{3,7},{7,3},{8,12},{12,8},{9,1... | collective-permute-start | bytes 405512 | tf_op jit(solution)/shard_map/ppermute | solution.py:441
  179.8 5.2 %collective-permute-done.1.met = bf16[33,16,128]{2,1,0:T(8,128)(2,1)S(1)} collective-permute-done((bf16[33,16,128]{2,1,0:T(8,128)(2,1)S(1)}, bf16[33,16,128]{2,1,0:T(8,128)(2,1)S(1)}, u32[]{:S(2)}, u32[]{:S(2)}) %collective-permute-start.1) | collective-permute-done | bytes 135200 | tf_op jit(solution)/shard_map/ppermute | solution.py:441
  185.0 0.1 shard_map.176
  185.2 18.5 %all_to_all.21.shares = bf16[32,16,128]{2,1,0:T(8,128)(2,1)S(1)} all-to-all(bf16[32,16,128]{2,1,0:T(8,128)(2,1)S(1)} %get-tuple-element.21), channel_id=1, replica_groups=mesh['z'=4,'c'=2,'y'=4,'h'=2,'x'=4] {'z','c','x'}, dimensions={0} | all-to-all | bytes 262144 | tf_op jit(solution)/shard_map/all_to_all | solution.py:443
  203.7 0.7 shard_map.177
  204.3 3.3 %all-to-all-start.3 = ((f32[8,16,128]{2,1,0:T(8,128)}), f32[8,16,128]{2,1,0:T(8,128)S(1)}, u32[]{:S(2)}, u32[]{:S(2)}) async-start(f32[8,16,128]{2,1,0:T(8,128)} %shard_map.177), calls=%async_computation.3 | async-start | bytes 131072 | tf_op jit(solution)/shard_map/all_to_all | solution.py:446
  207.7 0.5 slice.3
  209.0 7.8 %all-to-all-done.3.total = f32[8,16,128]{2,1,0:T(8,128)S(1)} async-done(((f32[8,16,128]{2,1,0:T(8,128)}), f32[8,16,128]{2,1,0:T(8,128)S(1)}, u32[]{:S(2)}, u32[]{:S(2)}) %all-to-all-start.3) | async-done | bytes 65568 | tf_op jit(solution)/shard_map/all_to_all | solution.py:446
  216.7 0.7 shard_map.178
  (6 shorter events, 0.0 us)
Async XLA Ops:
  7.2 126.0 %all-gather.2.cloned.1.call-start = ((), (), s32[]{:S(2)}) async-start(), calls=%async_computation.4 | async-start | bytes 22364160 | tf_op jit(solution)/shard_map/all_gather | solution.py:412
  10.7 23.0 %collective-permute-start = (bf16[128,2048]{1,0:T(8,128)(2,1)}, bf16[128,2048]{1,0:T(8,128)(2,1)S(1)}, u32[]{:S(2)}, u32[]{:S(2)}) collective-permute-start(bf16[128,2048]{1,0:T(8,128)(2,1)} %get-tuple-element.17), channel_id=1, source_target_pairs={{0,4},{4,0},{1,5},{5,1},{2,6},{6,2},{3,7},{7,3},{8,12},{12,8},{9,1... | collective-permute-start | bytes 1572872 | tf_op jit(solution)/shard_map/ppermute | solution.py:411
  37.5 5.3 %copy-start.3 = (s32[1,2,64]{2,1,0:T(2,128)S(1)}, s32[1,2,64]{2,1,0:T(2,128)}, u32[]{:S(2)}) copy-start(s32[1,2,64]{2,1,0:T(2,128)} %param.16) | copy-start | bytes 1540
  37.5 5.4 %copy-start.4 = (f32[2]{0:T(128)S(1)}, f32[2]{0:T(128)}, u32[]{:S(2)}) copy-start(f32[2]{0:T(128)} %constant.64.clone) | copy-start | bytes 28
  37.5 48.8 %all-to-all-start = ((bf16[4,256,2048]{2,1,0:T(8,128)(2,1)}), bf16[4,256,2048]{2,1,0:T(8,128)(2,1)}, u32[]{:S(2)}, u32[]{:S(2)}) async-start(bf16[4,256,2048]{2,1,0:T(8,128)(2,1)} %broadcast_in_dim.10), calls=%async_computation | async-start | bytes 8388608 | tf_op jit(solution)/shard_map/all_to_all | solution.py:415
  42.6 90.6 %copy-start = (bf16[1,2,64,2048]{3,2,1,0:T(8,128)(2,1)S(1)}, bf16[1,2,64,2048]{3,2,1,0:T(8,128)(2,1)}, u32[]{:S(2)}) copy-start(bf16[1,2,64,2048]{3,2,1,0:T(8,128)(2,1)} %param.14) | copy-start | bytes 1572868
  42.6 90.6 %copy-start.1 = (bf16[1,2,64,2048]{3,2,1,0:T(8,128)(2,1)S(1)}, bf16[1,2,64,2048]{3,2,1,0:T(8,128)(2,1)}, u32[]{:S(2)}) copy-start(bf16[1,2,64,2048]{3,2,1,0:T(8,128)(2,1)} %param.15) | copy-start | bytes 1572868
  42.6 90.6 %copy-start.2 = (f32[2048]{0:T(1024)S(1)}, f32[2048]{0:T(1024)}, u32[]{:S(2)}) copy-start(f32[2048]{0:T(1024)} %param.18) | copy-start | bytes 24580
  177.1 8.0 %collective-permute-start.1 = (bf16[33,16,128]{2,1,0:T(8,128)(2,1)S(1)}, bf16[33,16,128]{2,1,0:T(8,128)(2,1)S(1)}, u32[]{:S(2)}, u32[]{:S(2)}) collective-permute-start(bf16[33,16,128]{2,1,0:T(8,128)(2,1)S(1)} %get-tuple-element.19), channel_id=1, source_target_pairs={{0,4},{4,0},{1,5},{5,1},{2,6},{6,2},{3,7},{7,3},{8,12},{12,8},{9,1... | collective-permute-start | bytes 405512 | tf_op jit(solution)/shard_map/ppermute | solution.py:441
  204.3 12.4 %all-to-all-start.3 = ((f32[8,16,128]{2,1,0:T(8,128)}), f32[8,16,128]{2,1,0:T(8,128)S(1)}, u32[]{:S(2)}, u32[]{:S(2)}) async-start(f32[8,16,128]{2,1,0:T(8,128)} %shard_map.177), calls=%async_computation.3 | async-start | bytes 131072 | tf_op jit(solution)/shard_map/all_to_all | solution.py:446
Sparse Core Ops, SparseCore 0:
  10.9 122.2 all-gather.1
